TPU v7x, 128 devices: a whole 4x4x4 slice. The times are simulated.
128 devices in a mesh: member: 8 (over z_hi, y), domain: 16 (over x, z_lo, core).
Axes of the slice: x: 4, y: 4, z: 4 (z_hi: 2, z_lo: 2; z = z_hi * 2 + z_lo), core: 2. Of those that a mesh axis runs over, the one named last changes fastest.
Arguments:
- ensemble: float32 [32, 3, 4, 2048, 128], P('member', None, None, 'domain'), may hold values from -6 to 6
- control: float32 [8, 3, 4, 2048, 128], P('member', None, None, 'domain'), may hold values from -6 to 6
- owner: int32 [16], replicated, may hold values from 0 to 7
- neighbours: int32 [16, 4], replicated, may hold values from 0 to 15
- edge_codes: int32 [16, 4], replicated, may hold values from 0 to 7
Outputs:
- advanced: float32 [32, 3, 4, 2048, 128], P('member', None, None, 'domain')
Inputs may be any that keep to these rules, and one draw needn't show every extreme that they name: `owner`: one member position for each patch. `neighbours`: index of a patch. `edge_codes`: side code plus 4 if reversed.
All inputs are finite; a program needn't handle non-finite values.
Results may differ from a plain program's by a relative error of at most 0.0003.
Values sent between devices are 32-bit elements; how exact they have to be, the bound alone decides.
No kernel may reach another device: no remote copies, remote signals or barrier semaphores. Data moves between devices by JAX's collectives and lax.ppermute only.
A program may use at most 64 MiB of HBM per device.

v0:
```python
import jax
import jax.numpy as jnp
from jax import lax
from jax.sharding import PartitionSpec as P


def spread(array, axis, root):
    mine = lax.axis_index(axis) == root
    return lax.psum(jnp.where(mine, array, jnp.zeros_like(array)), axis)


def edge_strips(field):
    size = field.shape[-1]
    top = field[..., 0:2, :]
    bottom = jnp.flip(field[..., size - 2 :, :], axis=-2)
    left = jnp.swapaxes(field[..., :, 0:2], -1, -2)
    right = jnp.swapaxes(jnp.flip(field[..., :, size - 2 :], axis=-1), -1, -2)
    return jnp.stack([top, bottom, left, right], axis=0)


def pick_rims(strips_all, neigh_row, code_row):
    chosen = []
    for border in range(4):
        source = strips_all[neigh_row[border], code_row[border] % 4]
        flipped = jnp.flip(source, axis=-1)
        chosen.append(jnp.where(code_row[border] // 4 == 1, flipped, source))
    return chosen


def assemble(center, rims):
    top, bottom, left, right = rims
    middle = jnp.concatenate(
        [jnp.flip(jnp.swapaxes(left, -1, -2), axis=-1), center, jnp.swapaxes(right, -1, -2)],
        axis=-1,
    )
    zeros = jnp.zeros(top.shape[:-1] + (2,), center.dtype)
    upper = jnp.concatenate([zeros, jnp.flip(top, axis=-2), zeros], axis=-1)
    lower = jnp.concatenate([zeros, bottom, zeros], axis=-1)
    return jnp.concatenate([upper, middle, lower], axis=-2)


def stencil_step(padded):
    wind_x = padded[..., 0, :, :, :]
    wind_y = padded[..., 1, :, :, :]
    divergence = 0.5 * (
        wind_x[..., 1:-1, 2:]
        - wind_x[..., 1:-1, :-2]
        + wind_y[..., 2:, 1:-1]
        - wind_y[..., :-2, 1:-1]
    )
    center = padded[..., 2:-2, 2:-2]
    diff_x = padded[..., 2:-2, 3:-1] - padded[..., 2:-2, 1:-3]
    diff_y = padded[..., 3:-1, 2:-2] - padded[..., 1:-3, 2:-2]
    center_x = center[..., 0:1, :, :, :]
    center_y = center[..., 1:2, :, :, :]
    moved = center - 0.2 * (center_x * diff_x + center_y * diff_y)
    grad_x = divergence[..., 1:-1, 2:] - divergence[..., 1:-1, :-2]
    grad_y = divergence[..., 2:, 1:-1] - divergence[..., :-2, 1:-1]
    first = moved[..., 0, :, :, :] + 0.1 * grad_x
    second = moved[..., 1, :, :, :] + 0.1 * grad_y
    return jnp.stack([first, second, moved[..., 2, :, :, :]], axis=-4)


def on_device(ensemble, control, owner, neighbours, edge_codes):
    members_all = ensemble.shape[0] * lax.axis_size("member")
    local_sum = jnp.sum(ensemble, axis=0)
    position = lax.axis_index("domain")
    patch_owner = owner[position]
    chosen_control = spread(control[0], "member", patch_owner)
    total = lax.psum(local_sum, "member")
    shift = chosen_control - total / members_all
    recentered = ensemble + shift[None]
    neigh_row = neighbours[position]
    code_row = edge_codes[position]
    gathered = lax.all_gather(edge_strips(recentered)[None], "domain", axis=0, tiled=True)
    chosen = pick_rims(gathered, neigh_row, code_row)
    padded = assemble(recentered, chosen)
    return stencil_step(padded)


def solution(mesh):
    in_specs = (
        P("member", None, None, "domain", None),
        P("member", None, None, "domain", None),
        P(),
        P(),
        P(),
    )
    out_specs = P("member", None, None, "domain", None)
    return jax.shard_map(
        on_device, mesh=mesh, in_specs=in_specs, out_specs=out_specs, check_vma=False
    )
```

profile of v0, /device:TPU:0, one launch (start us, length us, event | category | flops | bytes accessed | tf_op | source)
XLA Modules:
  0.0 206.9 jit_solution(12940220049064927799)
XLA Ops:
  6.5 0.0 all-reduce.3.cloned.1.call-start
  6.5 1.2 dynamic_slice.21
  8.4 0.9 select_bitcast_fusion
  9.4 3.2 %reduce_sum.9 = f32[3,4,128,128]{3,2,1,0:T(8,128)} reduce(f32[4,3,4,128,128]{4,3,2,1,0:T(8,128)} %param.5, f32[]{:T(128)} %constant.75.clone.1), dimensions={0}, to_apply=%region_1.2 | reduce | flops 589824 | bytes 3932164 | tf_op jit(solution)/shard_map/reduce_sum | solution.py:66
  12.6 0.0 all-reduce.3.cloned.1.call-update
  12.6 0.0 all-gather.3.cloned.1.call-start
  12.7 0.0 copy-done.4
  12.7 2.8 %copy.33 = f32[4,3,4,128,128]{3,2,4,1,0:T(4,128)} copy(f32[4,3,4,128,128]{4,3,2,1,0:T(8,128)S(1)} %copy-done.4) | data formatting | bytes 6291456 | tf_op args[0]
  15.4 90.3 %all-reduce.3.cloned.1.call-done = (f32[3,4,128,128]{3,2,1,0:T(8,128)}, f32[3,4,128,128]{3,2,1,0:T(8,128)}) async-done(((f32[3,4,128,128]{3,2,1,0:T(8,128)}, f32[3,4,128,128]{3,2,1,0:T(8,128)}), (f32[3,4,128,128]{3,2,1,0:T(8,128)}, f32[3,4,128,128]{3,2,1,0:T(8,128)})) %all-reduce.3.cloned.1.call-update) | async-done | bytes 1572880 | tf_op jit(solution)/shard_map/psum | solution.py:9
  105.8 1.5 multiply_subtract_fusion
  107.2 1.2 copy.32
  108.4 2.3 %broadcast_add_fusion = f32[4,3,8,128,64]{3,2,4,1,0:T(8,128)S(1)} fusion(f32[4,3,8,128,64]{3,2,4,1,0:T(8,128)} %bitcast.80, f32[3,8,128,64]{2,1,3,0:T(8,128)} %bitcast.81), kind=kLoop, calls=%fused_computation.27 | loop fusion | flops 786432 | bytes 7077888 | tf_op jit(solution)/shard_map/add | solution.py:72
  110.7 4.5 %slice_bitcast_fusion = (f32[1,4,3,4,2,128]{4,3,5,2,1,0:T(4,128)}, f32[4,3,4,2,128]{3,2,4,1,0:T(4,128)}) fusion(f32[4,3,4,128,128]{3,2,4,1,0:T(4,128)S(1)} %bitcast.77), kind=kLoop, calls=%fused_computation.14 | loop fusion | bytes 196608 | tf_op jit(solution)/shard_map/stack | solution.py:18
  115.3 3.1 %copy.34 = f32[1,4,3,4,2,128]{5,3,4,2,1,0:T(4,128)S(1)} copy(f32[1,4,3,4,2,128]{4,3,5,2,1,0:T(4,128)} %get-tuple-element.17) | data formatting | bytes 98304 | tf_op jit(solution)/shard_map/stack | solution.py:18
  118.4 9.8 %rev.27 = f32[4,3,4,2,128]{3,2,4,1,0:T(4,128)} reverse(f32[4,3,4,2,128]{3,2,4,1,0:T(4,128)} %get-tuple-element.18), dimensions={3} | reverse | bytes 98304 | tf_op jit(solution)/shard_map/jit(_flip)/rev | solution.py:15
  128.3 3.1 %copy.35 = f32[1,4,3,4,2,128]{5,3,4,2,1,0:T(4,128)S(1)} copy(f32[1,4,3,4,2,128]{4,3,5,2,1,0:T(4,128)} %bitcast.82) | data formatting | bytes 98304 | tf_op jit(solution)/shard_map/stack | solution.py:18
  131.4 0.7 pad_maximum_fusion.13
  132.1 0.0 all-gather.3.cloned.1.call-update
  132.2 0.0 copy-done.7
  132.2 0.0 copy-done.8
  132.2 0.1 constant_dynamic-slice_fusion.2
  132.3 0.6 fusion.15
  138.0 0.6 fusion.14
  150.7 1.6 slice_bitcast_fusion.4
  152.2 13.9 %all-gather.3.cloned.1.call-done = f32[64,4,3,4,2,128]{5,3,4,2,1,0:T(4,128)} async-done(((f32[4,4,3,4,2,128]{5,3,4,2,1,0:T(4,128)}), f32[64,4,3,4,2,128]{5,3,4,2,1,0:T(4,128)}) %all-gather.3.cloned.1.call-update) | async-done | bytes 3145744 | tf_op jit(solution)/shard_map/all_gather | solution.py:75
  166.1 0.9 dynamic-slice_bitcast_fusion.1
  167.0 0.1 rev.32
  167.1 0.1 rev.33
  167.3 0.1 rev.30
  167.5 0.1 rev.29
  167.7 0.2 pad_maximum_fusion.15
  167.9 3.3 %copy.41 = f32[4,3,4,2,132]{3,2,4,0,1:T(4,128)} copy(f32[4,3,4,2,132]{4,2,3,1,0:T(4,128)S(1)} %get-tuple-element.21) | data formatting | bytes 101376 | tf_op jit(solution)/shard_map/concatenate | solution.py:38
  171.2 3.3 %copy.42 = f32[4,3,4,2,132]{3,2,4,0,1:T(4,128)} copy(f32[4,3,4,2,132]{4,2,3,1,0:T(4,128)S(1)} %get-tuple-element.22) | data formatting | bytes 101376 | tf_op jit(solution)/shard_map/concatenate | solution.py:37
  174.5 0.0 copy-start
  174.5 0.0 copy-start.1
  174.6 8.5 %maximum_bitcast_fusion = (f32[4,4,132,132]{2,1,3,0:T(4,128)S(1)}, f32[4,4,132,132]{2,1,3,0:T(4,128)S(1)}) fusion(f32[4,3,4,2,132]{3,2,4,0,1:T(4,128)} %copy.41, f32[4,3,4,2,132]{3,2,4,0,1:T(4,128)} %copy.42, f32[4,3,4,128,2]{3,2,4,0,1:T(4,128)S(1)} %select_bitcast_fusion.2, f32[4,3,4,128,2]{3,2,4,0,1:T(4,128)S(1)} %rev.31, f32[4,3,4,128,128]{3,2,4,1,0:T(4,128)} %copy.33, ...), kind=kLoop, calls=%fused_computation.22 | loop fusion | flops 3016704 | bytes 6362112 | tf_op jit(solution)/shard_map/squeeze | solution.py:43
  183.0 0.0 copy-done
  183.0 0.0 copy-done.1
  183.1 0.0 copy-done.2
  183.1 0.0 copy-done.3
  183.1 0.0 copy-done.5
  183.1 0.0 copy-done.6
  183.1 8.2 %copy_subtract_fusion = f32[4,3,4,128,128]{3,2,4,1,0:T(4,128)S(1)} fusion(f32[4,3,4,128,128]{3,2,4,1,0:T(4,128)S(1)} %copy-done, f32[3,4,128,128]{2,1,3,0:T(4,128)S(1)} %copy-done.3, f32[4,3,4,2,132]{3,2,4,0,1:T(4,128)S(1)} %copy-done.2, f32[4,3,4,128,2]{3,2,4,0,1:T(4,128)S(1)} %select_bitcast_fusion.2, f32[4,3,4,128,2]{3,2,4,0,1:T(4,128)S(1)} %rev.31, ...), kind=kLoop, calls=%fused_computation.16 | loop fusion | flops 12582912 | bytes 12520448 | tf_op jit(solution)/shard_map/sub | solution.py:56
  191.3 0.1 slice.156
  191.4 3.4 %fusion.7 = f32[4,4,130,130]{2,1,3,0:T(4,128)S(1)} fusion(f32[4,4,132,132]{2,1,3,0:T(4,128)S(1)} %get-tuple-element.8, f32[4,4,132,132]{2,1,3,0:T(4,128)S(1)} %get-tuple-element.7), kind=kLoop, calls=%fused_computation.24 | loop fusion | flops 1081600 | bytes 5408000 | tf_op jit(solution)/shard_map/mul | solution.py:45
  194.7 1.7 fusion.13
  196.4 0.8 pad_maximum_fusion.8
  197.3 2.8 %copy.49 = f32[4,3,4,128,128]{4,3,2,1,0:T(8,128)} copy(f32[4,3,4,128,128]{3,2,4,1,0:T(4,128)S(1)} %pad_maximum_fusion.8) | data formatting | bytes 6291456 | tf_op jit(solution)/shard_map/stack | solution.py:61
  (18 shorter events, 0.1 us)
Async XLA Ops:
  6.5 99.2 %all-reduce.3.cloned.1.call-start = ((), (), s32[]{:S(2)}) async-start(), calls=%async_computation.1 | async-start | bytes 3145728 | tf_op jit(solution)/shard_map/psum | solution.py:9
  9.4 3.3 %copy-start.4 = (f32[4,3,4,128,128]{4,3,2,1,0:T(8,128)S(1)}, f32[4,3,4,128,128]{4,3,2,1,0:T(8,128)}, u32[]{:S(2)}) copy-start(f32[4,3,4,128,128]{4,3,2,1,0:T(8,128)} %param.5) | copy-start | bytes 9437188
  12.6 153.5 %all-gather.3.cloned.1.call-start = ((), (), s32[]{:S(2)}) async-start(), calls=%async_computation | async-start | bytes 3342336 | tf_op jit(solution)/shard_map/all_gather | solution.py:75
  128.3 3.9 %copy-start.7 = (s32[16,4]{0,1:T(4,128)S(1)}, s32[16,4]{0,1:T(4,128)}, u32[]{:S(2)}) copy-start(s32[16,4]{0,1:T(4,128)} %param.8) | copy-start | bytes 772
  128.3 3.9 %copy-start.8 = (s32[16,4]{0,1:T(4,128)S(1)}, s32[16,4]{0,1:T(4,128)}, u32[]{:S(2)}) copy-start(s32[16,4]{0,1:T(4,128)} %param.9) | copy-start | bytes 772
  174.5 8.5 %copy-start = (f32[4,3,4,128,128]{3,2,4,1,0:T(4,128)S(1)}, f32[4,3,4,128,128]{3,2,4,1,0:T(4,128)}, u32[]{:S(2)}) copy-start(f32[4,3,4,128,128]{3,2,4,1,0:T(4,128)} %copy.33) | copy-start | bytes 9437188
  174.5 8.5 %copy-start.1 = (f32[4,3,4,2,132]{3,2,4,0,1:T(4,128)S(1)}, f32[4,3,4,2,132]{3,2,4,0,1:T(4,128)}, u32[]{:S(2)}) copy-start(f32[4,3,4,2,132]{3,2,4,0,1:T(4,128)} %copy.41) | copy-start | bytes 152068
  174.5 8.5 %copy-start.2 = (f32[4,3,4,2,132]{3,2,4,0,1:T(4,128)S(1)}, f32[4,3,4,2,132]{3,2,4,0,1:T(4,128)}, u32[]{:S(2)}) copy-start(f32[4,3,4,2,132]{3,2,4,0,1:T(4,128)} %copy.42) | copy-start | bytes 152068
  174.5 8.5 %copy-start.3 = (f32[3,4,128,128]{2,1,3,0:T(4,128)S(1)}, f32[3,4,128,128]{2,1,3,0:T(4,128)}, u32[]{:S(2)}) copy-start(f32[3,4,128,128]{2,1,3,0:T(4,128)} %copy.32) | copy-start | bytes 2359300
  174.6 8.5 %copy-start.5 = (f32[4,4,128,128]{2,1,3,0:T(4,128)S(1)}, f32[4,4,128,128]{2,1,3,0:T(4,128)}, u32[]{:S(2)}) copy-start(f32[4,4,128,128]{2,1,3,0:T(4,128)} %get-tuple-element.11) | copy-start | bytes 3145732
  174.6 8.5 %copy-start.6 = (f32[4,4,128,128]{2,1,3,0:T(4,128)S(1)}, f32[4,4,128,128]{2,1,3,0:T(4,128)}, u32[]{:S(2)}) copy-start(f32[4,4,128,128]{2,1,3,0:T(4,128)} %get-tuple-element.12) | copy-start | bytes 3145732
Sparse Core Ops, SparseCore 0:
  12.7 92.9 all-reduce.2
  132.3 33.7 all-gather.2
where the time goes:
time: 209 us; the launch traced here: 207 us
  waiting for transfers between devices  104 us (50%)
  local copies, waits for them, and re-layouts  39.7 us (19%)
  between operations  31.6 us (15%)
  other arithmetic  31.4 us (15%)
    psum x1, waiting for transfers between devices, spread(): return lax.psum(jnp.where(mine, array, jnp.zeros_like(array)), axis)  90.3 us
    all_gather x1, waiting for transfers between devices, on_device(): lax.all_gather(edge_strips(recentered)[None], 'domain', axis=0, tiled=True)  13.9 us
    another operation x5, local copies, waits for them, and re-layouts, edge_strips(): return jnp.stack([top, bottom, left, right], axis=0)  10.8 us
    rev x1, local copies, waits for them, and re-layouts, edge_strips(): bottom = jnp.flip(field[..., size - 2:, :], axis=-2)  9.85 us
    squeeze x1, other arithmetic, stencil_step(): wind_x = padded[..., 0, :, :, :]  8.46 us
    sub x1, other arithmetic, stencil_step(): moved = center - 0.2 * (center_x * diff_x + center_y * diff_y)  8.19 us
  transfers between devices with their start and end apart: 2, of which 2 were waited for; matrix products, arithmetic and copies ran while one was open for 3% of the time, Pallas kernels for 0%

commit v1 on v0

v1 whole, which is shorter than its diff:
```python
import jax
import jax.numpy as jnp
from jax import lax
from jax.experimental import pallas as pl
from jax.experimental.pallas import tpu as pltpu
from jax.sharding import PartitionSpec as P

MESH = ("member", "domain")
N_MEMBER = 8
N_DOMAIN = 16
SIZE = 128
PLANES = 12
LEV = 4
LOCAL = 4
MEMBERS = 32
ROWS = PLANES * SIZE
CHUNK = ROWS // N_MEMBER
OFFSETS = ((6, 5, 1, 0), (7, 4, 3, 2))
EDGE = 24
STRIP = 4 * EDGE
F32 = jnp.float32


def pairs(target):
    out = []
    for m in range(N_MEMBER):
        for d in range(N_DOMAIN):
            to = target(m, d)
            if to is not None:
                out.append((m * N_DOMAIN + d, to[0] * N_DOMAIN + to[1]))
    return out


def send(array, target):
    return lax.ppermute(array, MESH, pairs(target))


def swap_cores(array):
    return send(array, lambda m, d: (m, d ^ 1))


def exchange(messages):
    out = []
    for j, message in enumerate(messages):

        def target(m, d, j=j):
            offset = OFFSETS[d % 2][j]
            return (m ^ offset, d) if offset else None

        out.append(send(message, target))
    return out


def vmem():
    return pl.BlockSpec(memory_space=pltpu.VMEM)


def smem():
    return pl.BlockSpec(memory_space=pltpu.SMEM)


def hbm():
    return pl.BlockSpec(memory_space=pl.ANY)


def shaped(*shape):
    return jax.ShapeDtypeStruct(shape, F32)


def slot_chunk(member, core, j):
    zero, one = OFFSETS[0][j % 4], OFFSETS[1][j % 4]
    if j >= 4:
        zero, one = one, zero
    return member ^ jnp.where(core == 0, zero, one)


def prepare_kernel(place, owner, ens_hbm, ctl_hbm, keep, give, strips, ens, ctl, part, tile, turned, sems):
    member, patch = place[0], place[1]
    core = patch % 2
    flag = jnp.where(owner[patch] == member, 1.0, 0.0).astype(F32)
    copies = []
    for i in range(PLANES):
        a = pltpu.make_async_copy(ens_hbm.at[:, i], ens.at[:, i], sems.at[0, i])
        b = pltpu.make_async_copy(ctl_hbm.at[i], ctl.at[i], sems.at[1, i])
        a.start()
        b.start()
        copies.append((a, b))
    for i in range(PLANES):
        for c in copies[i]:
            c.wait()
        for r in range(0, SIZE, 32):
            rows = pl.ds(r, 32)
            lane = lax.broadcasted_iota(jnp.int32, (32, SIZE), 1)
            group = lane // 4
            xs = [ens[a, i, rows, :] for a in range(LOCAL)]
            total = (xs[0] + xs[1]) + (xs[2] + xs[3])
            value = flag * ctl[i, rows, :] - total * (1.0 / MEMBERS)
            part[pl.ds(i * SIZE + r, 32), :] = value
            spots = [a * PLANES + i for a in range(LOCAL)] + [LOCAL * PLANES + i]
            for t in (0, 1):
                mine = [(s % 32, x) for s, x in zip(spots, xs + [value]) if s // 32 == t]
                if not mine:
                    continue
                acc = tile[t, rows, :]
                for s, x in mine:
                    acc = jnp.where(group == s, pltpu.roll(x, (4 * s + 2) % SIZE, 1), acc)
                tile[t, rows, :] = acc
        for a in range(LOCAL):
            s = a * PLANES + i
            strips[s : s + 1, :] = ens[a, i, 0:1, :]
            strips[48 + s : 49 + s, :] = ens[a, i, 1:2, :]
            strips[96 + s : 97 + s, :] = ens[a, i, SIZE - 1 : SIZE, :]
            strips[144 + s : 145 + s, :] = ens[a, i, SIZE - 2 : SIZE - 1, :]
        base, row = 4 * CHUNK, i * SIZE
        give[base + i : base + i + 1, :] = part[row : row + 1, :]
        give[base + 12 + i : base + 13 + i, :] = part[row + 1 : row + 2, :]
        give[base + 24 + i : base + 25 + i, :] = part[row + SIZE - 1 : row + SIZE, :]
        give[base + 36 + i : base + 37 + i, :] = part[row + SIZE - 2 : row + SIZE - 1, :]
    turned[0] = tile[0].T
    turned[1] = tile[1].T
    for side, k, q in ((2, 0, 2), (2, 1, 3), (3, 0, 1), (3, 1, 0)):
        at = side * 96 + k * 48
        strips[at : at + 32, :] = turned[0, pl.ds(q, 32, stride=4), :]
        strips[at + 32 : at + 48, :] = turned[1, pl.ds(q, 16, stride=4), :]
        at = 4 * CHUNK + side * EDGE + k * PLANES
        give[at : at + PLANES, :] = turned[1, pl.ds(64 + q, PLANES, stride=4), :]
    for j in range(4):
        own = pl.multiple_of(slot_chunk(member, core, j) * CHUNK, 8)
        other = pl.multiple_of(slot_chunk(member, core, j + 4) * CHUNK, 8)
        keep[j * CHUNK : (j + 1) * CHUNK, :] = part[pl.ds(own, CHUNK), :]
        give[j * CHUNK : (j + 1) * CHUNK, :] = part[pl.ds(other, CHUNK), :]


def prepare(place, owner, ensemble, control):
    return pl.pallas_call(
        prepare_kernel,
        out_shape=[shaped(4 * CHUNK, SIZE), shaped(4 * CHUNK + STRIP, SIZE), shaped(4 * 96, SIZE)],
        in_specs=[smem(), smem(), hbm(), hbm()],
        out_specs=[vmem()] * 3,
        scratch_shapes=[
            pltpu.VMEM((LOCAL, PLANES, SIZE, SIZE), F32),
            pltpu.VMEM((PLANES, SIZE, SIZE), F32),
            pltpu.VMEM((ROWS, SIZE), F32),
            pltpu.VMEM((2, SIZE, SIZE), F32),
            pltpu.VMEM((2, SIZE, SIZE), F32),
            pltpu.SemaphoreType.DMA((2, PLANES)),
        ],
        compiler_params=pltpu.CompilerParams(vmem_limit_bytes=16 << 20),
        cost_estimate=pl.CostEstimate(flops=2_000_000, bytes_accessed=5_000_000, transcendentals=0),
        name="prepare",
    )(place, owner, ensemble, control)


def pack_kernel(keep, give, got, m0, m1, m2, m3, edges):
    for j, m in enumerate((m0, m1, m2, m3)):
        m[0:CHUNK, :] = keep[j * CHUNK : (j + 1) * CHUNK, :]
        m[CHUNK:, :] = got[j * CHUNK : (j + 1) * CHUNK, :]
    edges[0:STRIP, :] = give[4 * CHUNK :, :]
    edges[STRIP:, :] = got[4 * CHUNK :, :]


def pack(keep, give, got):
    return pl.pallas_call(
        pack_kernel,
        out_shape=[shaped(2 * CHUNK, SIZE)] * 4 + [shaped(2 * STRIP, SIZE)],
        in_specs=[vmem()] * 3,
        out_specs=[vmem()] * 5,
        name="pack",
    )(keep, give, got)


def add_kernel(place, a, b, c, d, own, out):
    first = place[1] % 2 == 0
    out[...] = (a[...] + b[...]) + (c[...] + jnp.where(first, own[...], d[...]))


def add(place, received, own):
    return pl.pallas_call(
        add_kernel,
        out_shape=shaped(2 * CHUNK, SIZE),
        in_specs=[smem()] + [vmem()] * 5,
        out_specs=vmem(),
        name="add",
    )(place, *received, own)


def flipped(x, turn):
    lane = lax.broadcasted_iota(jnp.int32, x.shape, 1)
    return jnp.take_along_axis(x, jnp.where(turn, SIZE - 1 - lane, lane), axis=1)


def reduce_kernel(place, neighbours, codes, acc, sib, g0, g1, g2, g3, out):
    out[0:CHUNK, :] = acc[0:CHUNK, :] + sib[CHUNK:, :]
    out[CHUNK : 2 * CHUNK, :] = acc[CHUNK:, :] + sib[0:CHUNK, :]
    patch = place[1]
    for q in (0, 1):
        for side in range(4):
            code = codes[patch ^ q, side]
            away = neighbours[patch ^ q, side] ^ patch
            x_away = away // 4
            at = pl.multiple_of((away % 4) * STRIP + (code % 4) * EDGE, 8)
            picked = g0[pl.ds(at, EDGE), :]
            for x, g in ((1, g1), (2, g2), (3, g3)):
                picked = jnp.where(x_away == x, g[pl.ds(at, EDGE), :], picked)
            to = 2 * CHUNK + q * STRIP + side * EDGE
            out[to : to + EDGE, :] = flipped(picked, code // 4 == 1)


def reduce(place, neighbours, codes, acc, sib, groups):
    return pl.pallas_call(
        reduce_kernel,
        out_shape=shaped(2 * CHUNK + 2 * STRIP, SIZE),
        in_specs=[smem()] * 3 + [vmem()] * 6,
        out_specs=vmem(),
        name="reduce",
    )(place, neighbours, codes, acc, sib, *groups)


def share_kernel(place, a, b, c, d, own, out):
    first = place[1] % 2 == 0
    for j, m in enumerate((a, b, c)):
        out[j * CHUNK : (j + 1) * CHUNK, :] = m[CHUNK : 2 * CHUNK, :]
    out[3 * CHUNK : 4 * CHUNK, :] = jnp.where(first, own[CHUNK : 2 * CHUNK, :], d[CHUNK : 2 * CHUNK, :])
    rows = pl.ds(2 * CHUNK + STRIP, STRIP)
    out[4 * CHUNK :, :] = (a[rows, :] + b[rows, :]) + (c[rows, :] + jnp.where(first, own[rows, :], d[rows, :]))


def share(place, received, own):
    return pl.pallas_call(
        share_kernel,
        out_shape=shaped(4 * CHUNK + STRIP, SIZE),
        in_specs=[smem()] + [vmem()] * 5,
        out_specs=vmem(),
        name="share",
    )(place, *received, own)


def slope(x):
    lane = lax.broadcasted_iota(jnp.int32, x.shape, 1)
    ahead = jnp.where(lane == SIZE - 1, 0.0, pltpu.roll(x, SIZE - 1, 1))
    behind = jnp.where(lane == 0, 0.0, pltpu.roll(x, 1, 1))
    return ahead - behind


def advance_kernel(place, neighbours, codes, ens, e0, e1, e2, e3, a, b, c, d, own, got, out,
                   shift, rims, lines, columns, pad, div, slope_u):
    member, patch = place[0], place[1]
    core = patch % 2
    step = pl.program_id(0)

    @pl.when(step == 0)
    def _():
        first = core == 0
        for j, m in enumerate((a, b, c, d)):
            value = m[0:CHUNK, :]
            if j == 3:
                value = jnp.where(first, own[0:CHUNK, :], value)
            shift[pl.ds(pl.multiple_of(slot_chunk(member, core, j) * CHUNK, 8), CHUNK), :] = value
            at = pl.multiple_of(slot_chunk(member, core, j + 4) * CHUNK, 8)
            shift[pl.ds(at, CHUNK), :] = got[j * CHUNK : (j + 1) * CHUNK, :]
        for side, e in enumerate((e0, e1, e2, e3)):
            turn = codes[patch, side] // 4 == 1
            rows = pl.ds(2 * CHUNK + side * EDGE, EDGE)
            moved = (a[rows, :] + b[rows, :]) + (c[rows, :] + jnp.where(first, own[rows, :], d[rows, :]))
            moved = moved + got[4 * CHUNK + side * EDGE : 4 * CHUNK + (side + 1) * EDGE, :]
            strip = flipped(e[0, 0], turn)
            for k in (0, 1):
                for n in range(LOCAL):
                    at = k * 48 + n * PLANES
                    rims[n, side * 2 + k, 0:PLANES, :] = strip[at : at + PLANES, :] + moved[k * PLANES : (k + 1) * PLANES, :]
        for n in range(LOCAL):
            at = n * 32
            lines[pl.ds(at, PLANES, stride=2), :] = rims[n, 6, 0:PLANES, :]
            lines[pl.ds(at + 1, PLANES, stride=2), :] = rims[n, 4, 0:PLANES, :]
            right = 0.5 * (rims[n, 7, 0:LEV, :] + slope(rims[n, 6, LEV : 2 * LEV, :]))
            left = 0.5 * (slope(rims[n, 4, LEV : 2 * LEV, :]) - rims[n, 5, 0:LEV, :])
            lines[pl.ds(at + 24, LEV, stride=2), :] = right
            lines[pl.ds(at + 25, LEV, stride=2), :] = left
        turned = lines[...].T
        for n in range(LOCAL):
            columns[n] = turned if n == 0 else pltpu.roll(turned, SIZE - 32 * n, 1)

    part = 32
    lane = lax.broadcasted_iota(jnp.int32, (part, SIZE), 1)
    at_left, at_right = lane == 0, lane == SIZE - 1

    def across(x, r, line):
        edge = pltpu.roll(columns[step, r : r + part, :], (SIZE - 1 - 2 * line) % SIZE, 1)
        return jnp.where(at_right, edge, pltpu.roll(x, SIZE - 1, 1)) - jnp.where(at_left, edge, pltpu.roll(x, 1, 1))

    for lev in range(LEV):
        for f in range(3):
            i = f * LEV + lev
            pad[f, 8 : 8 + SIZE, :] = ens[0, i] + shift[i * SIZE : (i + 1) * SIZE, :]
            pad[f, 7:8, :] = rims[step, 0, i : i + 1, :]
            pad[f, 8 + SIZE : 9 + SIZE, :] = rims[step, 2, i : i + 1, :]
        i = LEV + lev
        div[7:8, :] = 0.5 * (slope(pad[0, 7:8, :]) + pad[1, 8:9, :] - rims[step, 1, i : i + 1, :])
        div[8 + SIZE : 9 + SIZE, :] = 0.5 * (
            slope(pad[0, 8 + SIZE : 9 + SIZE, :]) + rims[step, 3, i : i + 1, :] - pad[1, 7 + SIZE : 8 + SIZE, :]
        )
        for r in range(0, SIZE, part):
            at = 8 + r
            du = across(pad[0, at : at + part, :], r, lev)
            slope_u[r : r + part, :] = du
            div[at : at + part, :] = 0.5 * (du + pad[1, at + 1 : at + 1 + part, :] - pad[1, at - 1 : at - 1 + part, :])
        for r in range(0, SIZE, part):
            at = 8 + r
            here = slice(at, at + part)
            up, down = slice(at - 1, at - 1 + part), slice(at + 1, at + 1 + part)
            u, v, w = pad[0, here, :], pad[1, here, :], pad[2, here, :]
            edge = pltpu.roll(columns[step, r : r + part, :], (SIZE - 1 - 2 * (PLANES + lev)) % SIZE, 1)
            edge = edge + jnp.where(at_left, 0.5 * u, -0.5 * u)
            mid = div[here, :]
            grad_x = jnp.where(at_right, edge, pltpu.roll(mid, SIZE - 1, 1)) - jnp.where(at_left, edge, pltpu.roll(mid, 1, 1))
            grad_y = div[down, :] - div[up, :]
            new_u = u - 0.2 * (u * slope_u[r : r + part, :] + v * (pad[0, down, :] - pad[0, up, :]))
            new_v = v - 0.2 * (u * across(v, r, LEV + lev) + v * (pad[1, down, :] - pad[1, up, :]))
            new_w = w - 0.2 * (u * across(w, r, 2 * LEV + lev) + v * (pad[2, down, :] - pad[2, up, :]))
            out[0, lev, r : r + part, :] = new_u + 0.1 * grad_x
            out[0, LEV + lev, r : r + part, :] = new_v + 0.1 * grad_y
            out[0, 2 * LEV + lev, r : r + part, :] = new_w


def advance(place, neighbours, codes, ensemble, gathered, received, own, got):
    def strip(side):
        def where(n, place, neighbours, codes):
            patch = place[1]
            return neighbours[patch, side], codes[patch, side] % 4, 0, 0

        return pl.BlockSpec((1, 1, 96, SIZE), where)

    block = pl.BlockSpec((1, PLANES, SIZE, SIZE), lambda n, *_: (n, 0, 0, 0))
    return pl.pallas_call(
        advance_kernel,
        out_shape=shaped(LOCAL, PLANES, SIZE, SIZE),
        grid_spec=pltpu.PrefetchScalarGridSpec(
            num_scalar_prefetch=3,
            grid=(LOCAL,),
            in_specs=[block] + [strip(s) for s in range(4)] + [vmem()] * 6,
            out_specs=block,
            scratch_shapes=[
                pltpu.VMEM((ROWS, SIZE), F32),
                pltpu.VMEM((LOCAL, 8, 16, SIZE), F32),
                pltpu.VMEM((SIZE, SIZE), F32),
                pltpu.VMEM((LOCAL, SIZE, SIZE), F32),
                pltpu.VMEM((3, SIZE + 16, SIZE), F32),
                pltpu.VMEM((SIZE + 16, SIZE), F32),
                pltpu.VMEM((SIZE, SIZE), F32),
            ],
        ),
        compiler_params=pltpu.CompilerParams(vmem_limit_bytes=24 << 20),
        cost_estimate=pl.CostEstimate(flops=40_000_000, bytes_accessed=8_000_000, transcendentals=0),
        name="advance",
    )(place, neighbours, codes, ensemble, *([gathered] * 4), *received, own, got)


def on_device(ensemble, control, owner, neighbours, codes):
    shape = ensemble.shape
    ensemble = ensemble.reshape(LOCAL, PLANES, SIZE, SIZE)
    control = control.reshape(PLANES, SIZE, SIZE)
    place = jnp.stack([lax.axis_index("member"), lax.axis_index("domain")]).astype(jnp.int32)

    keep, give, strips = prepare(place, owner, ensemble, control)
    gathered = lax.all_gather(strips, "domain", axis=0, tiled=True)
    gathered = gathered.reshape(N_DOMAIN, 4, 96, SIZE)

    got = swap_cores(give)
    *messages, edges = pack(keep, give, got)
    over_z = send(edges, lambda m, d: (m, d ^ 2))
    group = jnp.concatenate([edges, over_z], axis=0)
    received = exchange(messages)
    groups = [group] + [send(group, lambda m, d, x=x: (m, d ^ (4 * x))) for x in (1, 2, 3)]
    acc = add(place, received, messages[3])
    reduced = reduce(place, neighbours, codes, acc, swap_cores(acc), groups)
    received = exchange([reduced] * 4)
    got = swap_cores(share(place, received, reduced))
    out = advance(place, neighbours, codes, ensemble, gathered, received, reduced, got)
    return out.reshape(shape)


def solution(mesh):
    spec = P("member", None, None, "domain", None)
    return jax.shard_map(
        on_device, mesh=mesh, in_specs=(spec, spec, P(), P(), P()), out_specs=spec, check_vma=False
    )
```

time: 209 us -> 107 us (0.51)
  the two profiles are of different devices: /device:TPU:0 before, /device:TPU:11 now
where the time goes in v1:
time: 107 us; the launch traced here: 106 us
  starting transfers between devices  33.8 us (32%)
  waiting for transfers between devices  24.3 us (23%)
  Pallas kernels  21 us (20%)
  local copies, waits for them, and re-layouts  13.7 us (13%)
  between operations  13.5 us (13%)
    ppermute x15, starting transfers between devices, send(): return lax.ppermute(array, MESH, pairs(target))  33.8 us
    ppermute x15, waiting for transfers between devices, send(): return lax.ppermute(array, MESH, pairs(target))  24.3 us
    unnamed x47, local copies, waits for them, and re-layouts  13.7 us
    pallas_call x1, Pallas kernels, advance(): pl.pallas_call(advance_kernel, out_shape=shaped(LOCAL, PLANES, SIZE, SIZE...  7.47 us
    pallas_call x1, Pallas kernels, prepare(): pl.pallas_call(prepare_kernel, out_shape=[shaped(4 * CHUNK, SIZE), shaped...  4.73 us
    pallas_call x1, Pallas kernels, pack(): pl.pallas_call(pack_kernel, out_shape=[shaped(2 * CHUNK, SIZE)] * 4 + [sh...  2.38 us
    pallas_call x1, Pallas kernels, reduce(): pl.pallas_call(reduce_kernel, out_shape=shaped(2 * CHUNK + 2 * STRIP, SIZ...  2.27 us
  transfers between devices with their start and end apart: 16, of which 7 were waited for; matrix products, arithmetic and copies ran while one was open for 2% of the time, Pallas kernels for 8%

profile of v1, /device:TPU:11, one launch (start us, length us, event | category | flops | bytes accessed | tf_op | source)
XLA Modules:
  0.0 106.4 jit_solution(4724311445160706642)
XLA Ops:
  6.5 0.1 pad_add_fusion.place
  6.6 1.9 %copy-done.1 = f32[4,3,4,128,128]{4,3,2,1,0:T(8,128)S(1)} copy-done((f32[4,3,4,128,128]{4,3,2,1,0:T(8,128)S(1)}, f32[4,3,4,128,128]{4,3,2,1,0:T(8,128)}, u32[]{:S(2)}) %copy-start.1) | copy-done | bytes 3145752
  8.5 1.1 %copy-done.6 = f32[1,3,4,128,128]{4,3,2,1,0:T(8,128)S(1)} copy-done((f32[1,3,4,128,128]{4,3,2,1,0:T(8,128)S(1)}, f32[1,3,4,128,128]{4,3,2,1,0:T(8,128)}, u32[]{:S(2)}) %copy-start.6) | copy-done | bytes 786456
  9.6 0.7 copy-done.15
  10.3 4.7 %prepare.1 = (f32[768,128]{1,0:T(8,128)S(1)}, f32[864,128]{1,0:T(8,128)S(1)}, f32[384,128]{1,0:T(8,128)}) custom-call(s32[2]{0:T(128)S(1)} %pad_add_fusion.place, s32[16]{0:T(128)S(1)} %copy-done.15, f32[4,12,128,128]{3,2,1,0:T(8,128)S(1)} %bitcast.10, f32[12,128,128]{2,1,0:T(8,128)S(1)} %bitcast.12), custom_call_target="tpu_custom_call" | custom-call | flops 2000000 | bytes 5000000 | tf_op jit(solution)/shard_map/prepare/pallas_call | solution.py:135
  15.0 0.7 copy-done.10
  15.8 0.0 all-gather.2.cloned.1.call-update
  15.8 0.8 collective-permute-start
  16.6 1.4 %collective-permute-done.got = f32[864,128]{1,0:T(8,128)S(1)} collective-permute-done((f32[864,128]{1,0:T(8,128)S(1)}, f32[864,128]{1,0:T(8,128)S(1)}, u32[]{:S(2)}, u32[]{:S(2)}) %collective-permute-start) | collective-permute-done | bytes 442400 | tf_op jit(solution)/shard_map/ppermute | solution.py:35
  18.0 0.8 copy-done.16
  18.8 2.4 %pack.1 = (f32[384,128]{1,0:T(8,128)}, f32[384,128]{1,0:T(8,128)}, f32[384,128]{1,0:T(8,128)}, f32[384,128]{1,0:T(8,128)}, f32[192,128]{1,0:T(8,128)}) custom-call(f32[768,128]{1,0:T(8,128)} %copy-done.10, f32[864,128]{1,0:T(8,128)} %copy-done.7, f32[864,128]{1,0:T(8,128)} %copy-done.16), custom_call_target="tpu_custom_call" | custom-call | tf_op jit(solution)/shard_map/pack/pallas_call | solution.py:163
  21.1 1.6 %collective-permute-start.6 = (f32[192,128]{1,0:T(8,128)}, f32[192,128]{1,0:T(8,128)S(1)}, u32[]{:S(2)}, u32[]{:S(2)}) collective-permute-start(f32[192,128]{1,0:T(8,128)} %get-tuple-element.20), channel_id=1, source_target_pairs={{0,2},{1,3},{2,0},{3,1},{4,6},{5,7},{6,4},{7,5},{8,10},{9,11},{10,... | collective-permute-start | bytes 294920 | tf_op jit(solution)/shard_map/ppermute | solution.py:35
  22.8 4.3 %collective-permute-start.1 = (f32[384,128]{1,0:T(8,128)}, f32[384,128]{1,0:T(8,128)S(1)}, u32[]{:S(2)}, u32[]{:S(2)}) collective-permute-start(f32[384,128]{1,0:T(8,128)} %get-tuple-element.16), channel_id=1, source_target_pairs={{0,96},{1,113},{2,98},{3,115},{4,100},{5,117},{6,102},{7,119},{8,1... | collective-permute-start | bytes 589832 | tf_op jit(solution)/shard_map/ppermute | solution.py:35
  27.1 0.0 collective-permute-start.2
  27.1 0.3 collective-permute-start.3
  27.4 5.0 %collective-permute-start.4 = (f32[384,128]{1,0:T(8,128)}, f32[384,128]{1,0:T(8,128)}, u32[]{:S(2)}, u32[]{:S(2)}) collective-permute-start(f32[384,128]{1,0:T(8,128)} %get-tuple-element.19.own), channel_id=1, source_target_pairs={{1,33},{3,35},{5,37},{7,39},{9,41},{11,43},{13,45},{15,47},{17,49}... | collective-permute-start | bytes 589832 | tf_op jit(solution)/shard_map/ppermute | solution.py:35
  32.4 0.9 constant_dynamic-update-slice_fusion.1
  33.3 1.3 %collective-permute-start.9 = (f32[384,128]{1,0:T(8,128)S(1)}, f32[384,128]{1,0:T(8,128)}, u32[]{:S(2)}, u32[]{:S(2)}) collective-permute-start(f32[384,128]{1,0:T(8,128)S(1)} %constant_dynamic-update-slice_fusion.g0), channel_id=1, source_target_pairs={{0,12},{1,13},{2,14},{3,15},{4,8},{5,9},{6,10},{7,11},{8,4},{9,5},... | collective-permute-start | bytes 589832 | tf_op jit(solution)/shard_map/ppermute | solution.py:35
  34.6 0.0 collective-permute-done.1.a
  34.6 0.8 collective-permute-start.8
  35.5 2.3 %collective-permute-done.2.b = f32[384,128]{1,0:T(8,128)S(1)} collective-permute-done((f32[384,128]{1,0:T(8,128)}, f32[384,128]{1,0:T(8,128)S(1)}, u32[]{:S(2)}, u32[]{:S(2)}) %collective-permute-start.2) | collective-permute-done | bytes 196640 | tf_op jit(solution)/shard_map/ppermute | solution.py:35
  37.8 0.7 copy-done.19
  38.5 5.0 %collective-permute-start.7 = (f32[384,128]{1,0:T(8,128)S(1)}, f32[384,128]{1,0:T(8,128)}, u32[]{:S(2)}, u32[]{:S(2)}) collective-permute-start(f32[384,128]{1,0:T(8,128)S(1)} %constant_dynamic-update-slice_fusion.g0), channel_id=1, source_target_pairs={{0,4},{1,5},{2,6},{3,7},{4,0},{5,1},{6,2},{7,3},{8,12},{9,13},{10,... | collective-permute-start | bytes 589832 | tf_op jit(solution)/shard_map/ppermute | solution.py:35
  43.5 0.0 collective-permute-done.3.c
  43.5 0.0 collective-permute-done.4.d
  43.5 2.0 %add.3.acc = f32[384,128]{1,0:T(8,128)} custom-call(s32[2]{0:T(128)} %copy-done.13, f32[384,128]{1,0:T(8,128)} %copy-done.18, f32[384,128]{1,0:T(8,128)} %copy-done.19, f32[384,128]{1,0:T(8,128)} %collective-permute-done.3.c, f32[384,128]{1,0:T(8,128)} %collective-permute-done.4.d, f32[384,128]{1,0:T(8,128)} %get-tuple-element.19.own), custom_call_target="tpu_custom_call" | custom-call | tf_op jit(solution)/shard_map/add/pallas_call | solution.py:178
  45.5 0.0 collective-permute-start.5
  45.5 0.7 copy.8.neighbours
  46.2 0.7 copy.9.codes
  46.9 0.0 collective-permute-done.9.g3
  46.9 7.2 %collective-permute-done.7.g1 = f32[384,128]{1,0:T(8,128)} collective-permute-done((f32[384,128]{1,0:T(8,128)S(1)}, f32[384,128]{1,0:T(8,128)}, u32[]{:S(2)}, u32[]{:S(2)}) %collective-permute-start.7) | collective-permute-done | bytes 196640 | tf_op jit(solution)/shard_map/ppermute | solution.py:35
  54.1 2.3 %reduce.1.own = f32[576,128]{1,0:T(8,128)} custom-call(s32[2]{0:T(128)} %copy-done.13, s32[16,4]{1,0:T(8,128)} %copy.8.neighbours, s32[16,4]{1,0:T(8,128)} %copy.9.codes, f32[384,128]{1,0:T(8,128)} %add.3.acc, f32[384,128]{1,0:T(8,128)} %collective-permute-done.5.sib, f32[384,128]{1,0:T(8,128)} %copy-done.17, f32[384,128]{1,0:T(8,128)} %collective-permute-done.7.g1, ...), custom_call_target="tpu_custom_call" | custom-call | tf_op jit(solution)/shard_map/reduce/pallas_call | solution.py:210
  56.3 4.0 %collective-permute-start.13 = (f32[576,128]{1,0:T(8,128)}, f32[576,128]{1,0:T(8,128)S(1)}, u32[]{:S(2)}, u32[]{:S(2)}) collective-permute-start(f32[576,128]{1,0:T(8,128)} %reduce.1.own), channel_id=1, source_target_pairs={{1,33},{3,35},{5,37},{7,39},{9,41},{11,43},{13,45},{15,47},{17,49}... | collective-permute-start | bytes 884744 | tf_op jit(solution)/shard_map/ppermute | solution.py:35
  60.4 0.4 collective-permute-start.12
  60.8 5.2 %collective-permute-start.11 = (f32[576,128]{1,0:T(8,128)}, f32[576,128]{1,0:T(8,128)}, u32[]{:S(2)}, u32[]{:S(2)}) collective-permute-start(f32[576,128]{1,0:T(8,128)} %reduce.1.own), channel_id=1, source_target_pairs={{0,80},{1,65},{2,82},{3,67},{4,84},{5,69},{6,86},{7,71},{8,88},{9,... | collective-permute-start | bytes 884744 | tf_op jit(solution)/shard_map/ppermute | solution.py:35
  66.0 1.1 %collective-permute-start.10 = (f32[576,128]{1,0:T(8,128)}, f32[576,128]{1,0:T(8,128)}, u32[]{:S(2)}, u32[]{:S(2)}) collective-permute-start(f32[576,128]{1,0:T(8,128)} %reduce.1.own), channel_id=1, source_target_pairs={{0,96},{1,113},{2,98},{3,115},{4,100},{5,117},{6,102},{7,119},{8,1... | collective-permute-start | bytes 884744 | tf_op jit(solution)/shard_map/ppermute | solution.py:35
  67.1 0.9 collective-permute-done.13.d
  68.0 1.1 %collective-permute-done.12.c = f32[576,128]{1,0:T(8,128)} collective-permute-done((f32[576,128]{1,0:T(8,128)}, f32[576,128]{1,0:T(8,128)}, u32[]{:S(2)}, u32[]{:S(2)}) %collective-permute-start.12) | collective-permute-done | bytes 294944 | tf_op jit(solution)/shard_map/ppermute | solution.py:35
  69.1 9.7 %collective-permute-done.11.b = f32[576,128]{1,0:T(8,128)} collective-permute-done((f32[576,128]{1,0:T(8,128)}, f32[576,128]{1,0:T(8,128)}, u32[]{:S(2)}, u32[]{:S(2)}) %collective-permute-start.11) | collective-permute-done | bytes 294944 | tf_op jit(solution)/shard_map/ppermute | solution.py:35
  78.9 2.1 %share.1 = f32[864,128]{1,0:T(8,128)} custom-call(s32[2]{0:T(128)} %copy-done.13, f32[576,128]{1,0:T(8,128)} %collective-permute-done.10.a, f32[576,128]{1,0:T(8,128)} %collective-permute-done.11.b, f32[576,128]{1,0:T(8,128)} %collective-permute-done.12.c, f32[576,128]{1,0:T(8,128)} %copy-done.4, f32[576,128]{1,0:T(8,128)} %reduce.1.own), custom_call_target="tpu_custom_call" | custom-call | tf_op jit(solution)/shard_map/share/pallas_call | solution.py:229
  81.0 3.9 %collective-permute-start.14 = (f32[864,128]{1,0:T(8,128)}, f32[864,128]{1,0:T(8,128)S(1)}, u32[]{:S(2)}, u32[]{:S(2)}) collective-permute-start(f32[864,128]{1,0:T(8,128)} %share.1), channel_id=1, source_target_pairs={{0,1},{1,0},{2,3},{3,2},{4,5},{5,4},{6,7},{7,6},{8,9},{9,8},{10,11... | collective-permute-start | bytes 1327112 | tf_op jit(solution)/shard_map/ppermute | solution.py:35
  84.9 1.6 %collective-permute-done.14.got = f32[864,128]{1,0:T(8,128)S(1)} collective-permute-done((f32[864,128]{1,0:T(8,128)}, f32[864,128]{1,0:T(8,128)S(1)}, u32[]{:S(2)}, u32[]{:S(2)}) %collective-permute-start.14) | collective-permute-done | bytes 442400 | tf_op jit(solution)/shard_map/ppermute | solution.py:35
  86.5 0.8 copy-done.8
  87.3 1.9 %copy-done = f32[6144,128]{1,0:T(8,128)S(1)} copy-done((f32[6144,128]{1,0:T(8,128)S(1)}, f32[6144,128]{1,0:T(8,128)}, u32[]{:S(2)}) %copy-start) | copy-done | bytes 3145752
  89.2 1.0 copy-done.3
  90.1 1.0 copy-done.5
  91.1 1.0 copy-done.9
  92.1 7.5 %advance.1 = f32[4,12,128,128]{3,2,1,0:T(8,128)} custom-call(s32[2]{0:T(128)S(1)} %copy-done.14, s32[16,4]{1,0:T(8,128)S(1)} %copy-done.11, s32[16,4]{1,0:T(8,128)S(1)} %copy-done.12, f32[4,12,128,128]{3,2,1,0:T(8,128)S(1)} %bitcast.11, f32[16,4,96,128]{3,2,1,0:T(8,128)S(1)} %bitcast.6, f32[16,4,96,128]{3,2,1,0:T(8,128)S(1)} %bitcast.7, ...), custom_call_target="tpu_custom_call" | custom-call | flops 40000000 | bytes 8000000 | tf_op jit(solution)/shard_map/advance/pallas_call | solution.py:334
  (40 shorter events, 0.1 us)
Async XLA Ops:
  6.5 80.7 %all-gather.2.cloned.1.call-start = ((), (), s32[]{:S(2)}) async-start(), calls=%async_computation | async-start | bytes 3342336 | tf_op jit(solution)/shard_map/all_gather | solution.py:365
  6.6 36.9 %copy-start.13 = (s32[2]{0:T(128)}, s32[2]{0:T(128)S(1)}, u32[]{:S(2)}) copy-start(s32[2]{0:T(128)S(1)} %pad_add_fusion.place) | copy-start | bytes 28
  6.6 1.9 %copy-start.1 = (f32[4,3,4,128,128]{4,3,2,1,0:T(8,128)S(1)}, f32[4,3,4,128,128]{4,3,2,1,0:T(8,128)}, u32[]{:S(2)}) copy-start(f32[4,3,4,128,128]{4,3,2,1,0:T(8,128)} %param.5) | copy-start | bytes 9437188
  8.5 1.1 %copy-start.6 = (f32[1,3,4,128,128]{4,3,2,1,0:T(8,128)S(1)}, f32[1,3,4,128,128]{4,3,2,1,0:T(8,128)}, u32[]{:S(2)}) copy-start(f32[1,3,4,128,128]{4,3,2,1,0:T(8,128)} %param.6) | copy-start | bytes 2359300
  9.6 0.7 copy-start.15
  10.3 35.2 %copy-start.20 = (s32[16,4]{0,1:T(4,128)S(1)}, s32[16,4]{0,1:T(4,128)}, u32[]{:S(2)}) copy-start(s32[16,4]{0,1:T(4,128)} %param.8) | copy-start | bytes 772
  10.3 35.9 %copy-start.21 = (s32[16,4]{0,1:T(4,128)S(1)}, s32[16,4]{0,1:T(4,128)}, u32[]{:S(2)}) copy-start(s32[16,4]{0,1:T(4,128)} %param.9) | copy-start | bytes 772
  15.0 0.7 copy-start.10
  15.8 2.2 %copy-start.7 = (f32[864,128]{1,0:T(8,128)}, f32[864,128]{1,0:T(8,128)S(1)}, u32[]{:S(2)}) copy-start(f32[864,128]{1,0:T(8,128)S(1)} %get-tuple-element.15.give) | copy-start | bytes 1327108
  15.8 2.2 %collective-permute-start = (f32[864,128]{1,0:T(8,128)S(1)}, f32[864,128]{1,0:T(8,128)S(1)}, u32[]{:S(2)}, u32[]{:S(2)}) collective-permute-start(f32[864,128]{1,0:T(8,128)S(1)} %get-tuple-element.15.give), channel_id=1, source_target_pairs={{0,1},{1,0},{2,3},{3,2},{4,5},{5,4},{6,7},{7,6},{8,9},{9,8},{10,11... | collective-permute-start | bytes 1327112 | tf_op jit(solution)/shard_map/ppermute | solution.py:35
  18.0 0.8 copy-start.16
  18.8 68.5 %copy-start.2 = (f32[4,3,4,128,128]{4,3,2,1,0:T(8,128)S(1)}, f32[4,3,4,128,128]{4,3,2,1,0:T(8,128)}, u32[]{:S(2)}) copy-start(f32[4,3,4,128,128]{4,3,2,1,0:T(8,128)} %param.5) | copy-start | bytes 9437188
  21.1 12.2 %collective-permute-start.6 = (f32[192,128]{1,0:T(8,128)}, f32[192,128]{1,0:T(8,128)S(1)}, u32[]{:S(2)}, u32[]{:S(2)}) collective-permute-start(f32[192,128]{1,0:T(8,128)} %get-tuple-element.20), channel_id=1, source_target_pairs={{0,2},{1,3},{2,0},{3,1},{4,6},{5,7},{6,4},{7,5},{8,10},{9,11},{10,... | collective-permute-start | bytes 294920 | tf_op jit(solution)/shard_map/ppermute | solution.py:35
  22.8 11.8 %collective-permute-start.1 = (f32[384,128]{1,0:T(8,128)}, f32[384,128]{1,0:T(8,128)S(1)}, u32[]{:S(2)}, u32[]{:S(2)}) collective-permute-start(f32[384,128]{1,0:T(8,128)} %get-tuple-element.16), channel_id=1, source_target_pairs={{0,96},{1,113},{2,98},{3,115},{4,100},{5,117},{6,102},{7,119},{8,1... | collective-permute-start | bytes 589832 | tf_op jit(solution)/shard_map/ppermute | solution.py:35
  27.1 10.7 %collective-permute-start.2 = (f32[384,128]{1,0:T(8,128)}, f32[384,128]{1,0:T(8,128)S(1)}, u32[]{:S(2)}, u32[]{:S(2)}) collective-permute-start(f32[384,128]{1,0:T(8,128)} %get-tuple-element.17), channel_id=1, source_target_pairs={{0,80},{1,65},{2,82},{3,67},{4,84},{5,69},{6,86},{7,71},{8,88},{9,... | collective-permute-start | bytes 589832 | tf_op jit(solution)/shard_map/ppermute | solution.py:35
  27.1 16.4 %collective-permute-start.3 = (f32[384,128]{1,0:T(8,128)}, f32[384,128]{1,0:T(8,128)}, u32[]{:S(2)}, u32[]{:S(2)}) collective-permute-start(f32[384,128]{1,0:T(8,128)} %get-tuple-element.18), channel_id=1, source_target_pairs={{0,16},{1,49},{2,18},{3,51},{4,20},{5,53},{6,22},{7,55},{8,24},{9,... | collective-permute-start | bytes 589832 | tf_op jit(solution)/shard_map/ppermute | solution.py:35
  27.4 16.1 %collective-permute-start.4 = (f32[384,128]{1,0:T(8,128)}, f32[384,128]{1,0:T(8,128)}, u32[]{:S(2)}, u32[]{:S(2)}) collective-permute-start(f32[384,128]{1,0:T(8,128)} %get-tuple-element.19.own), channel_id=1, source_target_pairs={{1,33},{3,35},{5,37},{7,39},{9,41},{11,43},{13,45},{15,47},{17,49}... | collective-permute-start | bytes 589832 | tf_op jit(solution)/shard_map/ppermute | solution.py:35
  33.3 20.7 %copy-start.17 = (f32[384,128]{1,0:T(8,128)}, f32[384,128]{1,0:T(8,128)S(1)}, u32[]{:S(2)}) copy-start(f32[384,128]{1,0:T(8,128)S(1)} %constant_dynamic-update-slice_fusion.g0) | copy-start | bytes 589828
  33.3 13.6 %collective-permute-start.9 = (f32[384,128]{1,0:T(8,128)S(1)}, f32[384,128]{1,0:T(8,128)}, u32[]{:S(2)}, u32[]{:S(2)}) collective-permute-start(f32[384,128]{1,0:T(8,128)S(1)} %constant_dynamic-update-slice_fusion.g0), channel_id=1, source_target_pairs={{0,12},{1,13},{2,14},{3,15},{4,8},{5,9},{6,10},{7,11},{8,4},{9,5},... | collective-permute-start | bytes 589832 | tf_op jit(solution)/shard_map/ppermute | solution.py:35
  34.6 0.8 copy-start.18
  34.6 12.3 %collective-permute-start.8 = (f32[384,128]{1,0:T(8,128)S(1)}, f32[384,128]{1,0:T(8,128)}, u32[]{:S(2)}, u32[]{:S(2)}) collective-permute-start(f32[384,128]{1,0:T(8,128)S(1)} %constant_dynamic-update-slice_fusion.g0), channel_id=1, source_target_pairs={{0,8},{1,9},{2,10},{3,11},{4,12},{5,13},{6,14},{7,15},{8,0},{9,1},... | collective-permute-start | bytes 589832 | tf_op jit(solution)/shard_map/ppermute | solution.py:35
  37.8 0.7 copy-start.19
  38.5 15.6 %collective-permute-start.7 = (f32[384,128]{1,0:T(8,128)S(1)}, f32[384,128]{1,0:T(8,128)}, u32[]{:S(2)}, u32[]{:S(2)}) collective-permute-start(f32[384,128]{1,0:T(8,128)S(1)} %constant_dynamic-update-slice_fusion.g0), channel_id=1, source_target_pairs={{0,4},{1,5},{2,6},{3,7},{4,0},{5,1},{6,2},{7,3},{8,12},{9,13},{10,... | collective-permute-start | bytes 589832 | tf_op jit(solution)/shard_map/ppermute | solution.py:35
  45.5 41.7 %copy-start.14 = (s32[2]{0:T(128)S(1)}, s32[2]{0:T(128)}, u32[]{:S(2)}) copy-start(s32[2]{0:T(128)} %copy-done.13) | copy-start | bytes 28
  45.5 8.5 %collective-permute-start.5 = (f32[384,128]{1,0:T(8,128)}, f32[384,128]{1,0:T(8,128)}, u32[]{:S(2)}, u32[]{:S(2)}) collective-permute-start(f32[384,128]{1,0:T(8,128)} %add.3.acc), channel_id=1, source_target_pairs={{0,1},{1,0},{2,3},{3,2},{4,5},{5,4},{6,7},{7,6},{8,9},{9,8},{10,11... | collective-permute-start | bytes 589832 | tf_op jit(solution)/shard_map/ppermute | solution.py:35
  46.2 41.1 %copy-start.11 = (s32[16,4]{1,0:T(8,128)S(1)}, s32[16,4]{1,0:T(8,128)}, u32[]{:S(2)}) copy-start(s32[16,4]{1,0:T(8,128)} %copy.8.neighbours) | copy-start | bytes 772
  46.9 40.4 %copy-start.12 = (s32[16,4]{1,0:T(8,128)S(1)}, s32[16,4]{1,0:T(8,128)}, u32[]{:S(2)}) copy-start(s32[16,4]{1,0:T(8,128)} %copy.9.codes) | copy-start | bytes 772
  56.3 11.7 %collective-permute-start.13 = (f32[576,128]{1,0:T(8,128)}, f32[576,128]{1,0:T(8,128)S(1)}, u32[]{:S(2)}, u32[]{:S(2)}) collective-permute-start(f32[576,128]{1,0:T(8,128)} %reduce.1.own), channel_id=1, source_target_pairs={{1,33},{3,35},{5,37},{7,39},{9,41},{11,43},{13,45},{15,47},{17,49}... | collective-permute-start | bytes 884744 | tf_op jit(solution)/shard_map/ppermute | solution.py:35
  60.4 8.8 %collective-permute-start.12 = (f32[576,128]{1,0:T(8,128)}, f32[576,128]{1,0:T(8,128)}, u32[]{:S(2)}, u32[]{:S(2)}) collective-permute-start(f32[576,128]{1,0:T(8,128)} %reduce.1.own), channel_id=1, source_target_pairs={{0,16},{1,49},{2,18},{3,51},{4,20},{5,53},{6,22},{7,55},{8,24},{9,... | collective-permute-start | bytes 884744 | tf_op jit(solution)/shard_map/ppermute | solution.py:35
  60.8 18.1 %collective-permute-start.11 = (f32[576,128]{1,0:T(8,128)}, f32[576,128]{1,0:T(8,128)}, u32[]{:S(2)}, u32[]{:S(2)}) collective-permute-start(f32[576,128]{1,0:T(8,128)} %reduce.1.own), channel_id=1, source_target_pairs={{0,80},{1,65},{2,82},{3,67},{4,84},{5,69},{6,86},{7,71},{8,88},{9,... | collective-permute-start | bytes 884744 | tf_op jit(solution)/shard_map/ppermute | solution.py:35
  66.0 12.8 %collective-permute-start.10 = (f32[576,128]{1,0:T(8,128)}, f32[576,128]{1,0:T(8,128)}, u32[]{:S(2)}, u32[]{:S(2)}) collective-permute-start(f32[576,128]{1,0:T(8,128)} %reduce.1.own), channel_id=1, source_target_pairs={{0,96},{1,113},{2,98},{3,115},{4,100},{5,117},{6,102},{7,119},{8,1... | collective-permute-start | bytes 884744 | tf_op jit(solution)/shard_map/ppermute | solution.py:35
  68.0 10.8 %copy-start.4 = (f32[576,128]{1,0:T(8,128)}, f32[576,128]{1,0:T(8,128)S(1)}, u32[]{:S(2)}) copy-start(f32[576,128]{1,0:T(8,128)S(1)} %collective-permute-done.13.d) | copy-start | bytes 884740
  81.0 5.5 %collective-permute-start.14 = (f32[864,128]{1,0:T(8,128)}, f32[864,128]{1,0:T(8,128)S(1)}, u32[]{:S(2)}, u32[]{:S(2)}) collective-permute-start(f32[864,128]{1,0:T(8,128)} %share.1), channel_id=1, source_target_pairs={{0,1},{1,0},{2,3},{3,2},{4,5},{5,4},{6,7},{7,6},{8,9},{9,8},{10,11... | collective-permute-start | bytes 1327112 | tf_op jit(solution)/shard_map/ppermute | solution.py:35
  86.5 0.8 copy-start.8
  87.3 1.9 %copy-start = (f32[6144,128]{1,0:T(8,128)S(1)}, f32[6144,128]{1,0:T(8,128)}, u32[]{:S(2)}) copy-start(f32[6144,128]{1,0:T(8,128)} %all-gather.2.cloned.1.call-done) | copy-start | bytes 9437188
  89.2 1.0 copy-start.3
  90.1 1.0 copy-start.5
  91.1 1.0 copy-start.9
Sparse Core Ops, SparseCore 0:
  15.9 45.8 all-gather.1

commit v2 on v1

v2 whole, which is shorter than its diff:
```python
import jax
import jax.numpy as jnp
from jax import lax
from jax.experimental import pallas as pl
from jax.experimental.pallas import tpu as pltpu
from jax.sharding import PartitionSpec as P

MESH = ("member", "domain")
N_MEMBER = 8
N_DOMAIN = 16
SIZE = 128
PLANES = 12
LEV = 4
LOCAL = 4
MEMBERS = 32
ROWS = PLANES * SIZE
CHUNK = ROWS // N_MEMBER
OFFSETS = ((6, 5, 1, 0), (7, 4, 3, 2))
TAKEN = 20
SLOT = 32
RECORD = 4 * SLOT
USED = 16
STRIP = 4 * USED
MAIN = 4 * CHUNK
F32 = jnp.float32


def pairs(target):
    out = []
    for m in range(N_MEMBER):
        for d in range(N_DOMAIN):
            to = target(m, d)
            if to is not None:
                out.append((m * N_DOMAIN + d, to[0] * N_DOMAIN + to[1]))
    return out


def send(array, target):
    return lax.ppermute(array, MESH, pairs(target))


def swap_cores(array):
    return send(array, lambda m, d: (m, d ^ 1))


def exchange(messages, order=(0, 1, 2, 3)):
    out = [None] * 4
    for j in order:
        message = messages[j]

        def target(m, d, j=j):
            offset = OFFSETS[d % 2][j]
            return (m ^ offset, d) if offset else None

        out[j] = send(message, target)
    return out


def over_x(array):
    return [send(array, lambda m, d, x=x: (m, d ^ (4 * x))) for x in (1, 2, 3)]


def vmem():
    return pl.BlockSpec(memory_space=pltpu.VMEM)


def hbm():
    return pl.BlockSpec(memory_space=pltpu.HBM)


def shaped(*rows):
    return [jax.ShapeDtypeStruct((r, SIZE), F32) for r in rows]


def on(space, *arrays):
    return [pltpu.with_memory_space_constraint(x, space) for x in arrays]


def limit(mib):
    return pltpu.CompilerParams(vmem_limit_bytes=mib << 20)


def here():
    return lax.axis_index("member"), lax.axis_index("domain")


def slot_chunk(member, core, j):
    zero, one = OFFSETS[0][j % 4], OFFSETS[1][j % 4]
    if j >= 4:
        zero, one = one, zero
    return member ^ jnp.where(core == 0, zero, one)


def prepare_kernel(owner_hbm, ens_hbm, ctl_hbm, keep, give, stay, leave, ens, ctl, part, tile, turned, lines, edge, owner, sems, osem):
    member, patch = here()
    core, z = patch % 2, (patch // 2) % 2
    table = pltpu.make_async_copy(owner_hbm, owner, osem)
    table.start()
    copies = []
    for i in range(PLANES):
        a = pltpu.make_async_copy(ens_hbm.at[:, i], ens.at[:, i], sems.at[0, i])
        b = pltpu.make_async_copy(ctl_hbm.at[i], ctl.at[i], sems.at[1, i])
        a.start()
        b.start()
        copies.append((a, b))
    table.wait()
    flag = jnp.where(owner[patch] == member, 1.0, 0.0).astype(F32)
    for i in range(PLANES):
        for c in copies[i]:
            c.wait()
        spots = [(a // 2, (a % 2) * PLANES + i) for a in range(LOCAL)] + [(0, 24 + i) if i < 8 else (1, 16 + i)]
        for r in range(0, SIZE, 32):
            rows = pl.ds(r, 32)
            group = lax.broadcasted_iota(jnp.int32, (32, SIZE), 1) // 4
            xs = [ens[a, i, rows, :] for a in range(LOCAL)]
            total = (xs[0] + xs[1]) + (xs[2] + xs[3])
            value = flag * ctl[i, rows, :] - total * (1.0 / MEMBERS)
            part[pl.ds(i * SIZE + r, 32), :] = value
            for t in (0, 1):
                acc = tile[t, rows, :]
                for (where, s), x in zip(spots, xs + [value]):
                    if where == t:
                        acc = jnp.where(group == s, pltpu.roll(x, (4 * s + 2) % SIZE, 1), acc)
                tile[t, rows, :] = acc
        for side, k, row in ((0, 0, 0), (0, 1, 1), (1, 0, SIZE - 1), (1, 1, SIZE - 2)):
            at = k * PLANES + i
            if at < TAKEN:
                for a in range(LOCAL):
                    lines[a, side, at : at + 1, :] = ens[a, i, row : row + 1, :]
                edge[side, at : at + 1, :] = part[i * SIZE + row : i * SIZE + row + 1, :]
    turned[0] = tile[0].T
    turned[1] = tile[1].T
    for side, k, q in ((2, 0, 2), (2, 1, 3), (3, 0, 1), (3, 1, 0)):
        count = 8 if k else PLANES
        at = k * PLANES
        for a in range(LOCAL):
            lines[a, side, at : at + count, :] = turned[a // 2, pl.ds((a % 2) * 48 + q, count, stride=4), :]
        edge[side, at : at + 8, :] = turned[0, pl.ds(96 + q, 8, stride=4), :]
        if k == 0:
            edge[side, 8:12, :] = turned[1, pl.ds(96 + q, 4, stride=4), :]
    for out, who in ((stay, z), (leave, 1 - z)):
        for c in (0, 1):
            for side in range(4):
                at = c * RECORD + side * SLOT
                out[at : at + TAKEN, :] = lines[2 * c + who, side, 0:TAKEN, :]
                out[at + 20 : at + 30, :] = edge[side, 10 * c : 10 * c + 10, :]
                out[at + 30 : at + 32, :] = jnp.zeros((2, SIZE), F32)
    for j in range(4):
        own = pl.multiple_of(slot_chunk(member, core, j) * CHUNK, 8)
        other = pl.multiple_of(slot_chunk(member, core, j + 4) * CHUNK, 8)
        keep[j * CHUNK : (j + 1) * CHUNK, :] = part[pl.ds(own, CHUNK), :]
        give[j * CHUNK : (j + 1) * CHUNK, :] = part[pl.ds(other, CHUNK), :]


def prepare(owner, ensemble, control):
    return pl.pallas_call(
        prepare_kernel,
        out_shape=shaped(MAIN, MAIN, 2 * RECORD, 2 * RECORD),
        in_specs=[hbm()] * 3,
        out_specs=[vmem()] * 4,
        scratch_shapes=[
            pltpu.VMEM((LOCAL, PLANES, SIZE, SIZE), F32),
            pltpu.VMEM((PLANES, SIZE, SIZE), F32),
            pltpu.VMEM((ROWS, SIZE), F32),
            pltpu.VMEM((2, SIZE, SIZE), F32),
            pltpu.VMEM((2, SIZE, SIZE), F32),
            pltpu.VMEM((LOCAL, 4, 24, SIZE), F32),
            pltpu.VMEM((4, 24, SIZE), F32),
            pltpu.SMEM((N_DOMAIN,), jnp.int32),
            pltpu.SemaphoreType.DMA((2, PLANES)),
            pltpu.SemaphoreType.DMA,
        ],
        compiler_params=limit(12),
        cost_estimate=pl.CostEstimate(flops=2_000_000, bytes_accessed=5_000_000, transcendentals=0),
        name="prepare",
    )(*on(pltpu.HBM, owner, ensemble, control))


def small(kernel, name, rows, arrays):
    one = isinstance(rows, int)
    return pl.pallas_call(
        kernel,
        out_shape=shaped(rows)[0] if one else shaped(*rows),
        in_specs=[vmem()] * len(arrays),
        out_specs=vmem() if one else [vmem()] * len(rows),
        compiler_params=limit(4),
        name=name,
    )(*on(pltpu.VMEM, *arrays))


def pack_kernel(keep, got, m0, m1, m2, m3):
    for j, m in enumerate((m0, m1, m2, m3)):
        m[0:CHUNK, :] = keep[j * CHUNK : (j + 1) * CHUNK, :]
        m[CHUNK:, :] = got[j * CHUNK : (j + 1) * CHUNK, :]


def split_kernel(stay, came, out):
    _, patch = here()
    rows = pl.ds(pl.multiple_of((1 - patch % 2) * RECORD, 8), RECORD)
    out[0:RECORD, :] = stay[rows, :]
    out[RECORD:, :] = came[rows, :]


def group_kernel(stay, came, got, out):
    _, patch = here()
    rows = pl.ds(pl.multiple_of((patch % 2) * RECORD, 8), RECORD)
    out[0:RECORD, :] = stay[rows, :]
    out[RECORD : 2 * RECORD, :] = got[0:RECORD, :]
    out[2 * RECORD : 3 * RECORD, :] = came[rows, :]
    out[3 * RECORD :, :] = got[RECORD:, :]


def pick_kernel(table_hbm, g0, g1, g3, g2, stay, leave, half, table, sem):
    _, patch = here()
    copy = pltpu.make_async_copy(table_hbm, table, sem)
    copy.start()
    copy.wait()
    for q in range(4):
        to, base, rows = (stay, leave)[q // 2], (q % 2) * STRIP, SLOT if q < 2 else 24
        for side in range(4):
            spot = (patch ^ q) * 4 + side
            away = table[spot] ^ patch
            code = table[64 + spot]
            source = pl.ds(pl.multiple_of((away % 4) * RECORD + (code % 4) * SLOT, 8), rows)
            value = g0[source, :]
            for x, g in ((1, g1), (2, g2), (3, g3)):
                value = jnp.where(away // 4 == x, g[source, :], value)
            lane = lax.broadcasted_iota(jnp.int32, value.shape, 1)
            value = jnp.take_along_axis(value, jnp.where(code // 4 == 1, SIZE - 1 - lane, lane), axis=1)
            at, depth = base + side * USED, 16 if side < 2 else 12
            to[at : at + PLANES, :] = value[0:PLANES]
            to[at + PLANES : at + USED, :] = value[depth : depth + LEV]
            if q < 2:
                half[at : at + 10, :] = value[20:30]
                half[at + 10 : at + USED, :] = jnp.zeros((6, SIZE), F32)


def pick(table, g0, g1, g2, g3):
    return pl.pallas_call(
        pick_kernel,
        out_shape=shaped(*[2 * STRIP] * 3),
        in_specs=[hbm()] + [vmem()] * 4,
        out_specs=[vmem()] * 3,
        scratch_shapes=[pltpu.SMEM((128,), jnp.int32), pltpu.SemaphoreType.DMA],
        compiler_params=limit(4),
        name="pick",
    )(*on(pltpu.HBM, table), *on(pltpu.VMEM, g0, g1, g3, g2))


def add_kernel(a, b, c, d, own, out):
    _, patch = here()
    out[...] = (a[...] + b[...]) + (c[...] + jnp.where(patch % 2 == 0, own[...], d[...]))


def reduce_kernel(acc, sib, half, sib_half, out):
    _, patch = here()
    first = patch % 2 == 0
    out[0:CHUNK, :] = acc[0:CHUNK, :] + sib[CHUNK : 2 * CHUNK, :]
    out[CHUNK : 2 * CHUNK, :] = acc[CHUNK : 2 * CHUNK, :] + sib[0:CHUNK, :]
    for q in (0, 1):
        for side in range(4):
            at = q * STRIP + side * USED
            mine = half[at : at + USED, :]
            at = (1 - q) * STRIP + side * USED
            other = sib_half[at : at + USED, :]
            low, high = jnp.where(first, mine, other), jnp.where(first, other, mine)
            at, depth = 2 * CHUNK + q * STRIP + side * USED, 6 if side < 2 else 2
            out[at : at + 10, :] = low[0:10]
            out[at + 10 : at + 12, :] = high[0:2]
            out[at + 12 : at + 16, :] = high[depth : depth + LEV]


def share_kernel(own, d, c, b, a, stay, back, out):
    _, patch = here()
    first = patch % 2 == 0
    rows = slice(CHUNK, 2 * CHUNK)
    for j, m in enumerate((a, b, c)):
        out[j * CHUNK : (j + 1) * CHUNK, :] = m[rows, :]
    out[3 * CHUNK : 4 * CHUNK, :] = jnp.where(first, own[rows, :], d[rows, :])
    rows = slice(2 * CHUNK + STRIP, 2 * CHUNK + 2 * STRIP)
    out[MAIN : MAIN + STRIP, :] = (a[rows, :] + b[rows, :]) + (c[rows, :] + jnp.where(first, own[rows, :], d[rows, :]))
    out[MAIN + STRIP : MAIN + 2 * STRIP, :] = stay[STRIP:, :]
    out[MAIN + 2 * STRIP :, :] = back[STRIP:, :]


def slope(x):
    lane = lax.broadcasted_iota(jnp.int32, x.shape, 1)
    ahead = jnp.where(lane == SIZE - 1, 0.0, pltpu.roll(x, SIZE - 1, 1))
    behind = jnp.where(lane == 0, 0.0, pltpu.roll(x, 1, 1))
    return ahead - behind


def advance_kernel(ens, stay, back, own, d, c, b, a, got, out, shift, rims, lines, columns, pad, div, slope_u):
    step = pl.program_id(0)

    @pl.when(step == 0)
    def _():
        member, patch = here()
        core, z = patch % 2, (patch // 2) % 2
        first = core == 0
        for j, m in enumerate((a, b, c, d)):
            value = m[0:CHUNK, :]
            if j == 3:
                value = jnp.where(first, own[0:CHUNK, :], value)
            shift[pl.ds(pl.multiple_of(slot_chunk(member, core, j) * CHUNK, 8), CHUNK), :] = value
            at = pl.multiple_of(slot_chunk(member, core, j + 4) * CHUNK, 8)
            shift[pl.ds(at, CHUNK), :] = got[j * CHUNK : (j + 1) * CHUNK, :]
        for side in range(4):
            rows = slice(2 * CHUNK + side * USED, 2 * CHUNK + (side + 1) * USED)
            moved = (a[rows, :] + b[rows, :]) + (c[rows, :] + jnp.where(first, own[rows, :], d[rows, :]))
            moved = moved + got[MAIN + side * USED : MAIN + (side + 1) * USED, :]
            rows = slice(side * USED, (side + 1) * USED)
            for source, who in (
                (stay[rows, :], 2 * core + z),
                (back[rows, :], 2 * core + 1 - z),
                (got[MAIN + STRIP + side * USED : MAIN + STRIP + (side + 1) * USED, :], 2 - 2 * core + z),
                (got[MAIN + 2 * STRIP + side * USED : MAIN + 2 * STRIP + (side + 1) * USED, :], 3 - 2 * core - z),
            ):
                rims[who, side] = source + moved
        for n in range(LOCAL):
            at = n * 32
            lines[pl.ds(at, PLANES, stride=2), :] = rims[n, 3, 0:PLANES, :]
            lines[pl.ds(at + 1, PLANES, stride=2), :] = rims[n, 2, 0:PLANES, :]
            right = 0.5 * (rims[n, 3, PLANES:USED, :] + slope(rims[n, 3, LEV : 2 * LEV, :]))
            left = 0.5 * (slope(rims[n, 2, LEV : 2 * LEV, :]) - rims[n, 2, PLANES:USED, :])
            lines[pl.ds(at + 24, LEV, stride=2), :] = right
            lines[pl.ds(at + 25, LEV, stride=2), :] = left
        turned = lines[...].T
        for n in range(LOCAL):
            columns[n] = turned if n == 0 else pltpu.roll(turned, SIZE - 32 * n, 1)

    part = 32
    lane = lax.broadcasted_iota(jnp.int32, (part, SIZE), 1)
    at_left, at_right = lane == 0, lane == SIZE - 1

    def across(x, r, line):
        edge = pltpu.roll(columns[step, r : r + part, :], (SIZE - 1 - 2 * line) % SIZE, 1)
        return jnp.where(at_right, edge, pltpu.roll(x, SIZE - 1, 1)) - jnp.where(at_left, edge, pltpu.roll(x, 1, 1))

    for lev in range(LEV):
        for f in range(3):
            i = f * LEV + lev
            pad[f, 8 : 8 + SIZE, :] = ens[step, i] + shift[i * SIZE : (i + 1) * SIZE, :]
            pad[f, 7:8, :] = rims[step, 0, i : i + 1, :]
            pad[f, 8 + SIZE : 9 + SIZE, :] = rims[step, 1, i : i + 1, :]
        i = PLANES + lev
        div[7:8, :] = 0.5 * (slope(pad[0, 7:8, :]) + pad[1, 8:9, :] - rims[step, 0, i : i + 1, :])
        div[8 + SIZE : 9 + SIZE, :] = 0.5 * (
            slope(pad[0, 8 + SIZE : 9 + SIZE, :]) + rims[step, 1, i : i + 1, :] - pad[1, 7 + SIZE : 8 + SIZE, :]
        )
        for r in range(0, SIZE, part):
            at = 8 + r
            du = across(pad[0, at : at + part, :], r, lev)
            slope_u[r : r + part, :] = du
            div[at : at + part, :] = 0.5 * (du + pad[1, at + 1 : at + 1 + part, :] - pad[1, at - 1 : at - 1 + part, :])
        for r in range(0, SIZE, part):
            at = 8 + r
            now = slice(at, at + part)
            up, down = slice(at - 1, at - 1 + part), slice(at + 1, at + 1 + part)
            u, v, w = pad[0, now, :], pad[1, now, :], pad[2, now, :]
            edge = pltpu.roll(columns[step, r : r + part, :], (SIZE - 1 - 2 * (PLANES + lev)) % SIZE, 1)
            edge = edge + jnp.where(at_left, 0.5 * u, -0.5 * u)
            mid = div[now, :]
            grad_x = jnp.where(at_right, edge, pltpu.roll(mid, SIZE - 1, 1)) - jnp.where(at_left, edge, pltpu.roll(mid, 1, 1))
            grad_y = div[down, :] - div[up, :]
            new_u = u - 0.2 * (u * slope_u[r : r + part, :] + v * (pad[0, down, :] - pad[0, up, :]))
            new_v = v - 0.2 * (u * across(v, r, LEV + lev) + v * (pad[1, down, :] - pad[1, up, :]))
            new_w = w - 0.2 * (u * across(w, r, 2 * LEV + lev) + v * (pad[2, down, :] - pad[2, up, :]))
            out[0, lev, r : r + part, :] = new_u + 0.1 * grad_x
            out[0, LEV + lev, r : r + part, :] = new_v + 0.1 * grad_y
            out[0, 2 * LEV + lev, r : r + part, :] = new_w


def advance(ensemble, stay, back, received, own, got):
    return pl.pallas_call(
        advance_kernel,
        out_shape=jax.ShapeDtypeStruct((LOCAL, PLANES, SIZE, SIZE), F32),
        grid=(LOCAL,),
        in_specs=[vmem()] * 9,
        out_specs=pl.BlockSpec((1, PLANES, SIZE, SIZE), lambda n: (n, 0, 0, 0)),
        scratch_shapes=[
            pltpu.VMEM((ROWS, SIZE), F32),
            pltpu.VMEM((LOCAL, 4, USED, SIZE), F32),
            pltpu.VMEM((SIZE, SIZE), F32),
            pltpu.VMEM((LOCAL, SIZE, SIZE), F32),
            pltpu.VMEM((3, SIZE + 16, SIZE), F32),
            pltpu.VMEM((SIZE + 16, SIZE), F32),
            pltpu.VMEM((SIZE, SIZE), F32),
        ],
        compiler_params=limit(12),
        cost_estimate=pl.CostEstimate(flops=40_000_000, bytes_accessed=8_000_000, transcendentals=0),
        name="advance",
    )(*on(pltpu.VMEM, ensemble, stay, back, own, *received[::-1], got))


def on_device(ensemble, control, owner, neighbours, codes):
    shape = ensemble.shape
    ensemble = ensemble.reshape(LOCAL, PLANES, SIZE, SIZE)
    control = control.reshape(PLANES, SIZE, SIZE)
    table = jnp.concatenate([neighbours.reshape(-1), codes.reshape(-1)])

    keep, give, stay, leave = prepare(owner, ensemble, control)
    came = send(leave, lambda m, d: (m, d ^ 2))
    got = swap_cores(give)
    messages = small(pack_kernel, "pack", [2 * CHUNK] * 4, [keep, got])
    received = exchange(messages)
    got = swap_cores(small(split_kernel, "split", 2 * RECORD, [stay, came]))
    group = small(group_kernel, "group", 4 * RECORD, [stay, came, got])
    acc = small(add_kernel, "add", 2 * CHUNK, received + [messages[3]])
    stay, leave, half = pick(table, group, *over_x(group))
    back = send(leave, lambda m, d: (m, d ^ 2))
    reduced = small(
        reduce_kernel, "reduce", 2 * CHUNK + 2 * STRIP, [acc, swap_cores(acc), half, swap_cores(half)]
    )
    received = exchange([reduced] * 4)
    got = swap_cores(
        small(share_kernel, "share", MAIN + 3 * STRIP, [reduced, *received[::-1], stay, back])
    )
    out = advance(ensemble, stay, back, received, reduced, got)
    return out.reshape(shape)


def solution(mesh):
    spec = P("member", None, None, "domain", None)
    return jax.shard_map(
        on_device, mesh=mesh, in_specs=(spec, spec, P(), P(), P()), out_specs=spec, check_vma=False
    )
```

time: 107 us -> 67.7 us (0.63)
  the two profiles are of different devices: /device:TPU:11 before, /device:TPU:1 now
where the time goes in v2:
time: 67.7 us; the launch traced here: 67.5 us
  starting transfers between devices  34.7 us (51%)
  waiting for transfers between devices  19.1 us (28%)
  Pallas kernels  12.6 us (19%)
    ppermute x18, starting transfers between devices, send(): return lax.ppermute(array, MESH, pairs(target))  34.7 us
    ppermute x18, waiting for transfers between devices, send(): return lax.ppermute(array, MESH, pairs(target))  19.1 us
    pallas_call x1, Pallas kernels, advance(): pl.pallas_call(advance_kernel, out_shape=jax.ShapeDtypeStruct((LOCAL, PLA...  5.37 us
    pallas_call x1, Pallas kernels, prepare(): pl.pallas_call(prepare_kernel, out_shape=shaped(MAIN, MAIN, 2 * RECORD, 2...  3.25 us
    pallas_call x1, Pallas kernels, pick(): pl.pallas_call(pick_kernel, out_shape=shaped(*[2 * STRIP] * 3), in_specs=...  2.12 us
    pallas_call x6, Pallas kernels, small(): pl.pallas_call(kernel, out_shape=shaped(rows)[0] if one else shaped(*rows...  1.91 us
  transfers between devices with their start and end apart: 18, of which 7 were waited for; matrix products, arithmetic and copies ran while one was open for 1% of the time, Pallas kernels for 4%

profile of v2, /device:TPU:1, one launch (start us, length us, event | category | flops | bytes accessed | tf_op | source)
XLA Modules:
  0.0 67.5 jit_solution(2953353092027018340)
XLA Ops:
  0.0 3.3 %prepare.1 = (f32[768,128]{1,0:T(8,128)S(1)}, f32[768,128]{1,0:T(8,128)S(1)}, f32[256,128]{1,0:T(8,128)S(1)}, f32[256,128]{1,0:T(8,128)S(1)}) custom-call(s32[16]{0:T(128)} %owner_hbm.1, f32[4,12,128,128]{3,2,1,0:T(8,128)} %bitcast.3, f32[12,128,128]{2,1,0:T(8,128)} %bitcast.5), custom_call_target="tpu_custom_call" | custom-call | flops 2000000 | bytes 5000000 | tf_op jit(solution)/shard_map/prepare/pallas_call | solution.py:156
  3.3 1.5 %collective-permute-start.6 = (f32[768,128]{1,0:T(8,128)S(1)}, f32[768,128]{1,0:T(8,128)S(1)}, u32[]{:S(2)}, u32[]{:S(2)}) collective-permute-start(f32[768,128]{1,0:T(8,128)S(1)} %get-tuple-element.21), channel_id=1, source_target_pairs={{0,1},{1,0},{2,3},{3,2},{4,5},{5,4},{6,7},{7,6},{8,9},{9,8},{10,11... | collective-permute-start | bytes 1179656 | tf_op jit(solution)/shard_map/ppermute | solution.py:39
  4.8 1.7 %collective-permute-start = (f32[256,128]{1,0:T(8,128)S(1)}, f32[256,128]{1,0:T(8,128)S(1)}, u32[]{:S(2)}, u32[]{:S(2)}) collective-permute-start(f32[256,128]{1,0:T(8,128)S(1)} %get-tuple-element.17), channel_id=1, source_target_pairs={{0,2},{1,3},{2,0},{3,1},{4,6},{5,7},{6,4},{7,5},{8,10},{9,11},{10,... | collective-permute-start | bytes 393224 | tf_op jit(solution)/shard_map/ppermute | solution.py:39
  6.5 0.0 collective-permute-done.6.got
  6.5 0.1 pack.1
  6.6 0.0 copy-start
  6.6 5.8 %collective-permute-start.7 = (f32[384,128]{1,0:T(8,128)S(1)}, f32[384,128]{1,0:T(8,128)S(1)}, u32[]{:S(2)}, u32[]{:S(2)}) collective-permute-start(f32[384,128]{1,0:T(8,128)S(1)} %get-tuple-element.22), channel_id=1, source_target_pairs={{0,96},{1,113},{2,98},{3,115},{4,100},{5,117},{6,102},{7,119},{8,1... | collective-permute-start | bytes 589832 | tf_op jit(solution)/shard_map/ppermute | solution.py:39
  12.4 0.0 collective-permute-start.8
  12.4 0.0 collective-permute-done.came
  12.4 1.0 %collective-permute-start.1 = (f32[256,128]{1,0:T(8,128)S(1)}, f32[256,128]{1,0:T(8,128)S(1)}, u32[]{:S(2)}, u32[]{:S(2)}) collective-permute-start(f32[256,128]{1,0:T(8,128)S(1)} %split.1), channel_id=1, source_target_pairs={{0,1},{1,0},{2,3},{3,2},{4,5},{5,4},{6,7},{7,6},{8,9},{9,8},{10,11... | collective-permute-start | bytes 393224 | tf_op jit(solution)/shard_map/ppermute | solution.py:39
  13.4 0.7 %collective-permute-start.9 = (f32[384,128]{1,0:T(8,128)S(1)}, f32[384,128]{1,0:T(8,128)S(1)}, u32[]{:S(2)}, u32[]{:S(2)}) collective-permute-start(f32[384,128]{1,0:T(8,128)S(1)} %get-tuple-element.24), channel_id=1, source_target_pairs={{0,16},{1,49},{2,18},{3,51},{4,20},{5,53},{6,22},{7,55},{8,24},{9,... | collective-permute-start | bytes 589832 | tf_op jit(solution)/shard_map/ppermute | solution.py:39
  14.1 4.0 %collective-permute-start.10 = (f32[384,128]{1,0:T(8,128)S(1)}, f32[384,128]{1,0:T(8,128)S(1)}, u32[]{:S(2)}, u32[]{:S(2)}) collective-permute-start(f32[384,128]{1,0:T(8,128)S(1)} %get-tuple-element.25.own), channel_id=1, source_target_pairs={{1,33},{3,35},{5,37},{7,39},{9,41},{11,43},{13,45},{15,47},{17,49}... | collective-permute-start | bytes 589832 | tf_op jit(solution)/shard_map/ppermute | solution.py:39
  18.1 0.0 collective-permute-done.1.got
  18.2 2.8 %collective-permute-start.4 = (f32[512,128]{1,0:T(8,128)S(1)}, f32[512,128]{1,0:T(8,128)}, u32[]{:S(2)}, u32[]{:S(2)}) collective-permute-start(f32[512,128]{1,0:T(8,128)S(1)} %group.1.g0), channel_id=1, source_target_pairs={{0,8},{1,9},{2,10},{3,11},{4,12},{5,13},{6,14},{7,15},{8,0},{9,1},... | collective-permute-start | bytes 786440 | tf_op jit(solution)/shard_map/ppermute | solution.py:39
  21.0 0.0 collective-permute-done.7.a
  21.0 0.9 %collective-permute-start.3 = (f32[512,128]{1,0:T(8,128)S(1)}, f32[512,128]{1,0:T(8,128)}, u32[]{:S(2)}, u32[]{:S(2)}) collective-permute-start(f32[512,128]{1,0:T(8,128)S(1)} %group.1.g0), channel_id=1, source_target_pairs={{0,12},{1,13},{2,14},{3,15},{4,8},{5,9},{6,10},{7,11},{8,4},{9,5},... | collective-permute-start | bytes 786440 | tf_op jit(solution)/shard_map/ppermute | solution.py:39
  21.9 0.5 collective-permute-done.8.b
  22.4 0.8 %collective-permute-start.2 = (f32[512,128]{1,0:T(8,128)S(1)}, f32[512,128]{1,0:T(8,128)}, u32[]{:S(2)}, u32[]{:S(2)}) collective-permute-start(f32[512,128]{1,0:T(8,128)S(1)} %group.1.g0), channel_id=1, source_target_pairs={{0,4},{1,5},{2,6},{3,7},{4,0},{5,1},{6,2},{7,3},{8,12},{9,13},{10,... | collective-permute-start | bytes 786440 | tf_op jit(solution)/shard_map/ppermute | solution.py:39
  23.2 0.0 collective-permute-done.9.c
  23.2 1.1 %collective-permute-done.10.d = f32[384,128]{1,0:T(8,128)S(1)} collective-permute-done((f32[384,128]{1,0:T(8,128)S(1)}, f32[384,128]{1,0:T(8,128)S(1)}, u32[]{:S(2)}, u32[]{:S(2)}) %collective-permute-start.10) | collective-permute-done | bytes 196640 | tf_op jit(solution)/shard_map/ppermute | solution.py:39
  24.3 0.7 %add.3.acc = f32[384,128]{1,0:T(8,128)} custom-call(f32[384,128]{1,0:T(8,128)S(1)} %collective-permute-done.7.a, f32[384,128]{1,0:T(8,128)S(1)} %collective-permute-done.8.b, f32[384,128]{1,0:T(8,128)S(1)} %collective-permute-done.9.c, f32[384,128]{1,0:T(8,128)S(1)} %collective-permute-done.10.d, f32[384,128]{1,0:T(8,128)S(1)} %get-tuple-element.25.own), custom_call_target="tpu_custom_call" | custom-call | tf_op jit(solution)/shard_map/add/pallas_call | solution.py:181
  25.0 0.3 collective-permute-start.11
  25.3 0.1 copy.8
  25.4 0.1 reshape.16
  25.5 0.1 copy.9
  25.6 0.1 reshape.17
  25.7 0.6 pad_add_fusion.table_hbm
  26.3 0.1 collective-permute-done.4.g2
  26.3 5.2 %collective-permute-done.3.g3 = f32[512,128]{1,0:T(8,128)} collective-permute-done((f32[512,128]{1,0:T(8,128)S(1)}, f32[512,128]{1,0:T(8,128)}, u32[]{:S(2)}, u32[]{:S(2)}) %collective-permute-start.3) | collective-permute-done | bytes 262176 | tf_op jit(solution)/shard_map/ppermute | solution.py:39
  31.5 0.0 collective-permute-done.2.g1
  31.5 2.1 %pick.1 = (f32[128,128]{1,0:T(8,128)S(1)}, f32[128,128]{1,0:T(8,128)S(1)}, f32[128,128]{1,0:T(8,128)S(1)}) custom-call(s32[128]{0:T(128)} %pad_add_fusion.table_hbm, f32[512,128]{1,0:T(8,128)S(1)} %group.1.g0, f32[512,128]{1,0:T(8,128)} %collective-permute-done.2.g1, f32[512,128]{1,0:T(8,128)} %collective-permute-done.3.g3, f32[512,128]{1,0:T(8,128)} %collective-permute-done.4.g2), custom_call_target="tpu_custom_call" | custom-call | tf_op jit(solution)/shard_map/pick/pallas_call | solution.py:239
  33.7 0.5 collective-permute-start.12
  34.1 0.9 %collective-permute-done.12.sib_half = f32[128,128]{1,0:T(8,128)S(1)} collective-permute-done((f32[128,128]{1,0:T(8,128)S(1)}, f32[128,128]{1,0:T(8,128)S(1)}, u32[]{:S(2)}, u32[]{:S(2)}) %collective-permute-start.12) | collective-permute-done | bytes 65568 | tf_op jit(solution)/shard_map/ppermute | solution.py:39
  35.0 0.0 collective-permute-done.11.sib
  35.0 1.1 %reduce.1.own = f32[512,128]{1,0:T(8,128)S(1)} custom-call(f32[384,128]{1,0:T(8,128)} %add.3.acc, f32[384,128]{1,0:T(8,128)} %collective-permute-done.11.sib, f32[128,128]{1,0:T(8,128)S(1)} %get-tuple-element.26.half, f32[128,128]{1,0:T(8,128)S(1)} %collective-permute-done.12.sib_half), custom_call_target="tpu_custom_call" | custom-call | tf_op jit(solution)/shard_map/reduce/pallas_call | solution.py:181
  36.1 9.3 %collective-permute-start.16 = (f32[512,128]{1,0:T(8,128)S(1)}, f32[512,128]{1,0:T(8,128)S(1)}, u32[]{:S(2)}, u32[]{:S(2)}) collective-permute-start(f32[512,128]{1,0:T(8,128)S(1)} %reduce.1.own), channel_id=1, source_target_pairs={{0,96},{1,113},{2,98},{3,115},{4,100},{5,117},{6,102},{7,119},{8,1... | collective-permute-start | bytes 786440 | tf_op jit(solution)/shard_map/ppermute | solution.py:39
  45.4 0.0 collective-permute-start.15
  45.4 0.4 collective-permute-start.14
  45.8 3.2 %collective-permute-start.13 = (f32[512,128]{1,0:T(8,128)S(1)}, f32[512,128]{1,0:T(8,128)S(1)}, u32[]{:S(2)}, u32[]{:S(2)}) collective-permute-start(f32[512,128]{1,0:T(8,128)S(1)} %reduce.1.own), channel_id=1, source_target_pairs={{1,33},{3,35},{5,37},{7,39},{9,41},{11,43},{13,45},{15,47},{17,49}... | collective-permute-start | bytes 786440 | tf_op jit(solution)/shard_map/ppermute | solution.py:39
  49.0 1.7 %collective-permute-start.5 = (f32[128,128]{1,0:T(8,128)S(1)}, f32[128,128]{1,0:T(8,128)S(1)}, u32[]{:S(2)}, u32[]{:S(2)}) collective-permute-start(f32[128,128]{1,0:T(8,128)S(1)} %get-tuple-element.19), channel_id=1, source_target_pairs={{0,2},{1,3},{2,0},{3,1},{4,6},{5,7},{6,4},{7,5},{8,10},{9,11},{10,... | collective-permute-start | bytes 196616 | tf_op jit(solution)/shard_map/ppermute | solution.py:39
  50.7 9.4 %collective-permute-done.5.back = f32[128,128]{1,0:T(8,128)S(1)} collective-permute-done((f32[128,128]{1,0:T(8,128)S(1)}, f32[128,128]{1,0:T(8,128)S(1)}, u32[]{:S(2)}, u32[]{:S(2)}) %collective-permute-start.5) | collective-permute-done | bytes 65568 | tf_op jit(solution)/shard_map/ppermute | solution.py:39
  60.1 0.0 collective-permute-done.16.a
  60.1 0.0 collective-permute-done.15.b
  60.1 0.0 collective-permute-done.14.c
  60.1 0.0 collective-permute-done.13.d
  60.2 0.1 collective-permute-start.17
  60.3 1.9 %collective-permute-done.17.got = f32[960,128]{1,0:T(8,128)S(1)} collective-permute-done((f32[960,128]{1,0:T(8,128)S(1)}, f32[960,128]{1,0:T(8,128)S(1)}, u32[]{:S(2)}, u32[]{:S(2)}) %collective-permute-start.17) | collective-permute-done | bytes 491552 | tf_op jit(solution)/shard_map/ppermute | solution.py:39
  62.1 5.4 %advance.1 = f32[4,12,128,128]{3,2,1,0:T(8,128)} custom-call(f32[4,12,128,128]{3,2,1,0:T(8,128)S(1)} %bitcast.4, f32[128,128]{1,0:T(8,128)S(1)} %get-tuple-element.18.stay, f32[128,128]{1,0:T(8,128)S(1)} %collective-permute-done.5.back, f32[512,128]{1,0:T(8,128)S(1)} %reduce.1.own, f32[512,128]{1,0:T(8,128)S(1)} %collective-permute-done.13.d, ...), custom_call_target="tpu_custom_call" | custom-call | flops 40000000 | bytes 8000000 | tf_op jit(solution)/shard_map/advance/pallas_call | solution.py:375
  (8 shorter events, 0.1 us)
Async XLA Ops:
  0.0 25.3 %copy-start.1 = (s32[16,4]{0,1:T(4,128)S(1)}, s32[16,4]{0,1:T(4,128)}, u32[]{:S(2)}) copy-start(s32[16,4]{0,1:T(4,128)} %param.8) | copy-start | bytes 772
  0.0 25.5 %copy-start.2 = (s32[16,4]{0,1:T(4,128)S(1)}, s32[16,4]{0,1:T(4,128)}, u32[]{:S(2)}) copy-start(s32[16,4]{0,1:T(4,128)} %param.9) | copy-start | bytes 772
  3.3 3.2 %collective-permute-start.6 = (f32[768,128]{1,0:T(8,128)S(1)}, f32[768,128]{1,0:T(8,128)S(1)}, u32[]{:S(2)}, u32[]{:S(2)}) collective-permute-start(f32[768,128]{1,0:T(8,128)S(1)} %get-tuple-element.21), channel_id=1, source_target_pairs={{0,1},{1,0},{2,3},{3,2},{4,5},{5,4},{6,7},{7,6},{8,9},{9,8},{10,11... | collective-permute-start | bytes 1179656 | tf_op jit(solution)/shard_map/ppermute | solution.py:39
  4.8 7.6 %collective-permute-start = (f32[256,128]{1,0:T(8,128)S(1)}, f32[256,128]{1,0:T(8,128)S(1)}, u32[]{:S(2)}, u32[]{:S(2)}) collective-permute-start(f32[256,128]{1,0:T(8,128)S(1)} %get-tuple-element.17), channel_id=1, source_target_pairs={{0,2},{1,3},{2,0},{3,1},{4,6},{5,7},{6,4},{7,5},{8,10},{9,11},{10,... | collective-permute-start | bytes 393224 | tf_op jit(solution)/shard_map/ppermute | solution.py:39
  6.6 55.6 %copy-start = (f32[4,3,4,128,128]{4,3,2,1,0:T(8,128)S(1)}, f32[4,3,4,128,128]{4,3,2,1,0:T(8,128)}, u32[]{:S(2)}) copy-start(f32[4,3,4,128,128]{4,3,2,1,0:T(8,128)} %param.5) | copy-start | bytes 9437188
  6.6 14.4 %collective-permute-start.7 = (f32[384,128]{1,0:T(8,128)S(1)}, f32[384,128]{1,0:T(8,128)S(1)}, u32[]{:S(2)}, u32[]{:S(2)}) collective-permute-start(f32[384,128]{1,0:T(8,128)S(1)} %get-tuple-element.22), channel_id=1, source_target_pairs={{0,96},{1,113},{2,98},{3,115},{4,100},{5,117},{6,102},{7,119},{8,1... | collective-permute-start | bytes 589832 | tf_op jit(solution)/shard_map/ppermute | solution.py:39
  12.4 10.0 %collective-permute-start.8 = (f32[384,128]{1,0:T(8,128)S(1)}, f32[384,128]{1,0:T(8,128)S(1)}, u32[]{:S(2)}, u32[]{:S(2)}) collective-permute-start(f32[384,128]{1,0:T(8,128)S(1)} %get-tuple-element.23), channel_id=1, source_target_pairs={{0,80},{1,65},{2,82},{3,67},{4,84},{5,69},{6,86},{7,71},{8,88},{9,... | collective-permute-start | bytes 589832 | tf_op jit(solution)/shard_map/ppermute | solution.py:39
  12.4 5.7 %collective-permute-start.1 = (f32[256,128]{1,0:T(8,128)S(1)}, f32[256,128]{1,0:T(8,128)S(1)}, u32[]{:S(2)}, u32[]{:S(2)}) collective-permute-start(f32[256,128]{1,0:T(8,128)S(1)} %split.1), channel_id=1, source_target_pairs={{0,1},{1,0},{2,3},{3,2},{4,5},{5,4},{6,7},{7,6},{8,9},{9,8},{10,11... | collective-permute-start | bytes 393224 | tf_op jit(solution)/shard_map/ppermute | solution.py:39
  13.4 9.8 %collective-permute-start.9 = (f32[384,128]{1,0:T(8,128)S(1)}, f32[384,128]{1,0:T(8,128)S(1)}, u32[]{:S(2)}, u32[]{:S(2)}) collective-permute-start(f32[384,128]{1,0:T(8,128)S(1)} %get-tuple-element.24), channel_id=1, source_target_pairs={{0,16},{1,49},{2,18},{3,51},{4,20},{5,53},{6,22},{7,55},{8,24},{9,... | collective-permute-start | bytes 589832 | tf_op jit(solution)/shard_map/ppermute | solution.py:39
  14.1 10.2 %collective-permute-start.10 = (f32[384,128]{1,0:T(8,128)S(1)}, f32[384,128]{1,0:T(8,128)S(1)}, u32[]{:S(2)}, u32[]{:S(2)}) collective-permute-start(f32[384,128]{1,0:T(8,128)S(1)} %get-tuple-element.25.own), channel_id=1, source_target_pairs={{1,33},{3,35},{5,37},{7,39},{9,41},{11,43},{13,45},{15,47},{17,49}... | collective-permute-start | bytes 589832 | tf_op jit(solution)/shard_map/ppermute | solution.py:39
  18.2 8.1 %collective-permute-start.4 = (f32[512,128]{1,0:T(8,128)S(1)}, f32[512,128]{1,0:T(8,128)}, u32[]{:S(2)}, u32[]{:S(2)}) collective-permute-start(f32[512,128]{1,0:T(8,128)S(1)} %group.1.g0), channel_id=1, source_target_pairs={{0,8},{1,9},{2,10},{3,11},{4,12},{5,13},{6,14},{7,15},{8,0},{9,1},... | collective-permute-start | bytes 786440 | tf_op jit(solution)/shard_map/ppermute | solution.py:39
  21.0 10.5 %collective-permute-start.3 = (f32[512,128]{1,0:T(8,128)S(1)}, f32[512,128]{1,0:T(8,128)}, u32[]{:S(2)}, u32[]{:S(2)}) collective-permute-start(f32[512,128]{1,0:T(8,128)S(1)} %group.1.g0), channel_id=1, source_target_pairs={{0,12},{1,13},{2,14},{3,15},{4,8},{5,9},{6,10},{7,11},{8,4},{9,5},... | collective-permute-start | bytes 786440 | tf_op jit(solution)/shard_map/ppermute | solution.py:39
  22.4 9.1 %collective-permute-start.2 = (f32[512,128]{1,0:T(8,128)S(1)}, f32[512,128]{1,0:T(8,128)}, u32[]{:S(2)}, u32[]{:S(2)}) collective-permute-start(f32[512,128]{1,0:T(8,128)S(1)} %group.1.g0), channel_id=1, source_target_pairs={{0,4},{1,5},{2,6},{3,7},{4,0},{5,1},{6,2},{7,3},{8,12},{9,13},{10,... | collective-permute-start | bytes 786440 | tf_op jit(solution)/shard_map/ppermute | solution.py:39
  25.0 10.0 %collective-permute-start.11 = (f32[384,128]{1,0:T(8,128)}, f32[384,128]{1,0:T(8,128)}, u32[]{:S(2)}, u32[]{:S(2)}) collective-permute-start(f32[384,128]{1,0:T(8,128)} %add.3.acc), channel_id=1, source_target_pairs={{0,1},{1,0},{2,3},{3,2},{4,5},{5,4},{6,7},{7,6},{8,9},{9,8},{10,11... | collective-permute-start | bytes 589832 | tf_op jit(solution)/shard_map/ppermute | solution.py:39
  33.7 1.4 %collective-permute-start.12 = (f32[128,128]{1,0:T(8,128)S(1)}, f32[128,128]{1,0:T(8,128)S(1)}, u32[]{:S(2)}, u32[]{:S(2)}) collective-permute-start(f32[128,128]{1,0:T(8,128)S(1)} %get-tuple-element.26.half), channel_id=1, source_target_pairs={{0,1},{1,0},{2,3},{3,2},{4,5},{5,4},{6,7},{7,6},{8,9},{9,8},{10,11... | collective-permute-start | bytes 196616 | tf_op jit(solution)/shard_map/ppermute | solution.py:39
  36.1 24.0 %collective-permute-start.16 = (f32[512,128]{1,0:T(8,128)S(1)}, f32[512,128]{1,0:T(8,128)S(1)}, u32[]{:S(2)}, u32[]{:S(2)}) collective-permute-start(f32[512,128]{1,0:T(8,128)S(1)} %reduce.1.own), channel_id=1, source_target_pairs={{0,96},{1,113},{2,98},{3,115},{4,100},{5,117},{6,102},{7,119},{8,1... | collective-permute-start | bytes 786440 | tf_op jit(solution)/shard_map/ppermute | solution.py:39
  45.4 14.7 %collective-permute-start.15 = (f32[512,128]{1,0:T(8,128)S(1)}, f32[512,128]{1,0:T(8,128)S(1)}, u32[]{:S(2)}, u32[]{:S(2)}) collective-permute-start(f32[512,128]{1,0:T(8,128)S(1)} %reduce.1.own), channel_id=1, source_target_pairs={{0,80},{1,65},{2,82},{3,67},{4,84},{5,69},{6,86},{7,71},{8,88},{9,... | collective-permute-start | bytes 786440 | tf_op jit(solution)/shard_map/ppermute | solution.py:39
  45.4 14.7 %collective-permute-start.14 = (f32[512,128]{1,0:T(8,128)S(1)}, f32[512,128]{1,0:T(8,128)S(1)}, u32[]{:S(2)}, u32[]{:S(2)}) collective-permute-start(f32[512,128]{1,0:T(8,128)S(1)} %reduce.1.own), channel_id=1, source_target_pairs={{0,16},{1,49},{2,18},{3,51},{4,20},{5,53},{6,22},{7,55},{8,24},{9,... | collective-permute-start | bytes 786440 | tf_op jit(solution)/shard_map/ppermute | solution.py:39
  45.8 14.3 %collective-permute-start.13 = (f32[512,128]{1,0:T(8,128)S(1)}, f32[512,128]{1,0:T(8,128)S(1)}, u32[]{:S(2)}, u32[]{:S(2)}) collective-permute-start(f32[512,128]{1,0:T(8,128)S(1)} %reduce.1.own), channel_id=1, source_target_pairs={{1,33},{3,35},{5,37},{7,39},{9,41},{11,43},{13,45},{15,47},{17,49}... | collective-permute-start | bytes 786440 | tf_op jit(solution)/shard_map/ppermute | solution.py:39
  49.0 11.1 %collective-permute-start.5 = (f32[128,128]{1,0:T(8,128)S(1)}, f32[128,128]{1,0:T(8,128)S(1)}, u32[]{:S(2)}, u32[]{:S(2)}) collective-permute-start(f32[128,128]{1,0:T(8,128)S(1)} %get-tuple-element.19), channel_id=1, source_target_pairs={{0,2},{1,3},{2,0},{3,1},{4,6},{5,7},{6,4},{7,5},{8,10},{9,11},{10,... | collective-permute-start | bytes 196616 | tf_op jit(solution)/shard_map/ppermute | solution.py:39
  60.2 1.9 %collective-permute-start.17 = (f32[960,128]{1,0:T(8,128)S(1)}, f32[960,128]{1,0:T(8,128)S(1)}, u32[]{:S(2)}, u32[]{:S(2)}) collective-permute-start(f32[960,128]{1,0:T(8,128)S(1)} %share.1), channel_id=1, source_target_pairs={{0,1},{1,0},{2,3},{3,2},{4,5},{5,4},{6,7},{7,6},{8,9},{9,8},{10,11... | collective-permute-start | bytes 1474568 | tf_op jit(solution)/shard_map/ppermute | solution.py:39

commit v3 on v2

--- a/solution.py
+++ b/solution.py
@@ -15,13 +15,13 @@
 MEMBERS = 32
 ROWS = PLANES * SIZE
 CHUNK = ROWS // N_MEMBER
-OFFSETS = ((6, 5, 1, 0), (7, 4, 3, 2))
+HALF = ROWS // 2
 TAKEN = 20
 SLOT = 32
 RECORD = 4 * SLOT
 USED = 16
 STRIP = 4 * USED
-MAIN = 4 * CHUNK
+STEPS = (2, 1, 3)
 F32 = jnp.float32
 
 
@@ -43,17 +43,12 @@
     return send(array, lambda m, d: (m, d ^ 1))
 
 
-def exchange(messages, order=(0, 1, 2, 3)):
-    out = [None] * 4
-    for j in order:
-        message = messages[j]
-
-        def target(m, d, j=j):
-            offset = OFFSETS[d % 2][j]
-            return (m ^ offset, d) if offset else None
-
-        out[j] = send(message, target)
-    return out
+def over_y(arrays):
+    return [send(array, lambda m, d, k=k: (m ^ k, d)) for k, array in zip(STEPS, arrays)]
+
+
+def over_z_hi(array):
+    return send(array, lambda m, d: (m ^ 4, d))
 
 
 def over_x(array):
@@ -69,7 +64,7 @@
 
 
 def shaped(*rows):
-    return [jax.ShapeDtypeStruct((r, SIZE), F32) for r in rows]
+    return [pltpu.VMEM((r, SIZE), F32) for r in rows]
 
 
 def on(space, *arrays):
@@ -84,16 +79,9 @@
     return lax.axis_index("member"), lax.axis_index("domain")
 
 
-def slot_chunk(member, core, j):
-    zero, one = OFFSETS[0][j % 4], OFFSETS[1][j % 4]
-    if j >= 4:
-        zero, one = one, zero
-    return member ^ jnp.where(core == 0, zero, one)
-
-
 def prepare_kernel(owner_hbm, ens_hbm, ctl_hbm, keep, give, stay, leave, ens, ctl, part, tile, turned, lines, edge, owner, sems, osem):
     member, patch = here()
-    core, z = patch % 2, (patch // 2) % 2
+    z = (patch // 2) % 2
     table = pltpu.make_async_copy(owner_hbm, owner, osem)
     table.start()
     copies = []
@@ -145,17 +133,15 @@
                 out[at : at + TAKEN, :] = lines[2 * c + who, side, 0:TAKEN, :]
                 out[at + 20 : at + 30, :] = edge[side, 10 * c : 10 * c + 10, :]
                 out[at + 30 : at + 32, :] = jnp.zeros((2, SIZE), F32)
-    for j in range(4):
-        own = pl.multiple_of(slot_chunk(member, core, j) * CHUNK, 8)
-        other = pl.multiple_of(slot_chunk(member, core, j + 4) * CHUNK, 8)
-        keep[j * CHUNK : (j + 1) * CHUNK, :] = part[pl.ds(own, CHUNK), :]
-        give[j * CHUNK : (j + 1) * CHUNK, :] = part[pl.ds(other, CHUNK), :]
+    mine = member // 4
+    keep[...] = part[pl.ds(pl.multiple_of(mine * HALF, 8), HALF), :]
+    give[...] = part[pl.ds(pl.multiple_of((1 - mine) * HALF, 8), HALF), :]
 
 
 def prepare(owner, ensemble, control):
     return pl.pallas_call(
         prepare_kernel,
-        out_shape=shaped(MAIN, MAIN, 2 * RECORD, 2 * RECORD),
+        out_shape=shaped(HALF, HALF, 2 * RECORD, 2 * RECORD),
         in_specs=[hbm()] * 3,
         out_specs=[vmem()] * 4,
         scratch_shapes=[
@@ -188,10 +174,11 @@
     )(*on(pltpu.VMEM, *arrays))
 
 
-def pack_kernel(keep, got, m0, m1, m2, m3):
-    for j, m in enumerate((m0, m1, m2, m3)):
-        m[0:CHUNK, :] = keep[j * CHUNK : (j + 1) * CHUNK, :]
-        m[CHUNK:, :] = got[j * CHUNK : (j + 1) * CHUNK, :]
+def halve_kernel(keep, came, own, *outs):
+    member, _ = here()
+    for step, out in zip((0,) + STEPS, (own,) + outs):
+        rows = pl.ds(pl.multiple_of((member % 4 ^ step) * CHUNK, 8), CHUNK)
+        out[...] = keep[rows, :] + came[rows, :]
 
 
 def split_kernel(stay, came, out):
@@ -210,13 +197,13 @@
     out[3 * RECORD :, :] = got[RECORD:, :]
 
 
-def pick_kernel(table_hbm, g0, g1, g3, g2, stay, leave, half, table, sem):
+def pick_kernel(table_hbm, g0, g1, g3, g2, stay, stay_sib, leave, half, half_sib, table, sem):
     _, patch = here()
     copy = pltpu.make_async_copy(table_hbm, table, sem)
     copy.start()
     copy.wait()
     for q in range(4):
-        to, base, rows = (stay, leave)[q // 2], (q % 2) * STRIP, SLOT if q < 2 else 24
+        to, base, rows = ((stay, 0, SLOT), (stay_sib, 0, SLOT), (leave, 0, 24), (leave, STRIP, 24))[q]
         for side in range(4):
             spot = (patch ^ q) * 4 + side
             away = table[spot] ^ patch
@@ -231,56 +218,48 @@
             to[at : at + PLANES, :] = value[0:PLANES]
             to[at + PLANES : at + USED, :] = value[depth : depth + LEV]
             if q < 2:
-                half[at : at + 10, :] = value[20:30]
-                half[at + 10 : at + USED, :] = jnp.zeros((6, SIZE), F32)
+                to_half = (half, half_sib)[q]
+                to_half[at : at + 10, :] = value[20:30]
+                to_half[at + 10 : at + USED, :] = jnp.zeros((6, SIZE), F32)
 
 
 def pick(table, g0, g1, g2, g3):
     return pl.pallas_call(
         pick_kernel,
-        out_shape=shaped(*[2 * STRIP] * 3),
+        out_shape=shaped(STRIP, STRIP, 2 * STRIP, STRIP, STRIP),
         in_specs=[hbm()] + [vmem()] * 4,
-        out_specs=[vmem()] * 3,
+        out_specs=[vmem()] * 5,
         scratch_shapes=[pltpu.SMEM((128,), jnp.int32), pltpu.SemaphoreType.DMA],
         compiler_params=limit(4),
         name="pick",
     )(*on(pltpu.HBM, table), *on(pltpu.VMEM, g0, g1, g3, g2))
 
 
-def add_kernel(a, b, c, d, own, out):
-    _, patch = here()
-    out[...] = (a[...] + b[...]) + (c[...] + jnp.where(patch % 2 == 0, own[...], d[...]))
-
-
-def reduce_kernel(acc, sib, half, sib_half, out):
+def add_kernel(a, b, c, own, half, came, out):
     _, patch = here()
     first = patch % 2 == 0
-    out[0:CHUNK, :] = acc[0:CHUNK, :] + sib[CHUNK : 2 * CHUNK, :]
-    out[CHUNK : 2 * CHUNK, :] = acc[CHUNK : 2 * CHUNK, :] + sib[0:CHUNK, :]
-    for q in (0, 1):
-        for side in range(4):
-            at = q * STRIP + side * USED
-            mine = half[at : at + USED, :]
-            at = (1 - q) * STRIP + side * USED
-            other = sib_half[at : at + USED, :]
-            low, high = jnp.where(first, mine, other), jnp.where(first, other, mine)
-            at, depth = 2 * CHUNK + q * STRIP + side * USED, 6 if side < 2 else 2
-            out[at : at + 10, :] = low[0:10]
-            out[at + 10 : at + 12, :] = high[0:2]
-            out[at + 12 : at + 16, :] = high[depth : depth + LEV]
-
-
-def share_kernel(own, d, c, b, a, stay, back, out):
-    _, patch = here()
-    first = patch % 2 == 0
-    rows = slice(CHUNK, 2 * CHUNK)
-    for j, m in enumerate((a, b, c)):
-        out[j * CHUNK : (j + 1) * CHUNK, :] = m[rows, :]
-    out[3 * CHUNK : 4 * CHUNK, :] = jnp.where(first, own[rows, :], d[rows, :])
-    rows = slice(2 * CHUNK + STRIP, 2 * CHUNK + 2 * STRIP)
-    out[MAIN : MAIN + STRIP, :] = (a[rows, :] + b[rows, :]) + (c[rows, :] + jnp.where(first, own[rows, :], d[rows, :]))
-    out[MAIN + STRIP : MAIN + 2 * STRIP, :] = stay[STRIP:, :]
-    out[MAIN + 2 * STRIP :, :] = back[STRIP:, :]
+    out[0:CHUNK, :] = (a[...] + b[...]) + (c[...] + own[...])
+    for side in range(4):
+        at = side * USED
+        mine, other = half[at : at + USED, :], came[at : at + USED, :]
+        low, high = jnp.where(first, mine, other), jnp.where(first, other, mine)
+        at, depth = CHUNK + side * USED, 6 if side < 2 else 2
+        out[at : at + 10, :] = low[0:10]
+        out[at + 10 : at + 12, :] = high[0:2]
+        out[at + 12 : at + 16, :] = high[depth : depth + LEV]
+
+
+def gather_kernel(own, c, b, a, out):
+    member, _ = here()
+    for step, m in zip((0,) + STEPS, (own, a, b, c)):
+        out[pl.ds(pl.multiple_of((member % 4 ^ step) * CHUNK, 8), CHUNK), :] = m[0:CHUNK, :]
+    rows = slice(CHUNK, CHUNK + STRIP)
+    out[HALF:, :] = (a[rows, :] + b[rows, :]) + (c[rows, :] + own[rows, :])
+
+
+def couple_kernel(stay, back, out):
+    out[0:STRIP, :] = stay[...]
+    out[STRIP:, :] = back[STRIP:, :]
 
 
 def slope(x):
@@ -290,31 +269,27 @@
     return ahead - behind
 
 
-def advance_kernel(ens, stay, back, own, d, c, b, a, got, out, shift, rims, lines, columns, pad, div, slope_u):
+def advance_kernel(ens_hbm, stay, back, got, own, other, out, ens, sems, shift, rims, lines, columns, pad, div, slope_u):
     step = pl.program_id(0)
 
     @pl.when(step == 0)
     def _():
+        for n in range(LOCAL):
+            pltpu.make_async_copy(ens_hbm.at[n], ens.at[n], sems.at[n]).start()
         member, patch = here()
         core, z = patch % 2, (patch // 2) % 2
-        first = core == 0
-        for j, m in enumerate((a, b, c, d)):
-            value = m[0:CHUNK, :]
-            if j == 3:
-                value = jnp.where(first, own[0:CHUNK, :], value)
-            shift[pl.ds(pl.multiple_of(slot_chunk(member, core, j) * CHUNK, 8), CHUNK), :] = value
-            at = pl.multiple_of(slot_chunk(member, core, j + 4) * CHUNK, 8)
-            shift[pl.ds(at, CHUNK), :] = got[j * CHUNK : (j + 1) * CHUNK, :]
+        mine = member // 4
+        shift[pl.ds(pl.multiple_of(mine * HALF, 8), HALF), :] = own[0:HALF, :]
+        shift[pl.ds(pl.multiple_of((1 - mine) * HALF, 8), HALF), :] = other[0:HALF, :]
         for side in range(4):
-            rows = slice(2 * CHUNK + side * USED, 2 * CHUNK + (side + 1) * USED)
-            moved = (a[rows, :] + b[rows, :]) + (c[rows, :] + jnp.where(first, own[rows, :], d[rows, :]))
-            moved = moved + got[MAIN + side * USED : MAIN + (side + 1) * USED, :]
+            rows = slice(HALF + side * USED, HALF + (side + 1) * USED)
+            moved = own[rows, :] + other[rows, :]
             rows = slice(side * USED, (side + 1) * USED)
             for source, who in (
                 (stay[rows, :], 2 * core + z),
                 (back[rows, :], 2 * core + 1 - z),
-                (got[MAIN + STRIP + side * USED : MAIN + STRIP + (side + 1) * USED, :], 2 - 2 * core + z),
-                (got[MAIN + 2 * STRIP + side * USED : MAIN + 2 * STRIP + (side + 1) * USED, :], 3 - 2 * core - z),
+                (got[rows, :], 2 - 2 * core + z),
+                (got[STRIP + side * USED : STRIP + (side + 1) * USED, :], 3 - 2 * core - z),
             ):
                 rims[who, side] = source + moved
         for n in range(LOCAL):
@@ -329,6 +304,7 @@
         for n in range(LOCAL):
             columns[n] = turned if n == 0 else pltpu.roll(turned, SIZE - 32 * n, 1)
 
+    pltpu.make_async_copy(ens_hbm.at[step], ens.at[step], sems.at[step]).wait()
     part = 32
     lane = lax.broadcasted_iota(jnp.int32, (part, SIZE), 1)
     at_left, at_right = lane == 0, lane == SIZE - 1
@@ -371,14 +347,16 @@
             out[0, 2 * LEV + lev, r : r + part, :] = new_w
 
 
-def advance(ensemble, stay, back, received, own, got):
+def advance(ensemble, *arrays):
     return pl.pallas_call(
         advance_kernel,
         out_shape=jax.ShapeDtypeStruct((LOCAL, PLANES, SIZE, SIZE), F32),
         grid=(LOCAL,),
-        in_specs=[vmem()] * 9,
+        in_specs=[hbm()] + [vmem()] * len(arrays),
         out_specs=pl.BlockSpec((1, PLANES, SIZE, SIZE), lambda n: (n, 0, 0, 0)),
         scratch_shapes=[
+            pltpu.VMEM((LOCAL, PLANES, SIZE, SIZE), F32),
+            pltpu.SemaphoreType.DMA((LOCAL,)),
             pltpu.VMEM((ROWS, SIZE), F32),
             pltpu.VMEM((LOCAL, 4, USED, SIZE), F32),
             pltpu.VMEM((SIZE, SIZE), F32),
@@ -390,7 +368,7 @@
         compiler_params=limit(12),
         cost_estimate=pl.CostEstimate(flops=40_000_000, bytes_accessed=8_000_000, transcendentals=0),
         name="advance",
-    )(*on(pltpu.VMEM, ensemble, stay, back, own, *received[::-1], got))
+    )(*on(pltpu.HBM, ensemble), *on(pltpu.VMEM, *arrays))
 
 
 def on_device(ensemble, control, owner, neighbours, codes):
@@ -400,23 +378,20 @@
     table = jnp.concatenate([neighbours.reshape(-1), codes.reshape(-1)])
 
     keep, give, stay, leave = prepare(owner, ensemble, control)
-    came = send(leave, lambda m, d: (m, d ^ 2))
-    got = swap_cores(give)
-    messages = small(pack_kernel, "pack", [2 * CHUNK] * 4, [keep, got])
-    received = exchange(messages)
-    got = swap_cores(small(split_kernel, "split", 2 * RECORD, [stay, came]))
-    group = small(group_kernel, "group", 4 * RECORD, [stay, came, got])
-    acc = small(add_kernel, "add", 2 * CHUNK, received + [messages[3]])
-    stay, leave, half = pick(table, group, *over_x(group))
+    strips = send(leave, lambda m, d: (m, d ^ 2))
+    came = over_z_hi(give)
+    halves = swap_cores(small(split_kernel, "split", 2 * RECORD, [stay, strips]))
+    group = small(group_kernel, "group", 4 * RECORD, [stay, strips, halves])
+    chunk, *chunks = small(halve_kernel, "halve", [CHUNK] * 4, [keep, came])
+    chunks = over_y(chunks)
+    stay, stay_sib, leave, half, half_sib = pick(table, group, *over_x(group))
     back = send(leave, lambda m, d: (m, d ^ 2))
-    reduced = small(
-        reduce_kernel, "reduce", 2 * CHUNK + 2 * STRIP, [acc, swap_cores(acc), half, swap_cores(half)]
-    )
-    received = exchange([reduced] * 4)
-    got = swap_cores(
-        small(share_kernel, "share", MAIN + 3 * STRIP, [reduced, *received[::-1], stay, back])
-    )
-    out = advance(ensemble, stay, back, received, reduced, got)
+    got = swap_cores(small(couple_kernel, "couple", 2 * STRIP, [stay_sib, back]))
+    chunk = small(add_kernel, "add", CHUNK + STRIP, [*chunks, chunk, half, swap_cores(half_sib)])
+    chunks = over_y([chunk] * 3)
+    own = small(gather_kernel, "gather", HALF + STRIP, [chunk, *chunks[::-1]])
+    own, got = lax.optimization_barrier((own, got))
+    out = advance(ensemble, stay, back, got, own, over_z_hi(own))
     return out.reshape(shape)
 
 

time: 67.7 us -> 60 us (0.89)
  the two profiles are of different devices: /device:TPU:1 before, /device:TPU:0 now
where the time goes in v3:
time: 60 us; the launch traced here: 59.6 us
  starting transfers between devices  24.5 us (41%)
  waiting for transfers between devices  23.5 us (39%)
  Pallas kernels  10.6 us (18%)
    ppermute x16, starting transfers between devices, send(): return lax.ppermute(array, MESH, pairs(target))  24.5 us
    ppermute x16, waiting for transfers between devices, send(): return lax.ppermute(array, MESH, pairs(target))  23.5 us
    pallas_call x1, Pallas kernels, advance(): pl.pallas_call(advance_kernel, out_shape=jax.ShapeDtypeStruct((LOCAL, PLA...  6.19 us
    pallas_call x1, Pallas kernels, prepare(): pl.pallas_call(prepare_kernel, out_shape=shaped(HALF, HALF, 2 * RECORD, 2...  3.25 us
  transfers between devices with their start and end apart: 16, of which 9 were waited for; matrix products, arithmetic and copies ran while one was open for 2% of the time, Pallas kernels for 2%

profile of v3, /device:TPU:0, one launch (start us, length us, event | category | flops | bytes accessed | tf_op | source)
XLA Modules:
  0.0 59.6 jit_solution(1827482274180420113)
XLA Ops:
  0.0 0.0 copy-start
  0.0 0.0 copy-start.1
  0.0 3.3 %prepare.1 = (f32[768,128]{1,0:T(8,128)S(1)}, f32[768,128]{1,0:T(8,128)S(1)}, f32[256,128]{1,0:T(8,128)S(1)}, f32[256,128]{1,0:T(8,128)S(1)}) custom-call(s32[16]{0:T(128)} %owner_hbm.1, f32[4,12,128,128]{3,2,1,0:T(8,128)} %bitcast.3, f32[12,128,128]{2,1,0:T(8,128)} %bitcast.5), custom_call_target="tpu_custom_call" | custom-call | flops 2000000 | bytes 5000000 | tf_op jit(solution)/shard_map/prepare/pallas_call | solution.py:142
  3.3 2.1 %collective-permute-start = (f32[256,128]{1,0:T(8,128)S(1)}, f32[256,128]{1,0:T(8,128)S(1)}, u32[]{:S(2)}, u32[]{:S(2)}) collective-permute-start(f32[256,128]{1,0:T(8,128)S(1)} %get-tuple-element.21), channel_id=1, source_target_pairs={{0,2},{1,3},{2,0},{3,1},{4,6},{5,7},{6,4},{7,5},{8,10},{9,11},{10,... | collective-permute-start | bytes 393224 | tf_op jit(solution)/shard_map/ppermute | solution.py:39
  5.3 3.6 %collective-permute-start.6 = (f32[768,128]{1,0:T(8,128)S(1)}, f32[768,128]{1,0:T(8,128)S(1)}, u32[]{:S(2)}, u32[]{:S(2)}) collective-permute-start(f32[768,128]{1,0:T(8,128)S(1)} %get-tuple-element.25), channel_id=1, source_target_pairs={{0,64},{1,65},{2,66},{3,67},{4,68},{5,69},{6,70},{7,71},{8,72},{9,... | collective-permute-start | bytes 1179656 | tf_op jit(solution)/shard_map/ppermute | solution.py:39
  8.9 0.0 collective-permute-done.came
  8.9 0.1 collective-permute-start.1
  9.0 1.3 %collective-permute-done.1.got = f32[256,128]{1,0:T(8,128)S(1)} collective-permute-done((f32[256,128]{1,0:T(8,128)S(1)}, f32[256,128]{1,0:T(8,128)S(1)}, u32[]{:S(2)}, u32[]{:S(2)}) %collective-permute-start.1) | collective-permute-done | bytes 131104 | tf_op jit(solution)/shard_map/ppermute | solution.py:39
  10.4 3.1 %collective-permute-start.4 = (f32[512,128]{1,0:T(8,128)S(1)}, f32[512,128]{1,0:T(8,128)S(1)}, u32[]{:S(2)}, u32[]{:S(2)}) collective-permute-start(f32[512,128]{1,0:T(8,128)S(1)} %group.1.g0), channel_id=1, source_target_pairs={{0,8},{1,9},{2,10},{3,11},{4,12},{5,13},{6,14},{7,15},{8,0},{9,1},... | collective-permute-start | bytes 786440 | tf_op jit(solution)/shard_map/ppermute | solution.py:39
  13.5 1.1 %collective-permute-start.3 = (f32[512,128]{1,0:T(8,128)S(1)}, f32[512,128]{1,0:T(8,128)S(1)}, u32[]{:S(2)}, u32[]{:S(2)}) collective-permute-start(f32[512,128]{1,0:T(8,128)S(1)} %group.1.g0), channel_id=1, source_target_pairs={{0,12},{1,13},{2,14},{3,15},{4,8},{5,9},{6,10},{7,11},{8,4},{9,5},... | collective-permute-start | bytes 786440 | tf_op jit(solution)/shard_map/ppermute | solution.py:39
  14.6 0.0 collective-permute-start.2
  14.6 0.0 copy-done
  14.6 0.1 copy.8
  14.7 0.1 reshape.16
  14.8 0.0 copy-done.1
  14.8 0.1 copy.9
  14.9 0.1 reshape.17
  15.0 5.6 %collective-permute-done.6.came = f32[768,128]{1,0:T(8,128)S(1)} collective-permute-done((f32[768,128]{1,0:T(8,128)S(1)}, f32[768,128]{1,0:T(8,128)S(1)}, u32[]{:S(2)}, u32[]{:S(2)}) %collective-permute-start.6) | collective-permute-done | bytes 393248 | tf_op jit(solution)/shard_map/ppermute | solution.py:39
  20.6 3.3 %collective-permute-start.7 = (f32[192,128]{1,0:T(8,128)S(1)}, f32[192,128]{1,0:T(8,128)S(1)}, u32[]{:S(2)}, u32[]{:S(2)}) collective-permute-start(f32[192,128]{1,0:T(8,128)S(1)} %get-tuple-element.26), channel_id=1, source_target_pairs={{0,32},{1,33},{2,34},{3,35},{4,36},{5,37},{6,38},{7,39},{8,40},{9,... | collective-permute-start | bytes 294920 | tf_op jit(solution)/shard_map/ppermute | solution.py:39
  23.9 0.7 %collective-permute-start.8 = (f32[192,128]{1,0:T(8,128)S(1)}, f32[192,128]{1,0:T(8,128)S(1)}, u32[]{:S(2)}, u32[]{:S(2)}) collective-permute-start(f32[192,128]{1,0:T(8,128)S(1)} %get-tuple-element.27), channel_id=1, source_target_pairs={{0,16},{1,17},{2,18},{3,19},{4,20},{5,21},{6,22},{7,23},{8,24},{9,... | collective-permute-start | bytes 294920 | tf_op jit(solution)/shard_map/ppermute | solution.py:39
  24.6 0.0 collective-permute-done.4.g2
  24.6 0.4 collective-permute-start.9
  24.9 0.6 pad_add_fusion.table_hbm
  25.5 0.4 collective-permute-done.3.g3
  26.0 0.1 collective-permute-done.2.g1
  26.1 1.0 %pick.1 = (f32[64,128]{1,0:T(8,128)S(1)}, f32[64,128]{1,0:T(8,128)S(1)}, f32[128,128]{1,0:T(8,128)S(1)}, f32[64,128]{1,0:T(8,128)S(1)}, f32[64,128]{1,0:T(8,128)S(1)}) custom-call(s32[128]{0:T(128)} %pad_add_fusion.table_hbm, f32[512,128]{1,0:T(8,128)S(1)} %group.1.g0, f32[512,128]{1,0:T(8,128)S(1)} %collective-permute-done.2.g1, ...), custom_call_target="tpu_custom_call" | custom-call | tf_op jit(solution)/shard_map/pick/pallas_call | solution.py:227
  27.1 0.1 collective-permute-start.10
  27.2 1.7 %collective-permute-start.5 = (f32[128,128]{1,0:T(8,128)S(1)}, f32[128,128]{1,0:T(8,128)S(1)}, u32[]{:S(2)}, u32[]{:S(2)}) collective-permute-start(f32[128,128]{1,0:T(8,128)S(1)} %get-tuple-element.23), channel_id=1, source_target_pairs={{0,2},{1,3},{2,0},{3,1},{4,6},{5,7},{6,4},{7,5},{8,10},{9,11},{10,... | collective-permute-start | bytes 196616 | tf_op jit(solution)/shard_map/ppermute | solution.py:39
  28.9 0.0 collective-permute-done.7.a
  28.9 0.0 collective-permute-done.8.b
  28.9 1.5 %collective-permute-done.9.c = f32[192,128]{1,0:T(8,128)S(1)} collective-permute-done((f32[192,128]{1,0:T(8,128)S(1)}, f32[192,128]{1,0:T(8,128)S(1)}, u32[]{:S(2)}, u32[]{:S(2)}) %collective-permute-start.9) | collective-permute-done | bytes 98336 | tf_op jit(solution)/shard_map/ppermute | solution.py:39
  30.4 0.0 collective-permute-done.10.came
  30.4 1.8 %collective-permute-start.13 = (f32[256,128]{1,0:T(8,128)S(1)}, f32[256,128]{1,0:T(8,128)S(1)}, u32[]{:S(2)}, u32[]{:S(2)}) collective-permute-start(f32[256,128]{1,0:T(8,128)S(1)} %add.3.own), channel_id=1, source_target_pairs={{0,32},{1,33},{2,34},{3,35},{4,36},{5,37},{6,38},{7,39},{8,40},{9,... | collective-permute-start | bytes 393224 | tf_op jit(solution)/shard_map/ppermute | solution.py:39
  32.3 0.7 %collective-permute-start.12 = (f32[256,128]{1,0:T(8,128)S(1)}, f32[256,128]{1,0:T(8,128)S(1)}, u32[]{:S(2)}, u32[]{:S(2)}) collective-permute-start(f32[256,128]{1,0:T(8,128)S(1)} %add.3.own), channel_id=1, source_target_pairs={{0,16},{1,17},{2,18},{3,19},{4,20},{5,21},{6,22},{7,23},{8,24},{9,... | collective-permute-start | bytes 393224 | tf_op jit(solution)/shard_map/ppermute | solution.py:39
  32.9 1.7 %collective-permute-start.11 = (f32[256,128]{1,0:T(8,128)S(1)}, f32[256,128]{1,0:T(8,128)S(1)}, u32[]{:S(2)}, u32[]{:S(2)}) collective-permute-start(f32[256,128]{1,0:T(8,128)S(1)} %add.3.own), channel_id=1, source_target_pairs={{0,48},{1,49},{2,50},{3,51},{4,52},{5,53},{6,54},{7,55},{8,56},{9,... | collective-permute-start | bytes 393224 | tf_op jit(solution)/shard_map/ppermute | solution.py:39
  34.6 0.0 collective-permute-done.5.back
  34.6 0.1 collective-permute-start.14
  34.7 3.4 %collective-permute-done.13.a = f32[256,128]{1,0:T(8,128)S(1)} collective-permute-done((f32[256,128]{1,0:T(8,128)S(1)}, f32[256,128]{1,0:T(8,128)S(1)}, u32[]{:S(2)}, u32[]{:S(2)}) %collective-permute-start.13) | collective-permute-done | bytes 131104 | tf_op jit(solution)/shard_map/ppermute | solution.py:39
  38.1 1.1 %collective-permute-done.12.b = f32[256,128]{1,0:T(8,128)S(1)} collective-permute-done((f32[256,128]{1,0:T(8,128)S(1)}, f32[256,128]{1,0:T(8,128)S(1)}, u32[]{:S(2)}, u32[]{:S(2)}) %collective-permute-start.12) | collective-permute-done | bytes 131104 | tf_op jit(solution)/shard_map/ppermute | solution.py:39
  39.3 0.8 %collective-permute-done.11.c = f32[256,128]{1,0:T(8,128)S(1)} collective-permute-done((f32[256,128]{1,0:T(8,128)S(1)}, f32[256,128]{1,0:T(8,128)S(1)}, u32[]{:S(2)}, u32[]{:S(2)}) %collective-permute-start.11) | collective-permute-done | bytes 131104 | tf_op jit(solution)/shard_map/ppermute | solution.py:39
  40.2 0.0 collective-permute-done.14.got
  40.2 4.1 %collective-permute-start.15 = (f32[832,128]{1,0:T(8,128)S(1)}, f32[832,128]{1,0:T(8,128)S(1)}, u32[]{:S(2)}, u32[]{:S(2)}) collective-permute-start(f32[832,128]{1,0:T(8,128)S(1)} %gather.1.own), channel_id=1, source_target_pairs={{0,64},{1,65},{2,66},{3,67},{4,68},{5,69},{6,70},{7,71},{8,72},{9,... | collective-permute-start | bytes 1277960 | tf_op jit(solution)/shard_map/ppermute | solution.py:39
  44.3 9.1 %collective-permute-done.15.other = f32[832,128]{1,0:T(8,128)S(1)} collective-permute-done((f32[832,128]{1,0:T(8,128)S(1)}, f32[832,128]{1,0:T(8,128)S(1)}, u32[]{:S(2)}, u32[]{:S(2)}) %collective-permute-start.15) | collective-permute-done | bytes 426016 | tf_op jit(solution)/shard_map/ppermute | solution.py:39
  53.5 6.2 %advance.1 = f32[4,12,128,128]{3,2,1,0:T(8,128)} custom-call(f32[4,12,128,128]{3,2,1,0:T(8,128)} %bitcast.4, f32[64,128]{1,0:T(8,128)S(1)} %get-tuple-element.22.stay, f32[128,128]{1,0:T(8,128)S(1)} %collective-permute-done.5.back, f32[128,128]{1,0:T(8,128)S(1)} %collective-permute-done.14.got, f32[832,128]{1,0:T(8,128)S(1)} %gather.1.own, ...), custom_call_target="tpu_custom_call" | custom-call | flops 40000000 | bytes 8000000 | tf_op jit(solution)/shard_map/advance/pallas_call | solution.py:351
  (6 shorter events, 0.2 us)
Async XLA Ops:
  0.0 14.6 %copy-start = (s32[16,4]{0,1:T(4,128)S(1)}, s32[16,4]{0,1:T(4,128)}, u32[]{:S(2)}) copy-start(s32[16,4]{0,1:T(4,128)} %param.8) | copy-start | bytes 772
  0.0 14.8 %copy-start.1 = (s32[16,4]{0,1:T(4,128)S(1)}, s32[16,4]{0,1:T(4,128)}, u32[]{:S(2)}) copy-start(s32[16,4]{0,1:T(4,128)} %param.9) | copy-start | bytes 772
  3.3 5.7 %collective-permute-start = (f32[256,128]{1,0:T(8,128)S(1)}, f32[256,128]{1,0:T(8,128)S(1)}, u32[]{:S(2)}, u32[]{:S(2)}) collective-permute-start(f32[256,128]{1,0:T(8,128)S(1)} %get-tuple-element.21), channel_id=1, source_target_pairs={{0,2},{1,3},{2,0},{3,1},{4,6},{5,7},{6,4},{7,5},{8,10},{9,11},{10,... | collective-permute-start | bytes 393224 | tf_op jit(solution)/shard_map/ppermute | solution.py:39
  5.3 15.2 %collective-permute-start.6 = (f32[768,128]{1,0:T(8,128)S(1)}, f32[768,128]{1,0:T(8,128)S(1)}, u32[]{:S(2)}, u32[]{:S(2)}) collective-permute-start(f32[768,128]{1,0:T(8,128)S(1)} %get-tuple-element.25), channel_id=1, source_target_pairs={{0,64},{1,65},{2,66},{3,67},{4,68},{5,69},{6,70},{7,71},{8,72},{9,... | collective-permute-start | bytes 1179656 | tf_op jit(solution)/shard_map/ppermute | solution.py:39
  8.9 1.4 %collective-permute-start.1 = (f32[256,128]{1,0:T(8,128)S(1)}, f32[256,128]{1,0:T(8,128)S(1)}, u32[]{:S(2)}, u32[]{:S(2)}) collective-permute-start(f32[256,128]{1,0:T(8,128)S(1)} %split.1), channel_id=1, source_target_pairs={{0,1},{1,0},{2,3},{3,2},{4,5},{5,4},{6,7},{7,6},{8,9},{9,8},{10,11... | collective-permute-start | bytes 393224 | tf_op jit(solution)/shard_map/ppermute | solution.py:39
  10.4 14.2 %collective-permute-start.4 = (f32[512,128]{1,0:T(8,128)S(1)}, f32[512,128]{1,0:T(8,128)S(1)}, u32[]{:S(2)}, u32[]{:S(2)}) collective-permute-start(f32[512,128]{1,0:T(8,128)S(1)} %group.1.g0), channel_id=1, source_target_pairs={{0,8},{1,9},{2,10},{3,11},{4,12},{5,13},{6,14},{7,15},{8,0},{9,1},... | collective-permute-start | bytes 786440 | tf_op jit(solution)/shard_map/ppermute | solution.py:39
  13.5 12.5 %collective-permute-start.3 = (f32[512,128]{1,0:T(8,128)S(1)}, f32[512,128]{1,0:T(8,128)S(1)}, u32[]{:S(2)}, u32[]{:S(2)}) collective-permute-start(f32[512,128]{1,0:T(8,128)S(1)} %group.1.g0), channel_id=1, source_target_pairs={{0,12},{1,13},{2,14},{3,15},{4,8},{5,9},{6,10},{7,11},{8,4},{9,5},... | collective-permute-start | bytes 786440 | tf_op jit(solution)/shard_map/ppermute | solution.py:39
  14.6 11.4 %collective-permute-start.2 = (f32[512,128]{1,0:T(8,128)S(1)}, f32[512,128]{1,0:T(8,128)S(1)}, u32[]{:S(2)}, u32[]{:S(2)}) collective-permute-start(f32[512,128]{1,0:T(8,128)S(1)} %group.1.g0), channel_id=1, source_target_pairs={{0,4},{1,5},{2,6},{3,7},{4,0},{5,1},{6,2},{7,3},{8,12},{9,13},{10,... | collective-permute-start | bytes 786440 | tf_op jit(solution)/shard_map/ppermute | solution.py:39
  20.6 8.3 %collective-permute-start.7 = (f32[192,128]{1,0:T(8,128)S(1)}, f32[192,128]{1,0:T(8,128)S(1)}, u32[]{:S(2)}, u32[]{:S(2)}) collective-permute-start(f32[192,128]{1,0:T(8,128)S(1)} %get-tuple-element.26), channel_id=1, source_target_pairs={{0,32},{1,33},{2,34},{3,35},{4,36},{5,37},{6,38},{7,39},{8,40},{9,... | collective-permute-start | bytes 294920 | tf_op jit(solution)/shard_map/ppermute | solution.py:39
  23.9 5.0 %collective-permute-start.8 = (f32[192,128]{1,0:T(8,128)S(1)}, f32[192,128]{1,0:T(8,128)S(1)}, u32[]{:S(2)}, u32[]{:S(2)}) collective-permute-start(f32[192,128]{1,0:T(8,128)S(1)} %get-tuple-element.27), channel_id=1, source_target_pairs={{0,16},{1,17},{2,18},{3,19},{4,20},{5,21},{6,22},{7,23},{8,24},{9,... | collective-permute-start | bytes 294920 | tf_op jit(solution)/shard_map/ppermute | solution.py:39
  24.6 5.8 %collective-permute-start.9 = (f32[192,128]{1,0:T(8,128)S(1)}, f32[192,128]{1,0:T(8,128)S(1)}, u32[]{:S(2)}, u32[]{:S(2)}) collective-permute-start(f32[192,128]{1,0:T(8,128)S(1)} %get-tuple-element.28), channel_id=1, source_target_pairs={{0,48},{1,49},{2,50},{3,51},{4,52},{5,53},{6,54},{7,55},{8,56},{9,... | collective-permute-start | bytes 294920 | tf_op jit(solution)/shard_map/ppermute | solution.py:39
  27.1 3.3 %collective-permute-start.10 = (f32[64,128]{1,0:T(8,128)S(1)}, f32[64,128]{1,0:T(8,128)S(1)}, u32[]{:S(2)}, u32[]{:S(2)}) collective-permute-start(f32[64,128]{1,0:T(8,128)S(1)} %get-tuple-element.31), channel_id=1, source_target_pairs={{0,1},{1,0},{2,3},{3,2},{4,5},{5,4},{6,7},{7,6},{8,9},{9,8},{10,11... | collective-permute-start | bytes 98312 | tf_op jit(solution)/shard_map/ppermute | solution.py:39
  27.2 7.4 %collective-permute-start.5 = (f32[128,128]{1,0:T(8,128)S(1)}, f32[128,128]{1,0:T(8,128)S(1)}, u32[]{:S(2)}, u32[]{:S(2)}) collective-permute-start(f32[128,128]{1,0:T(8,128)S(1)} %get-tuple-element.23), channel_id=1, source_target_pairs={{0,2},{1,3},{2,0},{3,1},{4,6},{5,7},{6,4},{7,5},{8,10},{9,11},{10,... | collective-permute-start | bytes 196616 | tf_op jit(solution)/shard_map/ppermute | solution.py:39
  30.4 7.7 %collective-permute-start.13 = (f32[256,128]{1,0:T(8,128)S(1)}, f32[256,128]{1,0:T(8,128)S(1)}, u32[]{:S(2)}, u32[]{:S(2)}) collective-permute-start(f32[256,128]{1,0:T(8,128)S(1)} %add.3.own), channel_id=1, source_target_pairs={{0,32},{1,33},{2,34},{3,35},{4,36},{5,37},{6,38},{7,39},{8,40},{9,... | collective-permute-start | bytes 393224 | tf_op jit(solution)/shard_map/ppermute | solution.py:39
  32.3 7.0 %collective-permute-start.12 = (f32[256,128]{1,0:T(8,128)S(1)}, f32[256,128]{1,0:T(8,128)S(1)}, u32[]{:S(2)}, u32[]{:S(2)}) collective-permute-start(f32[256,128]{1,0:T(8,128)S(1)} %add.3.own), channel_id=1, source_target_pairs={{0,16},{1,17},{2,18},{3,19},{4,20},{5,21},{6,22},{7,23},{8,24},{9,... | collective-permute-start | bytes 393224 | tf_op jit(solution)/shard_map/ppermute | solution.py:39
  32.9 7.2 %collective-permute-start.11 = (f32[256,128]{1,0:T(8,128)S(1)}, f32[256,128]{1,0:T(8,128)S(1)}, u32[]{:S(2)}, u32[]{:S(2)}) collective-permute-start(f32[256,128]{1,0:T(8,128)S(1)} %add.3.own), channel_id=1, source_target_pairs={{0,48},{1,49},{2,50},{3,51},{4,52},{5,53},{6,54},{7,55},{8,56},{9,... | collective-permute-start | bytes 393224 | tf_op jit(solution)/shard_map/ppermute | solution.py:39
  34.6 5.6 %collective-permute-start.14 = (f32[128,128]{1,0:T(8,128)S(1)}, f32[128,128]{1,0:T(8,128)S(1)}, u32[]{:S(2)}, u32[]{:S(2)}) collective-permute-start(f32[128,128]{1,0:T(8,128)S(1)} %couple.1), channel_id=1, source_target_pairs={{0,1},{1,0},{2,3},{3,2},{4,5},{5,4},{6,7},{7,6},{8,9},{9,8},{10,11... | collective-permute-start | bytes 196616 | tf_op jit(solution)/shard_map/ppermute | solution.py:39
  40.2 13.3 %collective-permute-start.15 = (f32[832,128]{1,0:T(8,128)S(1)}, f32[832,128]{1,0:T(8,128)S(1)}, u32[]{:S(2)}, u32[]{:S(2)}) collective-permute-start(f32[832,128]{1,0:T(8,128)S(1)} %gather.1.own), channel_id=1, source_target_pairs={{0,64},{1,65},{2,66},{3,67},{4,68},{5,69},{6,70},{7,71},{8,72},{9,... | collective-permute-start | bytes 1277960 | tf_op jit(solution)/shard_map/ppermute | solution.py:39

commit v4 on v3

--- a/solution.py
+++ b/solution.py
@@ -79,7 +79,7 @@
     return lax.axis_index("member"), lax.axis_index("domain")
 
 
-def prepare_kernel(owner_hbm, ens_hbm, ctl_hbm, keep, give, stay, leave, ens, ctl, part, tile, turned, lines, edge, owner, sems, osem):
+def prepare_kernel(owner_hbm, ens_hbm, ctl_hbm, keep, give0, give1, give2, stay, leave, ens, ctl, part, tile, turned, lines, edge, owner, sems, osem):
     member, patch = here()
     z = (patch // 2) % 2
     table = pltpu.make_async_copy(owner_hbm, owner, osem)
@@ -133,17 +133,18 @@
                 out[at : at + TAKEN, :] = lines[2 * c + who, side, 0:TAKEN, :]
                 out[at + 20 : at + 30, :] = edge[side, 10 * c : 10 * c + 10, :]
                 out[at + 30 : at + 32, :] = jnp.zeros((2, SIZE), F32)
-    mine = member // 4
-    keep[...] = part[pl.ds(pl.multiple_of(mine * HALF, 8), HALF), :]
-    give[...] = part[pl.ds(pl.multiple_of((1 - mine) * HALF, 8), HALF), :]
+    for step, out in zip((0,) + STEPS, (keep, give0, give1, give2)):
+        for half in (0, 1):
+            at = pl.multiple_of(half * HALF + (member % 4 ^ step) * CHUNK, 8)
+            out[half * CHUNK : (half + 1) * CHUNK, :] = part[pl.ds(at, CHUNK), :]
 
 
 def prepare(owner, ensemble, control):
     return pl.pallas_call(
         prepare_kernel,
-        out_shape=shaped(HALF, HALF, 2 * RECORD, 2 * RECORD),
+        out_shape=shaped(*[2 * CHUNK] * 4, 2 * RECORD, 2 * RECORD),
         in_specs=[hbm()] * 3,
-        out_specs=[vmem()] * 4,
+        out_specs=[vmem()] * 6,
         scratch_shapes=[
             pltpu.VMEM((LOCAL, PLANES, SIZE, SIZE), F32),
             pltpu.VMEM((PLANES, SIZE, SIZE), F32),
@@ -174,11 +175,11 @@
     )(*on(pltpu.VMEM, *arrays))
 
 
-def halve_kernel(keep, came, own, *outs):
-    member, _ = here()
-    for step, out in zip((0,) + STEPS, (own,) + outs):
-        rows = pl.ds(pl.multiple_of((member % 4 ^ step) * CHUNK, 8), CHUNK)
-        out[...] = keep[rows, :] + came[rows, :]
+def sum_kernel(*refs):
+    *terms, out = [r[...] for r in refs[:-1]] + [refs[-1]]
+    while len(terms) > 1:
+        terms = [terms[i] + terms[i + 1] if i + 1 < len(terms) else terms[i] for i in range(0, len(terms), 2)]
+    out[...] = terms[0]
 
 
 def split_kernel(stay, came, out):
@@ -235,26 +236,17 @@
     )(*on(pltpu.HBM, table), *on(pltpu.VMEM, g0, g1, g3, g2))
 
 
-def add_kernel(a, b, c, own, half, came, out):
+def merge_kernel(half, came, out):
     _, patch = here()
     first = patch % 2 == 0
-    out[0:CHUNK, :] = (a[...] + b[...]) + (c[...] + own[...])
     for side in range(4):
         at = side * USED
         mine, other = half[at : at + USED, :], came[at : at + USED, :]
         low, high = jnp.where(first, mine, other), jnp.where(first, other, mine)
-        at, depth = CHUNK + side * USED, 6 if side < 2 else 2
+        depth = 6 if side < 2 else 2
         out[at : at + 10, :] = low[0:10]
         out[at + 10 : at + 12, :] = high[0:2]
         out[at + 12 : at + 16, :] = high[depth : depth + LEV]
-
-
-def gather_kernel(own, c, b, a, out):
-    member, _ = here()
-    for step, m in zip((0,) + STEPS, (own, a, b, c)):
-        out[pl.ds(pl.multiple_of((member % 4 ^ step) * CHUNK, 8), CHUNK), :] = m[0:CHUNK, :]
-    rows = slice(CHUNK, CHUNK + STRIP)
-    out[HALF:, :] = (a[rows, :] + b[rows, :]) + (c[rows, :] + own[rows, :])
 
 
 def couple_kernel(stay, back, out):
@@ -269,22 +261,22 @@
     return ahead - behind
 
 
-def advance_kernel(ens_hbm, stay, back, got, own, other, out, ens, sems, shift, rims, lines, columns, pad, div, slope_u):
-    step = pl.program_id(0)
-
-    @pl.when(step == 0)
+def advance_kernel(ens_hbm, stay, back, got, own, c, b, a, edge0, edge1, edge2, edge3, out, ens, sems, shift, rims, lines, columns, pad, div, slope_u):
+    now_at = pl.program_id(0)
+
+    @pl.when(now_at == 0)
     def _():
         for n in range(LOCAL):
             pltpu.make_async_copy(ens_hbm.at[n], ens.at[n], sems.at[n]).start()
         member, patch = here()
         core, z = patch % 2, (patch // 2) % 2
-        mine = member // 4
-        shift[pl.ds(pl.multiple_of(mine * HALF, 8), HALF), :] = own[0:HALF, :]
-        shift[pl.ds(pl.multiple_of((1 - mine) * HALF, 8), HALF), :] = other[0:HALF, :]
+        for step, m in zip((0,) + STEPS, (own, a, b, c)):
+            for half in (0, 1):
+                at = pl.multiple_of(half * HALF + (member % 4 ^ step) * CHUNK, 8)
+                shift[pl.ds(at, CHUNK), :] = m[half * CHUNK : (half + 1) * CHUNK, :]
         for side in range(4):
-            rows = slice(HALF + side * USED, HALF + (side + 1) * USED)
-            moved = own[rows, :] + other[rows, :]
             rows = slice(side * USED, (side + 1) * USED)
+            moved = (edge0[rows, :] + edge1[rows, :]) + (edge2[rows, :] + edge3[rows, :])
             for source, who in (
                 (stay[rows, :], 2 * core + z),
                 (back[rows, :], 2 * core + 1 - z),
@@ -304,6 +296,7 @@
         for n in range(LOCAL):
             columns[n] = turned if n == 0 else pltpu.roll(turned, SIZE - 32 * n, 1)
 
+    step = now_at
     pltpu.make_async_copy(ens_hbm.at[step], ens.at[step], sems.at[step]).wait()
     part = 32
     lane = lax.broadcasted_iota(jnp.int32, (part, SIZE), 1)
@@ -377,21 +370,20 @@
     control = control.reshape(PLANES, SIZE, SIZE)
     table = jnp.concatenate([neighbours.reshape(-1), codes.reshape(-1)])
 
-    keep, give, stay, leave = prepare(owner, ensemble, control)
+    keep, *gives, stay, leave = prepare(owner, ensemble, control)
     strips = send(leave, lambda m, d: (m, d ^ 2))
-    came = over_z_hi(give)
     halves = swap_cores(small(split_kernel, "split", 2 * RECORD, [stay, strips]))
     group = small(group_kernel, "group", 4 * RECORD, [stay, strips, halves])
-    chunk, *chunks = small(halve_kernel, "halve", [CHUNK] * 4, [keep, came])
-    chunks = over_y(chunks)
+    total = small(sum_kernel, "total", 2 * CHUNK, [*over_y(gives), keep])
+    total = small(sum_kernel, "shift", 2 * CHUNK, [total, over_z_hi(total)])
+    chunks = over_y([total] * 3)
     stay, stay_sib, leave, half, half_sib = pick(table, group, *over_x(group))
     back = send(leave, lambda m, d: (m, d ^ 2))
     got = swap_cores(small(couple_kernel, "couple", 2 * STRIP, [stay_sib, back]))
-    chunk = small(add_kernel, "add", CHUNK + STRIP, [*chunks, chunk, half, swap_cores(half_sib)])
-    chunks = over_y([chunk] * 3)
-    own = small(gather_kernel, "gather", HALF + STRIP, [chunk, *chunks[::-1]])
-    own, got = lax.optimization_barrier((own, got))
-    out = advance(ensemble, stay, back, got, own, over_z_hi(own))
+    edge = small(merge_kernel, "merge", STRIP, [half, swap_cores(half_sib)])
+    edge = small(sum_kernel, "edge", STRIP, [edge, over_z_hi(edge)])
+    edges = over_y([edge] * 3)
+    out = advance(ensemble, stay, back, got, total, *chunks[::-1], edge, *edges[::-1])
     return out.reshape(shape)
 
 

time: 60 us -> 54.8 us (0.913)
  waiting for transfers between devices: 23.5 us -> 14 us
  starting transfers between devices: 24.5 us -> 29 us
    ppermute x16 -> x19, waiting for transfers between devices: 23.5 us -> 14 us  [send(): return lax.ppermute(array, MESH, pairs(target))]
    ppermute x16 -> x19, starting transfers between devices: 24.5 us -> 29 us  [send(): return lax.ppermute(array, MESH, pairs(target))]
  transfers between devices with their start and end apart: 16 -> 19, of which waited for: 9 -> 10; matrix products, arithmetic and copies ran while one was open for 2% -> 2% of each run, Pallas kernels for 2% -> 2%
where the time goes in v4:
time: 54.8 us; the launch traced here: 54.7 us
  starting transfers between devices  29 us (53%)
  waiting for transfers between devices  14 us (26%)
  Pallas kernels  10.6 us (19%)
  other arithmetic  0.58 us (1%)
    ppermute x19, starting transfers between devices, send(): return lax.ppermute(array, MESH, pairs(target))  29 us
    ppermute x19, waiting for transfers between devices, send(): return lax.ppermute(array, MESH, pairs(target))  14 us
    pallas_call x1, Pallas kernels, advance(): pl.pallas_call(advance_kernel, out_shape=jax.ShapeDtypeStruct((LOCAL, PLA...  6.21 us
    pallas_call x1, Pallas kernels, prepare(): pl.pallas_call(prepare_kernel, out_shape=shaped(*[2 * CHUNK] * 4, 2 * REC...  3.25 us
  transfers between devices with their start and end apart: 19, of which 10 were waited for; matrix products, arithmetic and copies ran while one was open for 2% of the time, Pallas kernels for 2%

profile of v4, /device:TPU:0, one launch (start us, length us, event | category | flops | bytes accessed | tf_op | source)
XLA Modules:
  0.0 54.7 jit_solution(920571875714597681)
XLA Ops:
  0.0 3.3 %prepare.1 = (f32[384,128]{1,0:T(8,128)S(1)}, f32[384,128]{1,0:T(8,128)S(1)}, f32[384,128]{1,0:T(8,128)S(1)}, f32[384,128]{1,0:T(8,128)S(1)}, f32[256,128]{1,0:T(8,128)S(1)}, /*index=5*/f32[256,128]{1,0:T(8,128)S(1)}) custom-call(s32[16]{0:T(128)} %owner_hbm.1, f32[4,12,128,128]{3,2,1,0:T(8,128)} %bitcast.3, f32[12,128,128]{2,1,0:T(8,128)} %bitcast.5), custom_call_target="tpu_custom_call" | custom-call | flops 2000000 | bytes 5000000 | tf_op jit(solution)/shard_map/prepare/pallas_call | solution.py:143
  3.3 2.1 %collective-permute-start = (f32[256,128]{1,0:T(8,128)S(1)}, f32[256,128]{1,0:T(8,128)S(1)}, u32[]{:S(2)}, u32[]{:S(2)}) collective-permute-start(f32[256,128]{1,0:T(8,128)S(1)} %get-tuple-element.17), channel_id=1, source_target_pairs={{0,2},{1,3},{2,0},{3,1},{4,6},{5,7},{6,4},{7,5},{8,10},{9,11},{10,... | collective-permute-start | bytes 393224 | tf_op jit(solution)/shard_map/ppermute | solution.py:39
  5.3 3.2 %collective-permute-start.7 = (f32[384,128]{1,0:T(8,128)S(1)}, f32[384,128]{1,0:T(8,128)S(1)}, u32[]{:S(2)}, u32[]{:S(2)}) collective-permute-start(f32[384,128]{1,0:T(8,128)S(1)} %get-tuple-element.21), channel_id=1, source_target_pairs={{0,32},{1,33},{2,34},{3,35},{4,36},{5,37},{6,38},{7,39},{8,40},{9,... | collective-permute-start | bytes 589832 | tf_op jit(solution)/shard_map/ppermute | solution.py:39
  8.5 0.7 %collective-permute-start.8 = (f32[384,128]{1,0:T(8,128)S(1)}, f32[384,128]{1,0:T(8,128)S(1)}, u32[]{:S(2)}, u32[]{:S(2)}) collective-permute-start(f32[384,128]{1,0:T(8,128)S(1)} %get-tuple-element.22), channel_id=1, source_target_pairs={{0,16},{1,17},{2,18},{3,19},{4,20},{5,21},{6,22},{7,23},{8,24},{9,... | collective-permute-start | bytes 589832 | tf_op jit(solution)/shard_map/ppermute | solution.py:39
  9.2 0.4 collective-permute-start.9
  9.6 0.0 collective-permute-done.came
  9.6 0.1 collective-permute-start.1
  9.7 1.3 %collective-permute-done.1.got = f32[256,128]{1,0:T(8,128)S(1)} collective-permute-done((f32[256,128]{1,0:T(8,128)S(1)}, f32[256,128]{1,0:T(8,128)S(1)}, u32[]{:S(2)}, u32[]{:S(2)}) %collective-permute-start.1) | collective-permute-done | bytes 131104 | tf_op jit(solution)/shard_map/ppermute | solution.py:39
  11.1 3.1 %collective-permute-start.4 = (f32[512,128]{1,0:T(8,128)S(1)}, f32[512,128]{1,0:T(8,128)S(1)}, u32[]{:S(2)}, u32[]{:S(2)}) collective-permute-start(f32[512,128]{1,0:T(8,128)S(1)} %group.1.g0), channel_id=1, source_target_pairs={{0,8},{1,9},{2,10},{3,11},{4,12},{5,13},{6,14},{7,15},{8,0},{9,1},... | collective-permute-start | bytes 786440 | tf_op jit(solution)/shard_map/ppermute | solution.py:39
  14.2 0.5 collective-permute-done.7.refs_0_
  14.7 3.1 %collective-permute-done.8.refs_1_ = f32[384,128]{1,0:T(8,128)S(1)} collective-permute-done((f32[384,128]{1,0:T(8,128)S(1)}, f32[384,128]{1,0:T(8,128)S(1)}, u32[]{:S(2)}, u32[]{:S(2)}) %collective-permute-start.8) | collective-permute-done | bytes 196640 | tf_op jit(solution)/shard_map/ppermute | solution.py:39
  17.8 0.0 collective-permute-done.9.refs_2_
  17.9 3.7 %collective-permute-start.10 = (f32[384,128]{1,0:T(8,128)S(1)}, f32[384,128]{1,0:T(8,128)S(1)}, u32[]{:S(2)}, u32[]{:S(2)}) collective-permute-start(f32[384,128]{1,0:T(8,128)S(1)} %total.1.refs_0_), channel_id=1, source_target_pairs={{0,64},{1,65},{2,66},{3,67},{4,68},{5,69},{6,70},{7,71},{8,72},{9,... | collective-permute-start | bytes 589832 | tf_op jit(solution)/shard_map/ppermute | solution.py:39
  21.5 2.8 %collective-permute-start.3 = (f32[512,128]{1,0:T(8,128)S(1)}, f32[512,128]{1,0:T(8,128)S(1)}, u32[]{:S(2)}, u32[]{:S(2)}) collective-permute-start(f32[512,128]{1,0:T(8,128)S(1)} %group.1.g0), channel_id=1, source_target_pairs={{0,12},{1,13},{2,14},{3,15},{4,8},{5,9},{6,10},{7,11},{8,4},{9,5},... | collective-permute-start | bytes 786440 | tf_op jit(solution)/shard_map/ppermute | solution.py:39
  24.3 0.2 collective-permute-start.2
  24.5 0.0 copy-done
  24.5 0.1 copy.8
  24.6 0.1 reshape.16
  24.7 0.0 copy-done.1
  24.7 0.1 copy.9
  24.8 0.1 reshape.17
  24.9 0.7 %collective-permute-done.10.refs_1_ = f32[384,128]{1,0:T(8,128)S(1)} collective-permute-done((f32[384,128]{1,0:T(8,128)S(1)}, f32[384,128]{1,0:T(8,128)S(1)}, u32[]{:S(2)}, u32[]{:S(2)}) %collective-permute-start.10) | collective-permute-done | bytes 196640 | tf_op jit(solution)/shard_map/ppermute | solution.py:39
  25.6 4.0 %collective-permute-start.13 = (f32[384,128]{1,0:T(8,128)S(1)}, f32[384,128]{1,0:T(8,128)S(1)}, u32[]{:S(2)}, u32[]{:S(2)}) collective-permute-start(f32[384,128]{1,0:T(8,128)S(1)} %shift.1.own), channel_id=1, source_target_pairs={{0,32},{1,33},{2,34},{3,35},{4,36},{5,37},{6,38},{7,39},{8,40},{9,... | collective-permute-start | bytes 589832 | tf_op jit(solution)/shard_map/ppermute | solution.py:39
  29.5 0.7 %collective-permute-start.12 = (f32[384,128]{1,0:T(8,128)S(1)}, f32[384,128]{1,0:T(8,128)S(1)}, u32[]{:S(2)}, u32[]{:S(2)}) collective-permute-start(f32[384,128]{1,0:T(8,128)S(1)} %shift.1.own), channel_id=1, source_target_pairs={{0,16},{1,17},{2,18},{3,19},{4,20},{5,21},{6,22},{7,23},{8,24},{9,... | collective-permute-start | bytes 589832 | tf_op jit(solution)/shard_map/ppermute | solution.py:39
  30.2 0.0 collective-permute-done.4.g2
  30.2 0.0 collective-permute-start.11
  30.2 0.6 %pad_add_fusion.table_hbm = s32[128]{0:T(128)} fusion(s32[64]{0:T(128)S(1)} %reshape.17, s32[64]{0:T(128)S(1)} %reshape.16), kind=kLoop, calls=%fused_computation | loop fusion | flops 128 | bytes 1024 | tf_op jit(solution)/shard_map/concatenate | solution.py:371
  30.8 0.0 collective-permute-done.3.g3
  30.8 0.1 collective-permute-done.2.g1
  30.9 1.0 %pick.1 = (f32[64,128]{1,0:T(8,128)S(1)}, f32[64,128]{1,0:T(8,128)S(1)}, f32[128,128]{1,0:T(8,128)S(1)}, f32[64,128]{1,0:T(8,128)S(1)}, f32[64,128]{1,0:T(8,128)S(1)}) custom-call(s32[128]{0:T(128)} %pad_add_fusion.table_hbm, f32[512,128]{1,0:T(8,128)S(1)} %group.1.g0, f32[512,128]{1,0:T(8,128)S(1)} %collective-permute-done.2.g1, ...), custom_call_target="tpu_custom_call" | custom-call | tf_op jit(solution)/shard_map/pick/pallas_call | solution.py:228
  31.9 0.4 collective-permute-start.5
  32.3 0.0 collective-permute-start.14
  32.3 1.2 %collective-permute-done.14.came = f32[64,128]{1,0:T(8,128)S(1)} collective-permute-done((f32[64,128]{1,0:T(8,128)S(1)}, f32[64,128]{1,0:T(8,128)S(1)}, u32[]{:S(2)}, u32[]{:S(2)}) %collective-permute-start.14) | collective-permute-done | bytes 32800 | tf_op jit(solution)/shard_map/ppermute | solution.py:39
  33.5 3.3 %collective-permute-start.15 = (f32[64,128]{1,0:T(8,128)S(1)}, f32[64,128]{1,0:T(8,128)S(1)}, u32[]{:S(2)}, u32[]{:S(2)}) collective-permute-start(f32[64,128]{1,0:T(8,128)S(1)} %merge.1.refs_0_), channel_id=1, source_target_pairs={{0,64},{1,65},{2,66},{3,67},{4,68},{5,69},{6,70},{7,71},{8,72},{9,... | collective-permute-start | bytes 98312 | tf_op jit(solution)/shard_map/ppermute | solution.py:39
  36.8 0.0 collective-permute-done.5.back
  36.9 0.1 collective-permute-start.6
  36.9 2.0 %collective-permute-done.15.refs_1_ = f32[64,128]{1,0:T(8,128)S(1)} collective-permute-done((f32[64,128]{1,0:T(8,128)S(1)}, f32[64,128]{1,0:T(8,128)S(1)}, u32[]{:S(2)}, u32[]{:S(2)}) %collective-permute-start.15) | collective-permute-done | bytes 32800 | tf_op jit(solution)/shard_map/ppermute | solution.py:39
  39.0 3.7 %collective-permute-start.18 = (f32[64,128]{1,0:T(8,128)S(1)}, f32[64,128]{1,0:T(8,128)S(1)}, u32[]{:S(2)}, u32[]{:S(2)}) collective-permute-start(f32[64,128]{1,0:T(8,128)S(1)} %edge.1.edge0), channel_id=1, source_target_pairs={{0,32},{1,33},{2,34},{3,35},{4,36},{5,37},{6,38},{7,39},{8,40},{9,... | collective-permute-start | bytes 98312 | tf_op jit(solution)/shard_map/ppermute | solution.py:39
  42.7 0.0 collective-permute-done.13.a
  42.7 0.7 %collective-permute-start.17 = (f32[64,128]{1,0:T(8,128)S(1)}, f32[64,128]{1,0:T(8,128)S(1)}, u32[]{:S(2)}, u32[]{:S(2)}) collective-permute-start(f32[64,128]{1,0:T(8,128)S(1)} %edge.1.edge0), channel_id=1, source_target_pairs={{0,16},{1,17},{2,18},{3,19},{4,20},{5,21},{6,22},{7,23},{8,24},{9,... | collective-permute-start | bytes 98312 | tf_op jit(solution)/shard_map/ppermute | solution.py:39
  43.3 0.0 collective-permute-done.12.b
  43.4 0.1 collective-permute-start.16
  43.4 0.0 collective-permute-done.11.c
  43.4 1.4 %collective-permute-done.18.edge3 = f32[64,128]{1,0:T(8,128)S(1)} collective-permute-done((f32[64,128]{1,0:T(8,128)S(1)}, f32[64,128]{1,0:T(8,128)S(1)}, u32[]{:S(2)}, u32[]{:S(2)}) %collective-permute-start.18) | collective-permute-done | bytes 32800 | tf_op jit(solution)/shard_map/ppermute | solution.py:39
  44.8 1.8 %collective-permute-done.17.edge2 = f32[64,128]{1,0:T(8,128)S(1)} collective-permute-done((f32[64,128]{1,0:T(8,128)S(1)}, f32[64,128]{1,0:T(8,128)S(1)}, u32[]{:S(2)}, u32[]{:S(2)}) %collective-permute-start.17) | collective-permute-done | bytes 32800 | tf_op jit(solution)/shard_map/ppermute | solution.py:39
  46.6 1.9 %collective-permute-done.16.edge1 = f32[64,128]{1,0:T(8,128)S(1)} collective-permute-done((f32[64,128]{1,0:T(8,128)S(1)}, f32[64,128]{1,0:T(8,128)S(1)}, u32[]{:S(2)}, u32[]{:S(2)}) %collective-permute-start.16) | collective-permute-done | bytes 32800 | tf_op jit(solution)/shard_map/ppermute | solution.py:39
  48.5 0.0 collective-permute-done.6.got
  48.5 6.2 %advance.1 = f32[4,12,128,128]{3,2,1,0:T(8,128)} custom-call(f32[4,12,128,128]{3,2,1,0:T(8,128)} %bitcast.4, f32[64,128]{1,0:T(8,128)S(1)} %get-tuple-element.18.stay, f32[128,128]{1,0:T(8,128)S(1)} %collective-permute-done.5.back, f32[128,128]{1,0:T(8,128)S(1)} %collective-permute-done.6.got, f32[384,128]{1,0:T(8,128)S(1)} %shift.1.own, ...), custom_call_target="tpu_custom_call" | custom-call | flops 40000000 | bytes 8000000 | tf_op jit(solution)/shard_map/advance/pallas_call | solution.py:344
  (9 shorter events, 0.1 us)
Async XLA Ops:
  0.0 24.5 %copy-start = (s32[16,4]{0,1:T(4,128)S(1)}, s32[16,4]{0,1:T(4,128)}, u32[]{:S(2)}) copy-start(s32[16,4]{0,1:T(4,128)} %param.8) | copy-start | bytes 772
  0.0 24.7 %copy-start.1 = (s32[16,4]{0,1:T(4,128)S(1)}, s32[16,4]{0,1:T(4,128)}, u32[]{:S(2)}) copy-start(s32[16,4]{0,1:T(4,128)} %param.9) | copy-start | bytes 772
  3.3 6.3 %collective-permute-start = (f32[256,128]{1,0:T(8,128)S(1)}, f32[256,128]{1,0:T(8,128)S(1)}, u32[]{:S(2)}, u32[]{:S(2)}) collective-permute-start(f32[256,128]{1,0:T(8,128)S(1)} %get-tuple-element.17), channel_id=1, source_target_pairs={{0,2},{1,3},{2,0},{3,1},{4,6},{5,7},{6,4},{7,5},{8,10},{9,11},{10,... | collective-permute-start | bytes 393224 | tf_op jit(solution)/shard_map/ppermute | solution.py:39
  5.3 9.3 %collective-permute-start.7 = (f32[384,128]{1,0:T(8,128)S(1)}, f32[384,128]{1,0:T(8,128)S(1)}, u32[]{:S(2)}, u32[]{:S(2)}) collective-permute-start(f32[384,128]{1,0:T(8,128)S(1)} %get-tuple-element.21), channel_id=1, source_target_pairs={{0,32},{1,33},{2,34},{3,35},{4,36},{5,37},{6,38},{7,39},{8,40},{9,... | collective-permute-start | bytes 589832 | tf_op jit(solution)/shard_map/ppermute | solution.py:39
  8.5 9.3 %collective-permute-start.8 = (f32[384,128]{1,0:T(8,128)S(1)}, f32[384,128]{1,0:T(8,128)S(1)}, u32[]{:S(2)}, u32[]{:S(2)}) collective-permute-start(f32[384,128]{1,0:T(8,128)S(1)} %get-tuple-element.22), channel_id=1, source_target_pairs={{0,16},{1,17},{2,18},{3,19},{4,20},{5,21},{6,22},{7,23},{8,24},{9,... | collective-permute-start | bytes 589832 | tf_op jit(solution)/shard_map/ppermute | solution.py:39
  9.2 8.6 %collective-permute-start.9 = (f32[384,128]{1,0:T(8,128)S(1)}, f32[384,128]{1,0:T(8,128)S(1)}, u32[]{:S(2)}, u32[]{:S(2)}) collective-permute-start(f32[384,128]{1,0:T(8,128)S(1)} %get-tuple-element.23), channel_id=1, source_target_pairs={{0,48},{1,49},{2,50},{3,51},{4,52},{5,53},{6,54},{7,55},{8,56},{9,... | collective-permute-start | bytes 589832 | tf_op jit(solution)/shard_map/ppermute | solution.py:39
  9.6 1.4 %collective-permute-start.1 = (f32[256,128]{1,0:T(8,128)S(1)}, f32[256,128]{1,0:T(8,128)S(1)}, u32[]{:S(2)}, u32[]{:S(2)}) collective-permute-start(f32[256,128]{1,0:T(8,128)S(1)} %split.1), channel_id=1, source_target_pairs={{0,1},{1,0},{2,3},{3,2},{4,5},{5,4},{6,7},{7,6},{8,9},{9,8},{10,11... | collective-permute-start | bytes 393224 | tf_op jit(solution)/shard_map/ppermute | solution.py:39
  11.1 19.1 %collective-permute-start.4 = (f32[512,128]{1,0:T(8,128)S(1)}, f32[512,128]{1,0:T(8,128)S(1)}, u32[]{:S(2)}, u32[]{:S(2)}) collective-permute-start(f32[512,128]{1,0:T(8,128)S(1)} %group.1.g0), channel_id=1, source_target_pairs={{0,8},{1,9},{2,10},{3,11},{4,12},{5,13},{6,14},{7,15},{8,0},{9,1},... | collective-permute-start | bytes 786440 | tf_op jit(solution)/shard_map/ppermute | solution.py:39
  17.9 7.7 %collective-permute-start.10 = (f32[384,128]{1,0:T(8,128)S(1)}, f32[384,128]{1,0:T(8,128)S(1)}, u32[]{:S(2)}, u32[]{:S(2)}) collective-permute-start(f32[384,128]{1,0:T(8,128)S(1)} %total.1.refs_0_), channel_id=1, source_target_pairs={{0,64},{1,65},{2,66},{3,67},{4,68},{5,69},{6,70},{7,71},{8,72},{9,... | collective-permute-start | bytes 589832 | tf_op jit(solution)/shard_map/ppermute | solution.py:39
  21.5 9.3 %collective-permute-start.3 = (f32[512,128]{1,0:T(8,128)S(1)}, f32[512,128]{1,0:T(8,128)S(1)}, u32[]{:S(2)}, u32[]{:S(2)}) collective-permute-start(f32[512,128]{1,0:T(8,128)S(1)} %group.1.g0), channel_id=1, source_target_pairs={{0,12},{1,13},{2,14},{3,15},{4,8},{5,9},{6,10},{7,11},{8,4},{9,5},... | collective-permute-start | bytes 786440 | tf_op jit(solution)/shard_map/ppermute | solution.py:39
  24.3 6.6 %collective-permute-start.2 = (f32[512,128]{1,0:T(8,128)S(1)}, f32[512,128]{1,0:T(8,128)S(1)}, u32[]{:S(2)}, u32[]{:S(2)}) collective-permute-start(f32[512,128]{1,0:T(8,128)S(1)} %group.1.g0), channel_id=1, source_target_pairs={{0,4},{1,5},{2,6},{3,7},{4,0},{5,1},{6,2},{7,3},{8,12},{9,13},{10,... | collective-permute-start | bytes 786440 | tf_op jit(solution)/shard_map/ppermute | solution.py:39
  25.6 17.1 %collective-permute-start.13 = (f32[384,128]{1,0:T(8,128)S(1)}, f32[384,128]{1,0:T(8,128)S(1)}, u32[]{:S(2)}, u32[]{:S(2)}) collective-permute-start(f32[384,128]{1,0:T(8,128)S(1)} %shift.1.own), channel_id=1, source_target_pairs={{0,32},{1,33},{2,34},{3,35},{4,36},{5,37},{6,38},{7,39},{8,40},{9,... | collective-permute-start | bytes 589832 | tf_op jit(solution)/shard_map/ppermute | solution.py:39
  29.5 13.8 %collective-permute-start.12 = (f32[384,128]{1,0:T(8,128)S(1)}, f32[384,128]{1,0:T(8,128)S(1)}, u32[]{:S(2)}, u32[]{:S(2)}) collective-permute-start(f32[384,128]{1,0:T(8,128)S(1)} %shift.1.own), channel_id=1, source_target_pairs={{0,16},{1,17},{2,18},{3,19},{4,20},{5,21},{6,22},{7,23},{8,24},{9,... | collective-permute-start | bytes 589832 | tf_op jit(solution)/shard_map/ppermute | solution.py:39
  30.2 13.3 %collective-permute-start.11 = (f32[384,128]{1,0:T(8,128)S(1)}, f32[384,128]{1,0:T(8,128)S(1)}, u32[]{:S(2)}, u32[]{:S(2)}) collective-permute-start(f32[384,128]{1,0:T(8,128)S(1)} %shift.1.own), channel_id=1, source_target_pairs={{0,48},{1,49},{2,50},{3,51},{4,52},{5,53},{6,54},{7,55},{8,56},{9,... | collective-permute-start | bytes 589832 | tf_op jit(solution)/shard_map/ppermute | solution.py:39
  31.9 4.9 %collective-permute-start.5 = (f32[128,128]{1,0:T(8,128)S(1)}, f32[128,128]{1,0:T(8,128)S(1)}, u32[]{:S(2)}, u32[]{:S(2)}) collective-permute-start(f32[128,128]{1,0:T(8,128)S(1)} %get-tuple-element.19), channel_id=1, source_target_pairs={{0,2},{1,3},{2,0},{3,1},{4,6},{5,7},{6,4},{7,5},{8,10},{9,11},{10,... | collective-permute-start | bytes 196616 | tf_op jit(solution)/shard_map/ppermute | solution.py:39
  32.3 1.2 %collective-permute-start.14 = (f32[64,128]{1,0:T(8,128)S(1)}, f32[64,128]{1,0:T(8,128)S(1)}, u32[]{:S(2)}, u32[]{:S(2)}) collective-permute-start(f32[64,128]{1,0:T(8,128)S(1)} %get-tuple-element.26), channel_id=1, source_target_pairs={{0,1},{1,0},{2,3},{3,2},{4,5},{5,4},{6,7},{7,6},{8,9},{9,8},{10,11... | collective-permute-start | bytes 98312 | tf_op jit(solution)/shard_map/ppermute | solution.py:39
  33.5 5.5 %collective-permute-start.15 = (f32[64,128]{1,0:T(8,128)S(1)}, f32[64,128]{1,0:T(8,128)S(1)}, u32[]{:S(2)}, u32[]{:S(2)}) collective-permute-start(f32[64,128]{1,0:T(8,128)S(1)} %merge.1.refs_0_), channel_id=1, source_target_pairs={{0,64},{1,65},{2,66},{3,67},{4,68},{5,69},{6,70},{7,71},{8,72},{9,... | collective-permute-start | bytes 98312 | tf_op jit(solution)/shard_map/ppermute | solution.py:39
  36.9 11.6 %collective-permute-start.6 = (f32[128,128]{1,0:T(8,128)S(1)}, f32[128,128]{1,0:T(8,128)S(1)}, u32[]{:S(2)}, u32[]{:S(2)}) collective-permute-start(f32[128,128]{1,0:T(8,128)S(1)} %couple.1), channel_id=1, source_target_pairs={{0,1},{1,0},{2,3},{3,2},{4,5},{5,4},{6,7},{7,6},{8,9},{9,8},{10,11... | collective-permute-start | bytes 196616 | tf_op jit(solution)/shard_map/ppermute | solution.py:39
  39.0 5.8 %collective-permute-start.18 = (f32[64,128]{1,0:T(8,128)S(1)}, f32[64,128]{1,0:T(8,128)S(1)}, u32[]{:S(2)}, u32[]{:S(2)}) collective-permute-start(f32[64,128]{1,0:T(8,128)S(1)} %edge.1.edge0), channel_id=1, source_target_pairs={{0,32},{1,33},{2,34},{3,35},{4,36},{5,37},{6,38},{7,39},{8,40},{9,... | collective-permute-start | bytes 98312 | tf_op jit(solution)/shard_map/ppermute | solution.py:39
  42.7 3.9 %collective-permute-start.17 = (f32[64,128]{1,0:T(8,128)S(1)}, f32[64,128]{1,0:T(8,128)S(1)}, u32[]{:S(2)}, u32[]{:S(2)}) collective-permute-start(f32[64,128]{1,0:T(8,128)S(1)} %edge.1.edge0), channel_id=1, source_target_pairs={{0,16},{1,17},{2,18},{3,19},{4,20},{5,21},{6,22},{7,23},{8,24},{9,... | collective-permute-start | bytes 98312 | tf_op jit(solution)/shard_map/ppermute | solution.py:39
  43.4 5.1 %collective-permute-start.16 = (f32[64,128]{1,0:T(8,128)S(1)}, f32[64,128]{1,0:T(8,128)S(1)}, u32[]{:S(2)}, u32[]{:S(2)}) collective-permute-start(f32[64,128]{1,0:T(8,128)S(1)} %edge.1.edge0), channel_id=1, source_target_pairs={{0,48},{1,49},{2,50},{3,51},{4,52},{5,53},{6,54},{7,55},{8,56},{9,... | collective-permute-start | bytes 98312 | tf_op jit(solution)/shard_map/ppermute | solution.py:39

commit v5 on v4

--- a/solution.py
+++ b/solution.py
@@ -21,7 +21,7 @@
 RECORD = 4 * SLOT
 USED = 16
 STRIP = 4 * USED
-STEPS = (2, 1, 3)
+STEPS = (1, 3, 2)
 F32 = jnp.float32
 
 
@@ -198,17 +198,21 @@
     out[3 * RECORD :, :] = got[RECORD:, :]
 
 
-def pick_kernel(table_hbm, g0, g1, g3, g2, stay, stay_sib, leave, half, half_sib, table, sem):
+def pick_kernel(near_hbm, codes_hbm, g0, g1, g3, g2, stay, stay_sib, leave, half, half_sib, near, codes, sems):
     _, patch = here()
-    copy = pltpu.make_async_copy(table_hbm, table, sem)
-    copy.start()
-    copy.wait()
+    copies = [
+        pltpu.make_async_copy(near_hbm, near, sems.at[0]),
+        pltpu.make_async_copy(codes_hbm, codes, sems.at[1]),
+    ]
+    for copy in copies:
+        copy.start()
+    for copy in copies:
+        copy.wait()
     for q in range(4):
         to, base, rows = ((stay, 0, SLOT), (stay_sib, 0, SLOT), (leave, 0, 24), (leave, STRIP, 24))[q]
         for side in range(4):
-            spot = (patch ^ q) * 4 + side
-            away = table[spot] ^ patch
-            code = table[64 + spot]
+            away = near[side, patch ^ q] ^ patch
+            code = codes[side, patch ^ q]
             source = pl.ds(pl.multiple_of((away % 4) * RECORD + (code % 4) * SLOT, 8), rows)
             value = g0[source, :]
             for x, g in ((1, g1), (2, g2), (3, g3)):
@@ -224,16 +228,16 @@
                 to_half[at + 10 : at + USED, :] = jnp.zeros((6, SIZE), F32)
 
 
-def pick(table, g0, g1, g2, g3):
+def pick(neighbours, codes, g0, g1, g2, g3):
     return pl.pallas_call(
         pick_kernel,
         out_shape=shaped(STRIP, STRIP, 2 * STRIP, STRIP, STRIP),
-        in_specs=[hbm()] + [vmem()] * 4,
+        in_specs=[hbm()] * 2 + [vmem()] * 4,
         out_specs=[vmem()] * 5,
-        scratch_shapes=[pltpu.SMEM((128,), jnp.int32), pltpu.SemaphoreType.DMA],
+        scratch_shapes=[pltpu.SMEM((4, N_DOMAIN), jnp.int32)] * 2 + [pltpu.SemaphoreType.DMA((2,))],
         compiler_params=limit(4),
         name="pick",
-    )(*on(pltpu.HBM, table), *on(pltpu.VMEM, g0, g1, g3, g2))
+    )(*on(pltpu.HBM, neighbours, codes), *on(pltpu.VMEM, g0, g1, g3, g2))
 
 
 def merge_kernel(half, came, out):
@@ -261,22 +265,50 @@
     return ahead - behind
 
 
-def advance_kernel(ens_hbm, stay, back, got, own, c, b, a, edge0, edge1, edge2, edge3, out, ens, sems, shift, rims, lines, columns, pad, div, slope_u):
+def recentre_kernel(ens_hbm, own, c, b, a, out, ens, shift, sems):
+    copies = [pltpu.make_async_copy(ens_hbm.at[n], ens.at[n], sems.at[n]) for n in range(LOCAL)]
+    for copy in copies:
+        copy.start()
+    member, _ = here()
+    for step, m in zip((0,) + STEPS, (own, a, b, c)):
+        for half in (0, 1):
+            at = pl.multiple_of(half * HALF + (member % 4 ^ step) * CHUNK, 8)
+            shift[pl.ds(at, CHUNK), :] = m[half * CHUNK : (half + 1) * CHUNK, :]
+    for n in range(LOCAL):
+        copies[n].wait()
+        for i in range(PLANES):
+            out[n, i, 0:8, :] = jnp.zeros((8, SIZE), F32)
+            out[n, i, 8 + SIZE :, :] = jnp.zeros((8, SIZE), F32)
+            for r in range(0, SIZE, 32):
+                out[n, i, 8 + r : 40 + r, :] = ens[n, i, r : r + 32, :] + shift[i * SIZE + r : i * SIZE + r + 32, :]
+
+
+def recentre(ensemble, arrays):
+    return pl.pallas_call(
+        recentre_kernel,
+        out_shape=pltpu.VMEM((LOCAL, PLANES, SIZE + 16, SIZE), F32),
+        in_specs=[hbm()] + [vmem()] * len(arrays),
+        out_specs=vmem(),
+        scratch_shapes=[
+            pltpu.VMEM((LOCAL, PLANES, SIZE, SIZE), F32),
+            pltpu.VMEM((ROWS, SIZE), F32),
+            pltpu.SemaphoreType.DMA((LOCAL,)),
+        ],
+        compiler_params=limit(12),
+        name="recentre",
+    )(*on(pltpu.HBM, ensemble), *on(pltpu.VMEM, *arrays))
+
+
+def advance_kernel(fields, stay, back, got, edge0, edge1, out, rims, lines, columns, div, slope_u):
     now_at = pl.program_id(0)
 
     @pl.when(now_at == 0)
     def _():
-        for n in range(LOCAL):
-            pltpu.make_async_copy(ens_hbm.at[n], ens.at[n], sems.at[n]).start()
-        member, patch = here()
+        _, patch = here()
         core, z = patch % 2, (patch // 2) % 2
-        for step, m in zip((0,) + STEPS, (own, a, b, c)):
-            for half in (0, 1):
-                at = pl.multiple_of(half * HALF + (member % 4 ^ step) * CHUNK, 8)
-                shift[pl.ds(at, CHUNK), :] = m[half * CHUNK : (half + 1) * CHUNK, :]
         for side in range(4):
             rows = slice(side * USED, (side + 1) * USED)
-            moved = (edge0[rows, :] + edge1[rows, :]) + (edge2[rows, :] + edge3[rows, :])
+            moved = edge0[rows, :] + edge1[rows, :]
             for source, who in (
                 (stay[rows, :], 2 * core + z),
                 (back[rows, :], 2 * core + 1 - z),
@@ -297,78 +329,79 @@
             columns[n] = turned if n == 0 else pltpu.roll(turned, SIZE - 32 * n, 1)
 
     step = now_at
-    pltpu.make_async_copy(ens_hbm.at[step], ens.at[step], sems.at[step]).wait()
     part = 32
     lane = lax.broadcasted_iota(jnp.int32, (part, SIZE), 1)
+    row = lax.broadcasted_iota(jnp.int32, (part, SIZE), 0)
     at_left, at_right = lane == 0, lane == SIZE - 1
+
+    def rows_at(i, r):
+        return fields[step, i, 8 + r : 8 + r + part, :]
+
+    def above(i, r):
+        value = fields[step, i, 7 + r : 7 + r + part, :]
+        return jnp.where(row == 0, rims[step, 0, i : i + 1, :], value) if r == 0 else value
+
+    def below(i, r):
+        value = fields[step, i, 9 + r : 9 + r + part, :]
+        return jnp.where(row == part - 1, rims[step, 1, i : i + 1, :], value) if r == SIZE - part else value
 
     def across(x, r, line):
         edge = pltpu.roll(columns[step, r : r + part, :], (SIZE - 1 - 2 * line) % SIZE, 1)
         return jnp.where(at_right, edge, pltpu.roll(x, SIZE - 1, 1)) - jnp.where(at_left, edge, pltpu.roll(x, 1, 1))
 
     for lev in range(LEV):
-        for f in range(3):
-            i = f * LEV + lev
-            pad[f, 8 : 8 + SIZE, :] = ens[step, i] + shift[i * SIZE : (i + 1) * SIZE, :]
-            pad[f, 7:8, :] = rims[step, 0, i : i + 1, :]
-            pad[f, 8 + SIZE : 9 + SIZE, :] = rims[step, 1, i : i + 1, :]
-        i = PLANES + lev
-        div[7:8, :] = 0.5 * (slope(pad[0, 7:8, :]) + pad[1, 8:9, :] - rims[step, 0, i : i + 1, :])
+        iu, iv, iw, deep = lev, LEV + lev, 2 * LEV + lev, PLANES + lev
+        div[7:8, :] = 0.5 * (
+            slope(rims[step, 0, iu : iu + 1, :]) + fields[step, iv, 8:9, :] - rims[step, 0, deep : deep + 1, :]
+        )
         div[8 + SIZE : 9 + SIZE, :] = 0.5 * (
-            slope(pad[0, 8 + SIZE : 9 + SIZE, :]) + rims[step, 1, i : i + 1, :] - pad[1, 7 + SIZE : 8 + SIZE, :]
+            slope(rims[step, 1, iu : iu + 1, :])
+            + rims[step, 1, deep : deep + 1, :]
+            - fields[step, iv, 7 + SIZE : 8 + SIZE, :]
         )
         for r in range(0, SIZE, part):
-            at = 8 + r
-            du = across(pad[0, at : at + part, :], r, lev)
+            du = across(rows_at(iu, r), r, iu)
             slope_u[r : r + part, :] = du
-            div[at : at + part, :] = 0.5 * (du + pad[1, at + 1 : at + 1 + part, :] - pad[1, at - 1 : at - 1 + part, :])
+            div[8 + r : 8 + r + part, :] = 0.5 * (du + below(iv, r) - above(iv, r))
         for r in range(0, SIZE, part):
-            at = 8 + r
-            now = slice(at, at + part)
-            up, down = slice(at - 1, at - 1 + part), slice(at + 1, at + 1 + part)
-            u, v, w = pad[0, now, :], pad[1, now, :], pad[2, now, :]
-            edge = pltpu.roll(columns[step, r : r + part, :], (SIZE - 1 - 2 * (PLANES + lev)) % SIZE, 1)
+            u, v, w = rows_at(iu, r), rows_at(iv, r), rows_at(iw, r)
+            edge = pltpu.roll(columns[step, r : r + part, :], (SIZE - 1 - 2 * deep) % SIZE, 1)
             edge = edge + jnp.where(at_left, 0.5 * u, -0.5 * u)
-            mid = div[now, :]
+            mid = div[8 + r : 8 + r + part, :]
             grad_x = jnp.where(at_right, edge, pltpu.roll(mid, SIZE - 1, 1)) - jnp.where(at_left, edge, pltpu.roll(mid, 1, 1))
-            grad_y = div[down, :] - div[up, :]
-            new_u = u - 0.2 * (u * slope_u[r : r + part, :] + v * (pad[0, down, :] - pad[0, up, :]))
-            new_v = v - 0.2 * (u * across(v, r, LEV + lev) + v * (pad[1, down, :] - pad[1, up, :]))
-            new_w = w - 0.2 * (u * across(w, r, 2 * LEV + lev) + v * (pad[2, down, :] - pad[2, up, :]))
-            out[0, lev, r : r + part, :] = new_u + 0.1 * grad_x
-            out[0, LEV + lev, r : r + part, :] = new_v + 0.1 * grad_y
-            out[0, 2 * LEV + lev, r : r + part, :] = new_w
-
-
-def advance(ensemble, *arrays):
+            grad_y = div[9 + r : 9 + r + part, :] - div[7 + r : 7 + r + part, :]
+            new_u = u - 0.2 * (u * slope_u[r : r + part, :] + v * (below(iu, r) - above(iu, r)))
+            new_v = v - 0.2 * (u * across(v, r, iv) + v * (below(iv, r) - above(iv, r)))
+            new_w = w - 0.2 * (u * across(w, r, iw) + v * (below(iw, r) - above(iw, r)))
+            out[0, iu, r : r + part, :] = new_u + 0.1 * grad_x
+            out[0, iv, r : r + part, :] = new_v + 0.1 * grad_y
+            out[0, iw, r : r + part, :] = new_w
+
+
+def advance(*arrays):
     return pl.pallas_call(
         advance_kernel,
         out_shape=jax.ShapeDtypeStruct((LOCAL, PLANES, SIZE, SIZE), F32),
         grid=(LOCAL,),
-        in_specs=[hbm()] + [vmem()] * len(arrays),
+        in_specs=[vmem()] * len(arrays),
         out_specs=pl.BlockSpec((1, PLANES, SIZE, SIZE), lambda n: (n, 0, 0, 0)),
         scratch_shapes=[
-            pltpu.VMEM((LOCAL, PLANES, SIZE, SIZE), F32),
-            pltpu.SemaphoreType.DMA((LOCAL,)),
-            pltpu.VMEM((ROWS, SIZE), F32),
             pltpu.VMEM((LOCAL, 4, USED, SIZE), F32),
             pltpu.VMEM((SIZE, SIZE), F32),
             pltpu.VMEM((LOCAL, SIZE, SIZE), F32),
-            pltpu.VMEM((3, SIZE + 16, SIZE), F32),
             pltpu.VMEM((SIZE + 16, SIZE), F32),
             pltpu.VMEM((SIZE, SIZE), F32),
         ],
-        compiler_params=limit(12),
+        compiler_params=limit(8),
         cost_estimate=pl.CostEstimate(flops=40_000_000, bytes_accessed=8_000_000, transcendentals=0),
         name="advance",
-    )(*on(pltpu.HBM, ensemble), *on(pltpu.VMEM, *arrays))
+    )(*on(pltpu.VMEM, *arrays))
 
 
 def on_device(ensemble, control, owner, neighbours, codes):
     shape = ensemble.shape
     ensemble = ensemble.reshape(LOCAL, PLANES, SIZE, SIZE)
     control = control.reshape(PLANES, SIZE, SIZE)
-    table = jnp.concatenate([neighbours.reshape(-1), codes.reshape(-1)])
 
     keep, *gives, stay, leave = prepare(owner, ensemble, control)
     strips = send(leave, lambda m, d: (m, d ^ 2))
@@ -377,13 +410,16 @@
     total = small(sum_kernel, "total", 2 * CHUNK, [*over_y(gives), keep])
     total = small(sum_kernel, "shift", 2 * CHUNK, [total, over_z_hi(total)])
     chunks = over_y([total] * 3)
-    stay, stay_sib, leave, half, half_sib = pick(table, group, *over_x(group))
+    stay, stay_sib, leave, half, half_sib = pick(neighbours.T, codes.T, group, *over_x(group))
+    came = swap_cores(half_sib)
     back = send(leave, lambda m, d: (m, d ^ 2))
     got = swap_cores(small(couple_kernel, "couple", 2 * STRIP, [stay_sib, back]))
-    edge = small(merge_kernel, "merge", STRIP, [half, swap_cores(half_sib)])
+    edge = small(merge_kernel, "merge", STRIP, [half, came])
     edge = small(sum_kernel, "edge", STRIP, [edge, over_z_hi(edge)])
-    edges = over_y([edge] * 3)
-    out = advance(ensemble, stay, back, got, total, *chunks[::-1], edge, *edges[::-1])
+    edge = small(sum_kernel, "edge", STRIP, [edge, send(edge, lambda m, d: (m ^ 1, d))])
+    other = send(edge, lambda m, d: (m ^ 3, d))
+    fields = recentre(ensemble, [total, *chunks[::-1]])
+    out = advance(fields, stay, back, got, edge, other)
     return out.reshape(shape)
 
 

time: 54.8 us -> 52.7 us (0.962)
  starting transfers between devices: 29 us -> 25.1 us
  waiting for transfers between devices: 14 us -> 15.7 us
  Pallas kernels: 10.6 us -> 11.6 us
  other arithmetic: 0.58 us -> 0 us
    ppermute x19 -> x18, starting transfers between devices: 29 us -> 25.1 us  [send(): return lax.ppermute(array, MESH, pairs(target))]
    pallas_call x0 -> x1, Pallas kernels: none -> 1.97 us  [recentre(): pl.pallas_call(recentre_kernel, out_shape=pltpu.VMEM((LOCAL, PLANES, SIZE...]
    ppermute x19 -> x18, waiting for transfers between devices: 14 us -> 15.7 us  [send(): return lax.ppermute(array, MESH, pairs(target))]
    pallas_call x1, Pallas kernels: 6.21 us -> 5.21 us  [advance(): pl.pallas_call(advance_kernel, out_shape=jax.ShapeDtypeStruct((LOCAL, PLA...]
    concatenate x1 -> x0, other arithmetic: 0.58 us -> none  [on_device(): table = jnp.concatenate([neighbours.reshape(-1), codes.reshape(-1)])]
  transfers between devices with their start and end apart: 19 -> 18, of which waited for: 10 -> 8; matrix products, arithmetic and copies ran while one was open for 2% -> 0% of each run, Pallas kernels for 2% -> 6%
where the time goes in v5:
time: 52.7 us; the launch traced here: 52.5 us
  starting transfers between devices  25.1 us (48%)
  waiting for transfers between devices  15.7 us (30%)
  Pallas kernels  11.6 us (22%)
    ppermute x18, starting transfers between devices, send(): return lax.ppermute(array, MESH, pairs(target))  25.1 us
    ppermute x18, waiting for transfers between devices, send(): return lax.ppermute(array, MESH, pairs(target))  15.7 us
    pallas_call x1, Pallas kernels, advance(): pl.pallas_call(advance_kernel, out_shape=jax.ShapeDtypeStruct((LOCAL, PLA...  5.21 us
    pallas_call x1, Pallas kernels, prepare(): pl.pallas_call(prepare_kernel, out_shape=shaped(*[2 * CHUNK] * 4, 2 * REC...  3.22 us
    pallas_call x1, Pallas kernels, recentre(): pl.pallas_call(recentre_kernel, out_shape=pltpu.VMEM((LOCAL, PLANES, SIZE...  1.97 us
    pallas_call x1, Pallas kernels, pick(): pl.pallas_call(pick_kernel, out_shape=shaped(STRIP, STRIP, 2 * STRIP, STR...  1.08 us
  transfers between devices with their start and end apart: 18, of which 8 were waited for; matrix products, arithmetic and copies ran while one was open for 0% of the time, Pallas kernels for 6%

profile of v5, /device:TPU:0, one launch (start us, length us, event | category | flops | bytes accessed | tf_op | source)
XLA Modules:
  0.0 52.5 jit_solution(4880245021330460164)
XLA Ops:
  0.0 3.2 %prepare.1 = (f32[384,128]{1,0:T(8,128)S(1)}, f32[384,128]{1,0:T(8,128)S(1)}, f32[384,128]{1,0:T(8,128)S(1)}, f32[384,128]{1,0:T(8,128)S(1)}, f32[256,128]{1,0:T(8,128)S(1)}, /*index=5*/f32[256,128]{1,0:T(8,128)S(1)}) custom-call(s32[16]{0:T(128)} %owner_hbm.1, f32[4,12,128,128]{3,2,1,0:T(8,128)} %bitcast.5, f32[12,128,128]{2,1,0:T(8,128)} %bitcast.7), custom_call_target="tpu_custom_call" | custom-call | flops 2000000 | bytes 5000000 | tf_op jit(solution)/shard_map/prepare/pallas_call | solution.py:143
  3.2 2.1 %collective-permute-start.7 = (f32[256,128]{1,0:T(8,128)S(1)}, f32[256,128]{1,0:T(8,128)S(1)}, u32[]{:S(2)}, u32[]{:S(2)}) collective-permute-start(f32[256,128]{1,0:T(8,128)S(1)} %get-tuple-element.21), channel_id=1, source_target_pairs={{0,2},{1,3},{2,0},{3,1},{4,6},{5,7},{6,4},{7,5},{8,10},{9,11},{10,... | collective-permute-start | bytes 393224 | tf_op jit(solution)/shard_map/ppermute | solution.py:39
  5.3 1.6 %collective-permute-start = (f32[384,128]{1,0:T(8,128)S(1)}, f32[384,128]{1,0:T(8,128)S(1)}, u32[]{:S(2)}, u32[]{:S(2)}) collective-permute-start(f32[384,128]{1,0:T(8,128)S(1)} %get-tuple-element.16), channel_id=1, source_target_pairs={{0,16},{1,17},{2,18},{3,19},{4,20},{5,21},{6,22},{7,23},{8,24},{9,... | collective-permute-start | bytes 589832 | tf_op jit(solution)/shard_map/ppermute | solution.py:39
  6.9 2.2 %collective-permute-start.1 = (f32[384,128]{1,0:T(8,128)S(1)}, f32[384,128]{1,0:T(8,128)S(1)}, u32[]{:S(2)}, u32[]{:S(2)}) collective-permute-start(f32[384,128]{1,0:T(8,128)S(1)} %get-tuple-element.17), channel_id=1, source_target_pairs={{0,48},{1,49},{2,50},{3,51},{4,52},{5,53},{6,54},{7,55},{8,56},{9,... | collective-permute-start | bytes 589832 | tf_op jit(solution)/shard_map/ppermute | solution.py:39
  9.1 0.7 %collective-permute-start.2 = (f32[384,128]{1,0:T(8,128)S(1)}, f32[384,128]{1,0:T(8,128)S(1)}, u32[]{:S(2)}, u32[]{:S(2)}) collective-permute-start(f32[384,128]{1,0:T(8,128)S(1)} %get-tuple-element.18), channel_id=1, source_target_pairs={{0,32},{1,33},{2,34},{3,35},{4,36},{5,37},{6,38},{7,39},{8,40},{9,... | collective-permute-start | bytes 589832 | tf_op jit(solution)/shard_map/ppermute | solution.py:39
  9.8 0.0 collective-permute-done.7.came
  9.8 0.1 collective-permute-start.8
  9.9 1.3 %collective-permute-done.8.got = f32[256,128]{1,0:T(8,128)S(1)} collective-permute-done((f32[256,128]{1,0:T(8,128)S(1)}, f32[256,128]{1,0:T(8,128)S(1)}, u32[]{:S(2)}, u32[]{:S(2)}) %collective-permute-start.8) | collective-permute-done | bytes 131104 | tf_op jit(solution)/shard_map/ppermute | solution.py:39
  11.3 3.1 %collective-permute-start.11 = (f32[512,128]{1,0:T(8,128)S(1)}, f32[512,128]{1,0:T(8,128)S(1)}, u32[]{:S(2)}, u32[]{:S(2)}) collective-permute-start(f32[512,128]{1,0:T(8,128)S(1)} %group.1.g0), channel_id=1, source_target_pairs={{0,8},{1,9},{2,10},{3,11},{4,12},{5,13},{6,14},{7,15},{8,0},{9,1},... | collective-permute-start | bytes 786440 | tf_op jit(solution)/shard_map/ppermute | solution.py:39
  14.4 1.1 %collective-permute-start.10 = (f32[512,128]{1,0:T(8,128)S(1)}, f32[512,128]{1,0:T(8,128)S(1)}, u32[]{:S(2)}, u32[]{:S(2)}) collective-permute-start(f32[512,128]{1,0:T(8,128)S(1)} %group.1.g0), channel_id=1, source_target_pairs={{0,12},{1,13},{2,14},{3,15},{4,8},{5,9},{6,10},{7,11},{8,4},{9,5},... | collective-permute-start | bytes 786440 | tf_op jit(solution)/shard_map/ppermute | solution.py:39
  15.5 0.0 collective-permute-done.refs_0_
  15.5 0.0 collective-permute-start.9
  15.5 1.4 %collective-permute-done.1.refs_1_ = f32[384,128]{1,0:T(8,128)S(1)} collective-permute-done((f32[384,128]{1,0:T(8,128)S(1)}, f32[384,128]{1,0:T(8,128)S(1)}, u32[]{:S(2)}, u32[]{:S(2)}) %collective-permute-start.1) | collective-permute-done | bytes 196640 | tf_op jit(solution)/shard_map/ppermute | solution.py:39
  16.9 1.5 %collective-permute-done.2.refs_2_ = f32[384,128]{1,0:T(8,128)S(1)} collective-permute-done((f32[384,128]{1,0:T(8,128)S(1)}, f32[384,128]{1,0:T(8,128)S(1)}, u32[]{:S(2)}, u32[]{:S(2)}) %collective-permute-start.2) | collective-permute-done | bytes 196640 | tf_op jit(solution)/shard_map/ppermute | solution.py:39
  18.4 3.7 %collective-permute-start.3 = (f32[384,128]{1,0:T(8,128)S(1)}, f32[384,128]{1,0:T(8,128)S(1)}, u32[]{:S(2)}, u32[]{:S(2)}) collective-permute-start(f32[384,128]{1,0:T(8,128)S(1)} %total.1.refs_0_), channel_id=1, source_target_pairs={{0,64},{1,65},{2,66},{3,67},{4,68},{5,69},{6,70},{7,71},{8,72},{9,... | collective-permute-start | bytes 589832 | tf_op jit(solution)/shard_map/ppermute | solution.py:39
  22.1 3.7 %collective-permute-done.3.refs_1_ = f32[384,128]{1,0:T(8,128)S(1)} collective-permute-done((f32[384,128]{1,0:T(8,128)S(1)}, f32[384,128]{1,0:T(8,128)S(1)}, u32[]{:S(2)}, u32[]{:S(2)}) %collective-permute-start.3) | collective-permute-done | bytes 196640 | tf_op jit(solution)/shard_map/ppermute | solution.py:39
  25.8 0.3 collective-permute-start.6
  26.1 2.1 %collective-permute-start.5 = (f32[384,128]{1,0:T(8,128)S(1)}, f32[384,128]{1,0:T(8,128)S(1)}, u32[]{:S(2)}, u32[]{:S(2)}) collective-permute-start(f32[384,128]{1,0:T(8,128)S(1)} %shift.1.own), channel_id=1, source_target_pairs={{0,48},{1,49},{2,50},{3,51},{4,52},{5,53},{6,54},{7,55},{8,56},{9,... | collective-permute-start | bytes 589832 | tf_op jit(solution)/shard_map/ppermute | solution.py:39
  28.2 0.0 collective-permute-done.11.g2
  28.2 1.8 %collective-permute-start.4 = (f32[384,128]{1,0:T(8,128)S(1)}, f32[384,128]{1,0:T(8,128)S(1)}, u32[]{:S(2)}, u32[]{:S(2)}) collective-permute-start(f32[384,128]{1,0:T(8,128)S(1)} %shift.1.own), channel_id=1, source_target_pairs={{0,32},{1,33},{2,34},{3,35},{4,36},{5,37},{6,38},{7,39},{8,40},{9,... | collective-permute-start | bytes 589832 | tf_op jit(solution)/shard_map/ppermute | solution.py:39
  30.0 0.0 collective-permute-done.10.g3
  30.0 0.0 collective-permute-done.9.g1
  30.0 1.1 %pick.1 = (f32[64,128]{1,0:T(8,128)S(1)}, f32[64,128]{1,0:T(8,128)S(1)}, f32[128,128]{1,0:T(8,128)S(1)}, f32[64,128]{1,0:T(8,128)S(1)}, f32[64,128]{1,0:T(8,128)S(1)}) custom-call(s32[4,16]{1,0:T(4,128)} %bitcast.8, s32[4,16]{1,0:T(4,128)} %bitcast.9, f32[512,128]{1,0:T(8,128)S(1)} %group.1.g0, f32[512,128]{1,0:T(8,128)S(1)} %collective-permute-done.9.g1, ...), custom_call_target="tpu_custom_call" | custom-call | tf_op jit(solution)/shard_map/pick/pallas_call | solution.py:232
  31.1 0.1 collective-permute-start.14
  31.1 0.4 collective-permute-start.12
  31.6 0.8 %collective-permute-done.14.came = f32[64,128]{1,0:T(8,128)S(1)} collective-permute-done((f32[64,128]{1,0:T(8,128)S(1)}, f32[64,128]{1,0:T(8,128)S(1)}, u32[]{:S(2)}, u32[]{:S(2)}) %collective-permute-start.14) | collective-permute-done | bytes 32800 | tf_op jit(solution)/shard_map/ppermute | solution.py:39
  32.4 3.6 %collective-permute-start.15 = (f32[64,128]{1,0:T(8,128)S(1)}, f32[64,128]{1,0:T(8,128)S(1)}, u32[]{:S(2)}, u32[]{:S(2)}) collective-permute-start(f32[64,128]{1,0:T(8,128)S(1)} %merge.1.refs_0_), channel_id=1, source_target_pairs={{0,64},{1,65},{2,66},{3,67},{4,68},{5,69},{6,70},{7,71},{8,72},{9,... | collective-permute-start | bytes 98312 | tf_op jit(solution)/shard_map/ppermute | solution.py:39
  36.0 0.0 collective-permute-done.12.back
  36.0 2.3 %collective-permute-done.15.refs_1_ = f32[64,128]{1,0:T(8,128)S(1)} collective-permute-done((f32[64,128]{1,0:T(8,128)S(1)}, f32[64,128]{1,0:T(8,128)S(1)}, u32[]{:S(2)}, u32[]{:S(2)}) %collective-permute-start.15) | collective-permute-done | bytes 32800 | tf_op jit(solution)/shard_map/ppermute | solution.py:39
  38.3 0.1 collective-permute-start.16
  38.4 0.0 collective-permute-start.13
  38.4 3.8 %collective-permute-done.16.refs_1_ = f32[64,128]{1,0:T(8,128)S(1)} collective-permute-done((f32[64,128]{1,0:T(8,128)S(1)}, f32[64,128]{1,0:T(8,128)S(1)}, u32[]{:S(2)}, u32[]{:S(2)}) %collective-permute-start.16) | collective-permute-done | bytes 32800 | tf_op jit(solution)/shard_map/ppermute | solution.py:39
  42.2 2.2 %collective-permute-start.17 = (f32[64,128]{1,0:T(8,128)S(1)}, f32[64,128]{1,0:T(8,128)S(1)}, u32[]{:S(2)}, u32[]{:S(2)}) collective-permute-start(f32[64,128]{1,0:T(8,128)S(1)} %edge.3.edge0), channel_id=1, source_target_pairs={{0,48},{1,49},{2,50},{3,51},{4,52},{5,53},{6,54},{7,55},{8,56},{9,... | collective-permute-start | bytes 98312 | tf_op jit(solution)/shard_map/ppermute | solution.py:39
  44.4 0.0 collective-permute-done.6.a
  44.4 0.0 collective-permute-done.5.b
  44.4 0.0 collective-permute-done.4.c
  44.4 2.0 %recentre.1.fields = f32[4,12,144,128]{3,2,1,0:T(8,128)S(1)} custom-call(f32[4,12,128,128]{3,2,1,0:T(8,128)} %bitcast.6, f32[384,128]{1,0:T(8,128)S(1)} %shift.1.own, f32[384,128]{1,0:T(8,128)S(1)} %collective-permute-done.4.c, f32[384,128]{1,0:T(8,128)S(1)} %collective-permute-done.5.b, f32[384,128]{1,0:T(8,128)S(1)} %collective-permute-done.6.a), custom_call_target="tpu_custom_call" | custom-call | tf_op jit(solution)/shard_map/recentre/pallas_call | solution.py:287
  46.4 0.0 collective-permute-done.13.got
  46.4 0.9 %collective-permute-done.17.edge1 = f32[64,128]{1,0:T(8,128)S(1)} collective-permute-done((f32[64,128]{1,0:T(8,128)S(1)}, f32[64,128]{1,0:T(8,128)S(1)}, u32[]{:S(2)}, u32[]{:S(2)}) %collective-permute-start.17) | collective-permute-done | bytes 32800 | tf_op jit(solution)/shard_map/ppermute | solution.py:39
  47.3 5.2 %advance.1 = f32[4,12,128,128]{3,2,1,0:T(8,128)} custom-call(f32[4,12,144,128]{3,2,1,0:T(8,128)S(1)} %recentre.1.fields, f32[64,128]{1,0:T(8,128)S(1)} %get-tuple-element.22.stay, f32[128,128]{1,0:T(8,128)S(1)} %collective-permute-done.12.back, f32[128,128]{1,0:T(8,128)S(1)} %collective-permute-done.13.got, f32[64,128]{1,0:T(8,128)S(1)} %edge.3.edge0, ...), custom_call_target="tpu_custom_call" | custom-call | flops 40000000 | bytes 8000000 | tf_op jit(solution)/shard_map/advance/pallas_call | solution.py:382
  (8 shorter events, 0.1 us)
Async XLA Ops:
  3.2 6.6 %collective-permute-start.7 = (f32[256,128]{1,0:T(8,128)S(1)}, f32[256,128]{1,0:T(8,128)S(1)}, u32[]{:S(2)}, u32[]{:S(2)}) collective-permute-start(f32[256,128]{1,0:T(8,128)S(1)} %get-tuple-element.21), channel_id=1, source_target_pairs={{0,2},{1,3},{2,0},{3,1},{4,6},{5,7},{6,4},{7,5},{8,10},{9,11},{10,... | collective-permute-start | bytes 393224 | tf_op jit(solution)/shard_map/ppermute | solution.py:39
  5.3 10.2 %collective-permute-start = (f32[384,128]{1,0:T(8,128)S(1)}, f32[384,128]{1,0:T(8,128)S(1)}, u32[]{:S(2)}, u32[]{:S(2)}) collective-permute-start(f32[384,128]{1,0:T(8,128)S(1)} %get-tuple-element.16), channel_id=1, source_target_pairs={{0,16},{1,17},{2,18},{3,19},{4,20},{5,21},{6,22},{7,23},{8,24},{9,... | collective-permute-start | bytes 589832 | tf_op jit(solution)/shard_map/ppermute | solution.py:39
  6.9 10.0 %collective-permute-start.1 = (f32[384,128]{1,0:T(8,128)S(1)}, f32[384,128]{1,0:T(8,128)S(1)}, u32[]{:S(2)}, u32[]{:S(2)}) collective-permute-start(f32[384,128]{1,0:T(8,128)S(1)} %get-tuple-element.17), channel_id=1, source_target_pairs={{0,48},{1,49},{2,50},{3,51},{4,52},{5,53},{6,54},{7,55},{8,56},{9,... | collective-permute-start | bytes 589832 | tf_op jit(solution)/shard_map/ppermute | solution.py:39
  9.1 9.3 %collective-permute-start.2 = (f32[384,128]{1,0:T(8,128)S(1)}, f32[384,128]{1,0:T(8,128)S(1)}, u32[]{:S(2)}, u32[]{:S(2)}) collective-permute-start(f32[384,128]{1,0:T(8,128)S(1)} %get-tuple-element.18), channel_id=1, source_target_pairs={{0,32},{1,33},{2,34},{3,35},{4,36},{5,37},{6,38},{7,39},{8,40},{9,... | collective-permute-start | bytes 589832 | tf_op jit(solution)/shard_map/ppermute | solution.py:39
  9.8 1.4 %collective-permute-start.8 = (f32[256,128]{1,0:T(8,128)S(1)}, f32[256,128]{1,0:T(8,128)S(1)}, u32[]{:S(2)}, u32[]{:S(2)}) collective-permute-start(f32[256,128]{1,0:T(8,128)S(1)} %split.1), channel_id=1, source_target_pairs={{0,1},{1,0},{2,3},{3,2},{4,5},{5,4},{6,7},{7,6},{8,9},{9,8},{10,11... | collective-permute-start | bytes 393224 | tf_op jit(solution)/shard_map/ppermute | solution.py:39
  11.3 16.9 %collective-permute-start.11 = (f32[512,128]{1,0:T(8,128)S(1)}, f32[512,128]{1,0:T(8,128)S(1)}, u32[]{:S(2)}, u32[]{:S(2)}) collective-permute-start(f32[512,128]{1,0:T(8,128)S(1)} %group.1.g0), channel_id=1, source_target_pairs={{0,8},{1,9},{2,10},{3,11},{4,12},{5,13},{6,14},{7,15},{8,0},{9,1},... | collective-permute-start | bytes 786440 | tf_op jit(solution)/shard_map/ppermute | solution.py:39
  14.4 15.6 %collective-permute-start.10 = (f32[512,128]{1,0:T(8,128)S(1)}, f32[512,128]{1,0:T(8,128)S(1)}, u32[]{:S(2)}, u32[]{:S(2)}) collective-permute-start(f32[512,128]{1,0:T(8,128)S(1)} %group.1.g0), channel_id=1, source_target_pairs={{0,12},{1,13},{2,14},{3,15},{4,8},{5,9},{6,10},{7,11},{8,4},{9,5},... | collective-permute-start | bytes 786440 | tf_op jit(solution)/shard_map/ppermute | solution.py:39
  15.5 14.5 %collective-permute-start.9 = (f32[512,128]{1,0:T(8,128)S(1)}, f32[512,128]{1,0:T(8,128)S(1)}, u32[]{:S(2)}, u32[]{:S(2)}) collective-permute-start(f32[512,128]{1,0:T(8,128)S(1)} %group.1.g0), channel_id=1, source_target_pairs={{0,4},{1,5},{2,6},{3,7},{4,0},{5,1},{6,2},{7,3},{8,12},{9,13},{10,... | collective-permute-start | bytes 786440 | tf_op jit(solution)/shard_map/ppermute | solution.py:39
  18.4 7.3 %collective-permute-start.3 = (f32[384,128]{1,0:T(8,128)S(1)}, f32[384,128]{1,0:T(8,128)S(1)}, u32[]{:S(2)}, u32[]{:S(2)}) collective-permute-start(f32[384,128]{1,0:T(8,128)S(1)} %total.1.refs_0_), channel_id=1, source_target_pairs={{0,64},{1,65},{2,66},{3,67},{4,68},{5,69},{6,70},{7,71},{8,72},{9,... | collective-permute-start | bytes 589832 | tf_op jit(solution)/shard_map/ppermute | solution.py:39
  25.8 18.6 %collective-permute-start.6 = (f32[384,128]{1,0:T(8,128)S(1)}, f32[384,128]{1,0:T(8,128)S(1)}, u32[]{:S(2)}, u32[]{:S(2)}) collective-permute-start(f32[384,128]{1,0:T(8,128)S(1)} %shift.1.own), channel_id=1, source_target_pairs={{0,16},{1,17},{2,18},{3,19},{4,20},{5,21},{6,22},{7,23},{8,24},{9,... | collective-permute-start | bytes 589832 | tf_op jit(solution)/shard_map/ppermute | solution.py:39
  26.1 18.3 %collective-permute-start.5 = (f32[384,128]{1,0:T(8,128)S(1)}, f32[384,128]{1,0:T(8,128)S(1)}, u32[]{:S(2)}, u32[]{:S(2)}) collective-permute-start(f32[384,128]{1,0:T(8,128)S(1)} %shift.1.own), channel_id=1, source_target_pairs={{0,48},{1,49},{2,50},{3,51},{4,52},{5,53},{6,54},{7,55},{8,56},{9,... | collective-permute-start | bytes 589832 | tf_op jit(solution)/shard_map/ppermute | solution.py:39
  28.2 16.2 %collective-permute-start.4 = (f32[384,128]{1,0:T(8,128)S(1)}, f32[384,128]{1,0:T(8,128)S(1)}, u32[]{:S(2)}, u32[]{:S(2)}) collective-permute-start(f32[384,128]{1,0:T(8,128)S(1)} %shift.1.own), channel_id=1, source_target_pairs={{0,32},{1,33},{2,34},{3,35},{4,36},{5,37},{6,38},{7,39},{8,40},{9,... | collective-permute-start | bytes 589832 | tf_op jit(solution)/shard_map/ppermute | solution.py:39
  31.1 1.3 %collective-permute-start.14 = (f32[64,128]{1,0:T(8,128)S(1)}, f32[64,128]{1,0:T(8,128)S(1)}, u32[]{:S(2)}, u32[]{:S(2)}) collective-permute-start(f32[64,128]{1,0:T(8,128)S(1)} %get-tuple-element.26), channel_id=1, source_target_pairs={{0,1},{1,0},{2,3},{3,2},{4,5},{5,4},{6,7},{7,6},{8,9},{9,8},{10,11... | collective-permute-start | bytes 98312 | tf_op jit(solution)/shard_map/ppermute | solution.py:39
  31.1 4.8 %collective-permute-start.12 = (f32[128,128]{1,0:T(8,128)S(1)}, f32[128,128]{1,0:T(8,128)S(1)}, u32[]{:S(2)}, u32[]{:S(2)}) collective-permute-start(f32[128,128]{1,0:T(8,128)S(1)} %get-tuple-element.23), channel_id=1, source_target_pairs={{0,2},{1,3},{2,0},{3,1},{4,6},{5,7},{6,4},{7,5},{8,10},{9,11},{10,... | collective-permute-start | bytes 196616 | tf_op jit(solution)/shard_map/ppermute | solution.py:39
  32.4 5.9 %collective-permute-start.15 = (f32[64,128]{1,0:T(8,128)S(1)}, f32[64,128]{1,0:T(8,128)S(1)}, u32[]{:S(2)}, u32[]{:S(2)}) collective-permute-start(f32[64,128]{1,0:T(8,128)S(1)} %merge.1.refs_0_), channel_id=1, source_target_pairs={{0,64},{1,65},{2,66},{3,67},{4,68},{5,69},{6,70},{7,71},{8,72},{9,... | collective-permute-start | bytes 98312 | tf_op jit(solution)/shard_map/ppermute | solution.py:39
  38.3 3.9 %collective-permute-start.16 = (f32[64,128]{1,0:T(8,128)S(1)}, f32[64,128]{1,0:T(8,128)S(1)}, u32[]{:S(2)}, u32[]{:S(2)}) collective-permute-start(f32[64,128]{1,0:T(8,128)S(1)} %edge.2.refs_0_), channel_id=1, source_target_pairs={{0,16},{1,17},{2,18},{3,19},{4,20},{5,21},{6,22},{7,23},{8,24},{9,... | collective-permute-start | bytes 98312 | tf_op jit(solution)/shard_map/ppermute | solution.py:39
  38.4 8.0 %collective-permute-start.13 = (f32[128,128]{1,0:T(8,128)S(1)}, f32[128,128]{1,0:T(8,128)S(1)}, u32[]{:S(2)}, u32[]{:S(2)}) collective-permute-start(f32[128,128]{1,0:T(8,128)S(1)} %couple.1), channel_id=1, source_target_pairs={{0,1},{1,0},{2,3},{3,2},{4,5},{5,4},{6,7},{7,6},{8,9},{9,8},{10,11... | collective-permute-start | bytes 196616 | tf_op jit(solution)/shard_map/ppermute | solution.py:39
  42.2 5.1 %collective-permute-start.17 = (f32[64,128]{1,0:T(8,128)S(1)}, f32[64,128]{1,0:T(8,128)S(1)}, u32[]{:S(2)}, u32[]{:S(2)}) collective-permute-start(f32[64,128]{1,0:T(8,128)S(1)} %edge.3.edge0), channel_id=1, source_target_pairs={{0,48},{1,49},{2,50},{3,51},{4,52},{5,53},{6,54},{7,55},{8,56},{9,... | collective-permute-start | bytes 98312 | tf_op jit(solution)/shard_map/ppermute | solution.py:39

commit v6 on v5

--- a/solution.py
+++ b/solution.py
@@ -265,7 +265,7 @@
     return ahead - behind
 
 
-def recentre_kernel(ens_hbm, own, c, b, a, out, ens, shift, sems):
+def recentre_kernel(ens_hbm, own, c, b, a, out, slopes, ens, shift, sems):
     copies = [pltpu.make_async_copy(ens_hbm.at[n], ens.at[n], sems.at[n]) for n in range(LOCAL)]
     for copy in copies:
         copy.start()
@@ -280,15 +280,20 @@
             out[n, i, 0:8, :] = jnp.zeros((8, SIZE), F32)
             out[n, i, 8 + SIZE :, :] = jnp.zeros((8, SIZE), F32)
             for r in range(0, SIZE, 32):
-                out[n, i, 8 + r : 40 + r, :] = ens[n, i, r : r + 32, :] + shift[i * SIZE + r : i * SIZE + r + 32, :]
+                value = ens[n, i, r : r + 32, :] + shift[i * SIZE + r : i * SIZE + r + 32, :]
+                out[n, i, 8 + r : 40 + r, :] = value
+                slopes[n, i, r : r + 32, :] = slope(value)
 
 
 def recentre(ensemble, arrays):
     return pl.pallas_call(
         recentre_kernel,
-        out_shape=pltpu.VMEM((LOCAL, PLANES, SIZE + 16, SIZE), F32),
+        out_shape=[
+            pltpu.VMEM((LOCAL, PLANES, SIZE + 16, SIZE), F32),
+            pltpu.VMEM((LOCAL, PLANES, SIZE, SIZE), F32),
+        ],
         in_specs=[hbm()] + [vmem()] * len(arrays),
-        out_specs=vmem(),
+        out_specs=[vmem()] * 2,
         scratch_shapes=[
             pltpu.VMEM((LOCAL, PLANES, SIZE, SIZE), F32),
             pltpu.VMEM((ROWS, SIZE), F32),
@@ -299,7 +304,7 @@
     )(*on(pltpu.HBM, ensemble), *on(pltpu.VMEM, *arrays))
 
 
-def advance_kernel(fields, stay, back, got, edge0, edge1, out, rims, lines, columns, div, slope_u):
+def advance_kernel(fields, slopes, stay, back, got, edge0, edge1, out, rims, lines, columns, div):
     now_at = pl.program_id(0)
 
     @pl.when(now_at == 0)
@@ -319,7 +324,7 @@
         for n in range(LOCAL):
             at = n * 32
             lines[pl.ds(at, PLANES, stride=2), :] = rims[n, 3, 0:PLANES, :]
-            lines[pl.ds(at + 1, PLANES, stride=2), :] = rims[n, 2, 0:PLANES, :]
+            lines[pl.ds(at + 1, PLANES, stride=2), :] = -rims[n, 2, 0:PLANES, :]
             right = 0.5 * (rims[n, 3, PLANES:USED, :] + slope(rims[n, 3, LEV : 2 * LEV, :]))
             left = 0.5 * (slope(rims[n, 2, LEV : 2 * LEV, :]) - rims[n, 2, PLANES:USED, :])
             lines[pl.ds(at + 24, LEV, stride=2), :] = right
@@ -345,9 +350,11 @@
         value = fields[step, i, 9 + r : 9 + r + part, :]
         return jnp.where(row == part - 1, rims[step, 1, i : i + 1, :], value) if r == SIZE - part else value
 
-    def across(x, r, line):
-        edge = pltpu.roll(columns[step, r : r + part, :], (SIZE - 1 - 2 * line) % SIZE, 1)
-        return jnp.where(at_right, edge, pltpu.roll(x, SIZE - 1, 1)) - jnp.where(at_left, edge, pltpu.roll(x, 1, 1))
+    at_end = jnp.logical_or(at_left, at_right)
+
+    def across(i, r):
+        edge = pltpu.roll(columns[step, r : r + part, :], (SIZE - 1 - 2 * i) % SIZE, 1)
+        return slopes[step, i, r : r + part, :] + jnp.where(at_end, edge, 0.0)
 
     for lev in range(LEV):
         iu, iv, iw, deep = lev, LEV + lev, 2 * LEV + lev, PLANES + lev
@@ -360,9 +367,7 @@
             - fields[step, iv, 7 + SIZE : 8 + SIZE, :]
         )
         for r in range(0, SIZE, part):
-            du = across(rows_at(iu, r), r, iu)
-            slope_u[r : r + part, :] = du
-            div[8 + r : 8 + r + part, :] = 0.5 * (du + below(iv, r) - above(iv, r))
+            div[8 + r : 8 + r + part, :] = 0.5 * (across(iu, r) + below(iv, r) - above(iv, r))
         for r in range(0, SIZE, part):
             u, v, w = rows_at(iu, r), rows_at(iv, r), rows_at(iw, r)
             edge = pltpu.roll(columns[step, r : r + part, :], (SIZE - 1 - 2 * deep) % SIZE, 1)
@@ -370,9 +375,9 @@
             mid = div[8 + r : 8 + r + part, :]
             grad_x = jnp.where(at_right, edge, pltpu.roll(mid, SIZE - 1, 1)) - jnp.where(at_left, edge, pltpu.roll(mid, 1, 1))
             grad_y = div[9 + r : 9 + r + part, :] - div[7 + r : 7 + r + part, :]
-            new_u = u - 0.2 * (u * slope_u[r : r + part, :] + v * (below(iu, r) - above(iu, r)))
-            new_v = v - 0.2 * (u * across(v, r, iv) + v * (below(iv, r) - above(iv, r)))
-            new_w = w - 0.2 * (u * across(w, r, iw) + v * (below(iw, r) - above(iw, r)))
+            new_u = u - 0.2 * (u * across(iu, r) + v * (below(iu, r) - above(iu, r)))
+            new_v = v - 0.2 * (u * across(iv, r) + v * (below(iv, r) - above(iv, r)))
+            new_w = w - 0.2 * (u * across(iw, r) + v * (below(iw, r) - above(iw, r)))
             out[0, iu, r : r + part, :] = new_u + 0.1 * grad_x
             out[0, iv, r : r + part, :] = new_v + 0.1 * grad_y
             out[0, iw, r : r + part, :] = new_w
@@ -390,7 +395,6 @@
             pltpu.VMEM((SIZE, SIZE), F32),
             pltpu.VMEM((LOCAL, SIZE, SIZE), F32),
             pltpu.VMEM((SIZE + 16, SIZE), F32),
-            pltpu.VMEM((SIZE, SIZE), F32),
         ],
         compiler_params=limit(8),
         cost_estimate=pl.CostEstimate(flops=40_000_000, bytes_accessed=8_000_000, transcendentals=0),
@@ -418,8 +422,8 @@
     edge = small(sum_kernel, "edge", STRIP, [edge, over_z_hi(edge)])
     edge = small(sum_kernel, "edge", STRIP, [edge, send(edge, lambda m, d: (m ^ 1, d))])
     other = send(edge, lambda m, d: (m ^ 3, d))
-    fields = recentre(ensemble, [total, *chunks[::-1]])
-    out = advance(fields, stay, back, got, edge, other)
+    fields, slopes = recentre(ensemble, [total, *chunks[::-1]])
+    out = advance(fields, slopes, stay, back, got, edge, other)
     return out.reshape(shape)
 
 

time: 52.7 us -> 51.9 us (0.985)
  waiting for transfers between devices: 15.7 us -> 14.8 us
    pallas_call x1, Pallas kernels: 1.97 us -> 3.08 us  [recentre(): pl.pallas_call(recentre_kernel, out_shape=[pltpu.VMEM((LOCAL, PLANES, SIZ...]
    ppermute x18, waiting for transfers between devices: 15.7 us -> 14.8 us  [send(): return lax.ppermute(array, MESH, pairs(target))]
    pallas_call x1, Pallas kernels: 5.21 us -> 4.34 us  [advance(): pl.pallas_call(advance_kernel, out_shape=jax.ShapeDtypeStruct((LOCAL, PLA...]
  transfers between devices with their start and end apart: 18 -> 18, of which waited for: 8 -> 7; matrix products, arithmetic and copies ran while one was open for 0% -> 0% of each run, Pallas kernels for 6% -> 8%
where the time goes in v6:
time: 51.9 us; the launch traced here: 51.8 us
  starting transfers between devices  25.1 us (48%)
  waiting for transfers between devices  14.8 us (29%)
  Pallas kernels  11.8 us (23%)
    ppermute x18, starting transfers between devices, send(): return lax.ppermute(array, MESH, pairs(target))  25.1 us
    ppermute x18, waiting for transfers between devices, send(): return lax.ppermute(array, MESH, pairs(target))  14.8 us
    pallas_call x1, Pallas kernels, advance(): pl.pallas_call(advance_kernel, out_shape=jax.ShapeDtypeStruct((LOCAL, PLA...  4.34 us
    pallas_call x1, Pallas kernels, prepare(): pl.pallas_call(prepare_kernel, out_shape=shaped(*[2 * CHUNK] * 4, 2 * REC...  3.22 us
    pallas_call x1, Pallas kernels, recentre(): pl.pallas_call(recentre_kernel, out_shape=[pltpu.VMEM((LOCAL, PLANES, SIZ...  3.08 us
    pallas_call x1, Pallas kernels, pick(): pl.pallas_call(pick_kernel, out_shape=shaped(STRIP, STRIP, 2 * STRIP, STR...  1.08 us
  transfers between devices with their start and end apart: 18, of which 7 were waited for; matrix products, arithmetic and copies ran while one was open for 0% of the time, Pallas kernels for 8%

profile of v6, /device:TPU:0, one launch (start us, length us, event | category | flops | bytes accessed | tf_op | source)
XLA Modules:
  0.0 51.8 jit_solution(1919552024877368175)
XLA Ops:
  0.0 3.2 %prepare.1 = (f32[384,128]{1,0:T(8,128)S(1)}, f32[384,128]{1,0:T(8,128)S(1)}, f32[384,128]{1,0:T(8,128)S(1)}, f32[384,128]{1,0:T(8,128)S(1)}, f32[256,128]{1,0:T(8,128)S(1)}, /*index=5*/f32[256,128]{1,0:T(8,128)S(1)}) custom-call(s32[16]{0:T(128)} %owner_hbm.1, f32[4,12,128,128]{3,2,1,0:T(8,128)} %bitcast.5, f32[12,128,128]{2,1,0:T(8,128)} %bitcast.7), custom_call_target="tpu_custom_call" | custom-call | flops 2000000 | bytes 5000000 | tf_op jit(solution)/shard_map/prepare/pallas_call | solution.py:143
  3.2 2.1 %collective-permute-start.7 = (f32[256,128]{1,0:T(8,128)S(1)}, f32[256,128]{1,0:T(8,128)S(1)}, u32[]{:S(2)}, u32[]{:S(2)}) collective-permute-start(f32[256,128]{1,0:T(8,128)S(1)} %get-tuple-element.25), channel_id=1, source_target_pairs={{0,2},{1,3},{2,0},{3,1},{4,6},{5,7},{6,4},{7,5},{8,10},{9,11},{10,... | collective-permute-start | bytes 393224 | tf_op jit(solution)/shard_map/ppermute | solution.py:39
  5.3 1.6 %collective-permute-start = (f32[384,128]{1,0:T(8,128)S(1)}, f32[384,128]{1,0:T(8,128)S(1)}, u32[]{:S(2)}, u32[]{:S(2)}) collective-permute-start(f32[384,128]{1,0:T(8,128)S(1)} %get-tuple-element.18), channel_id=1, source_target_pairs={{0,16},{1,17},{2,18},{3,19},{4,20},{5,21},{6,22},{7,23},{8,24},{9,... | collective-permute-start | bytes 589832 | tf_op jit(solution)/shard_map/ppermute | solution.py:39
  6.9 2.2 %collective-permute-start.1 = (f32[384,128]{1,0:T(8,128)S(1)}, f32[384,128]{1,0:T(8,128)S(1)}, u32[]{:S(2)}, u32[]{:S(2)}) collective-permute-start(f32[384,128]{1,0:T(8,128)S(1)} %get-tuple-element.19), channel_id=1, source_target_pairs={{0,48},{1,49},{2,50},{3,51},{4,52},{5,53},{6,54},{7,55},{8,56},{9,... | collective-permute-start | bytes 589832 | tf_op jit(solution)/shard_map/ppermute | solution.py:39
  9.1 0.7 %collective-permute-start.2 = (f32[384,128]{1,0:T(8,128)S(1)}, f32[384,128]{1,0:T(8,128)S(1)}, u32[]{:S(2)}, u32[]{:S(2)}) collective-permute-start(f32[384,128]{1,0:T(8,128)S(1)} %get-tuple-element.20), channel_id=1, source_target_pairs={{0,32},{1,33},{2,34},{3,35},{4,36},{5,37},{6,38},{7,39},{8,40},{9,... | collective-permute-start | bytes 589832 | tf_op jit(solution)/shard_map/ppermute | solution.py:39
  9.8 0.0 collective-permute-done.7.came
  9.8 0.1 collective-permute-start.8
  9.9 1.3 %collective-permute-done.8.got = f32[256,128]{1,0:T(8,128)S(1)} collective-permute-done((f32[256,128]{1,0:T(8,128)S(1)}, f32[256,128]{1,0:T(8,128)S(1)}, u32[]{:S(2)}, u32[]{:S(2)}) %collective-permute-start.8) | collective-permute-done | bytes 131104 | tf_op jit(solution)/shard_map/ppermute | solution.py:39
  11.3 3.1 %collective-permute-start.11 = (f32[512,128]{1,0:T(8,128)S(1)}, f32[512,128]{1,0:T(8,128)S(1)}, u32[]{:S(2)}, u32[]{:S(2)}) collective-permute-start(f32[512,128]{1,0:T(8,128)S(1)} %group.1.g0), channel_id=1, source_target_pairs={{0,8},{1,9},{2,10},{3,11},{4,12},{5,13},{6,14},{7,15},{8,0},{9,1},... | collective-permute-start | bytes 786440 | tf_op jit(solution)/shard_map/ppermute | solution.py:39
  14.4 1.1 %collective-permute-start.10 = (f32[512,128]{1,0:T(8,128)S(1)}, f32[512,128]{1,0:T(8,128)S(1)}, u32[]{:S(2)}, u32[]{:S(2)}) collective-permute-start(f32[512,128]{1,0:T(8,128)S(1)} %group.1.g0), channel_id=1, source_target_pairs={{0,12},{1,13},{2,14},{3,15},{4,8},{5,9},{6,10},{7,11},{8,4},{9,5},... | collective-permute-start | bytes 786440 | tf_op jit(solution)/shard_map/ppermute | solution.py:39
  15.5 0.0 collective-permute-done.refs_0_
  15.5 0.0 collective-permute-start.9
  15.5 1.4 %collective-permute-done.1.refs_1_ = f32[384,128]{1,0:T(8,128)S(1)} collective-permute-done((f32[384,128]{1,0:T(8,128)S(1)}, f32[384,128]{1,0:T(8,128)S(1)}, u32[]{:S(2)}, u32[]{:S(2)}) %collective-permute-start.1) | collective-permute-done | bytes 196640 | tf_op jit(solution)/shard_map/ppermute | solution.py:39
  16.9 1.5 %collective-permute-done.2.refs_2_ = f32[384,128]{1,0:T(8,128)S(1)} collective-permute-done((f32[384,128]{1,0:T(8,128)S(1)}, f32[384,128]{1,0:T(8,128)S(1)}, u32[]{:S(2)}, u32[]{:S(2)}) %collective-permute-start.2) | collective-permute-done | bytes 196640 | tf_op jit(solution)/shard_map/ppermute | solution.py:39
  18.4 3.7 %collective-permute-start.3 = (f32[384,128]{1,0:T(8,128)S(1)}, f32[384,128]{1,0:T(8,128)S(1)}, u32[]{:S(2)}, u32[]{:S(2)}) collective-permute-start(f32[384,128]{1,0:T(8,128)S(1)} %total.1.refs_0_), channel_id=1, source_target_pairs={{0,64},{1,65},{2,66},{3,67},{4,68},{5,69},{6,70},{7,71},{8,72},{9,... | collective-permute-start | bytes 589832 | tf_op jit(solution)/shard_map/ppermute | solution.py:39
  22.1 3.7 %collective-permute-done.3.refs_1_ = f32[384,128]{1,0:T(8,128)S(1)} collective-permute-done((f32[384,128]{1,0:T(8,128)S(1)}, f32[384,128]{1,0:T(8,128)S(1)}, u32[]{:S(2)}, u32[]{:S(2)}) %collective-permute-start.3) | collective-permute-done | bytes 196640 | tf_op jit(solution)/shard_map/ppermute | solution.py:39
  25.8 0.3 collective-permute-start.6
  26.1 2.1 %collective-permute-start.5 = (f32[384,128]{1,0:T(8,128)S(1)}, f32[384,128]{1,0:T(8,128)S(1)}, u32[]{:S(2)}, u32[]{:S(2)}) collective-permute-start(f32[384,128]{1,0:T(8,128)S(1)} %shift.1.own), channel_id=1, source_target_pairs={{0,48},{1,49},{2,50},{3,51},{4,52},{5,53},{6,54},{7,55},{8,56},{9,... | collective-permute-start | bytes 589832 | tf_op jit(solution)/shard_map/ppermute | solution.py:39
  28.2 0.0 collective-permute-done.11.g2
  28.2 1.8 %collective-permute-start.4 = (f32[384,128]{1,0:T(8,128)S(1)}, f32[384,128]{1,0:T(8,128)S(1)}, u32[]{:S(2)}, u32[]{:S(2)}) collective-permute-start(f32[384,128]{1,0:T(8,128)S(1)} %shift.1.own), channel_id=1, source_target_pairs={{0,32},{1,33},{2,34},{3,35},{4,36},{5,37},{6,38},{7,39},{8,40},{9,... | collective-permute-start | bytes 589832 | tf_op jit(solution)/shard_map/ppermute | solution.py:39
  30.0 0.0 collective-permute-done.10.g3
  30.0 0.0 collective-permute-done.9.g1
  30.0 1.1 %pick.1 = (f32[64,128]{1,0:T(8,128)S(1)}, f32[64,128]{1,0:T(8,128)S(1)}, f32[128,128]{1,0:T(8,128)S(1)}, f32[64,128]{1,0:T(8,128)S(1)}, f32[64,128]{1,0:T(8,128)S(1)}) custom-call(s32[4,16]{1,0:T(4,128)} %bitcast.8, s32[4,16]{1,0:T(4,128)} %bitcast.9, f32[512,128]{1,0:T(8,128)S(1)} %group.1.g0, f32[512,128]{1,0:T(8,128)S(1)} %collective-permute-done.9.g1, ...), custom_call_target="tpu_custom_call" | custom-call | tf_op jit(solution)/shard_map/pick/pallas_call | solution.py:232
  31.1 0.1 collective-permute-start.14
  31.1 0.4 collective-permute-start.12
  31.6 0.8 %collective-permute-done.14.came = f32[64,128]{1,0:T(8,128)S(1)} collective-permute-done((f32[64,128]{1,0:T(8,128)S(1)}, f32[64,128]{1,0:T(8,128)S(1)}, u32[]{:S(2)}, u32[]{:S(2)}) %collective-permute-start.14) | collective-permute-done | bytes 32800 | tf_op jit(solution)/shard_map/ppermute | solution.py:39
  32.4 3.6 %collective-permute-start.15 = (f32[64,128]{1,0:T(8,128)S(1)}, f32[64,128]{1,0:T(8,128)S(1)}, u32[]{:S(2)}, u32[]{:S(2)}) collective-permute-start(f32[64,128]{1,0:T(8,128)S(1)} %merge.1.refs_0_), channel_id=1, source_target_pairs={{0,64},{1,65},{2,66},{3,67},{4,68},{5,69},{6,70},{7,71},{8,72},{9,... | collective-permute-start | bytes 98312 | tf_op jit(solution)/shard_map/ppermute | solution.py:39
  36.0 0.0 collective-permute-done.12.back
  36.0 2.3 %collective-permute-done.15.refs_1_ = f32[64,128]{1,0:T(8,128)S(1)} collective-permute-done((f32[64,128]{1,0:T(8,128)S(1)}, f32[64,128]{1,0:T(8,128)S(1)}, u32[]{:S(2)}, u32[]{:S(2)}) %collective-permute-start.15) | collective-permute-done | bytes 32800 | tf_op jit(solution)/shard_map/ppermute | solution.py:39
  38.3 0.1 collective-permute-start.16
  38.4 0.0 collective-permute-start.13
  38.4 3.8 %collective-permute-done.16.refs_1_ = f32[64,128]{1,0:T(8,128)S(1)} collective-permute-done((f32[64,128]{1,0:T(8,128)S(1)}, f32[64,128]{1,0:T(8,128)S(1)}, u32[]{:S(2)}, u32[]{:S(2)}) %collective-permute-start.16) | collective-permute-done | bytes 32800 | tf_op jit(solution)/shard_map/ppermute | solution.py:39
  42.2 2.2 %collective-permute-start.17 = (f32[64,128]{1,0:T(8,128)S(1)}, f32[64,128]{1,0:T(8,128)S(1)}, u32[]{:S(2)}, u32[]{:S(2)}) collective-permute-start(f32[64,128]{1,0:T(8,128)S(1)} %edge.3.edge0), channel_id=1, source_target_pairs={{0,48},{1,49},{2,50},{3,51},{4,52},{5,53},{6,54},{7,55},{8,56},{9,... | collective-permute-start | bytes 98312 | tf_op jit(solution)/shard_map/ppermute | solution.py:39
  44.4 0.0 collective-permute-done.6.a
  44.4 0.0 collective-permute-done.5.b
  44.4 0.0 collective-permute-done.4.c
  44.4 3.1 %recentre.1 = (f32[4,12,144,128]{3,2,1,0:T(8,128)S(1)}, f32[4,12,128,128]{3,2,1,0:T(8,128)S(1)}) custom-call(f32[4,12,128,128]{3,2,1,0:T(8,128)} %bitcast.6, f32[384,128]{1,0:T(8,128)S(1)} %shift.1.own, f32[384,128]{1,0:T(8,128)S(1)} %collective-permute-done.4.c, f32[384,128]{1,0:T(8,128)S(1)} %collective-permute-done.5.b, ...), custom_call_target="tpu_custom_call" | custom-call | tf_op jit(solution)/shard_map/recentre/pallas_call | solution.py:289
  47.5 0.0 collective-permute-done.13.got
  47.5 0.0 collective-permute-done.17.edge1
  47.5 4.3 %advance.1 = f32[4,12,128,128]{3,2,1,0:T(8,128)} custom-call(f32[4,12,144,128]{3,2,1,0:T(8,128)S(1)} %get-tuple-element.22.fields, f32[4,12,128,128]{3,2,1,0:T(8,128)S(1)} %get-tuple-element.23.slopes, f32[64,128]{1,0:T(8,128)S(1)} %get-tuple-element.26.stay, f32[128,128]{1,0:T(8,128)S(1)} %collective-permute-done.12.back, ...), custom_call_target="tpu_custom_call" | custom-call | flops 40000000 | bytes 8000000 | tf_op jit(solution)/shard_map/advance/pallas_call | solution.py:387
  (8 shorter events, 0.1 us)
Async XLA Ops:
  3.2 6.6 %collective-permute-start.7 = (f32[256,128]{1,0:T(8,128)S(1)}, f32[256,128]{1,0:T(8,128)S(1)}, u32[]{:S(2)}, u32[]{:S(2)}) collective-permute-start(f32[256,128]{1,0:T(8,128)S(1)} %get-tuple-element.25), channel_id=1, source_target_pairs={{0,2},{1,3},{2,0},{3,1},{4,6},{5,7},{6,4},{7,5},{8,10},{9,11},{10,... | collective-permute-start | bytes 393224 | tf_op jit(solution)/shard_map/ppermute | solution.py:39
  5.3 10.2 %collective-permute-start = (f32[384,128]{1,0:T(8,128)S(1)}, f32[384,128]{1,0:T(8,128)S(1)}, u32[]{:S(2)}, u32[]{:S(2)}) collective-permute-start(f32[384,128]{1,0:T(8,128)S(1)} %get-tuple-element.18), channel_id=1, source_target_pairs={{0,16},{1,17},{2,18},{3,19},{4,20},{5,21},{6,22},{7,23},{8,24},{9,... | collective-permute-start | bytes 589832 | tf_op jit(solution)/shard_map/ppermute | solution.py:39
  6.9 10.0 %collective-permute-start.1 = (f32[384,128]{1,0:T(8,128)S(1)}, f32[384,128]{1,0:T(8,128)S(1)}, u32[]{:S(2)}, u32[]{:S(2)}) collective-permute-start(f32[384,128]{1,0:T(8,128)S(1)} %get-tuple-element.19), channel_id=1, source_target_pairs={{0,48},{1,49},{2,50},{3,51},{4,52},{5,53},{6,54},{7,55},{8,56},{9,... | collective-permute-start | bytes 589832 | tf_op jit(solution)/shard_map/ppermute | solution.py:39
  9.1 9.3 %collective-permute-start.2 = (f32[384,128]{1,0:T(8,128)S(1)}, f32[384,128]{1,0:T(8,128)S(1)}, u32[]{:S(2)}, u32[]{:S(2)}) collective-permute-start(f32[384,128]{1,0:T(8,128)S(1)} %get-tuple-element.20), channel_id=1, source_target_pairs={{0,32},{1,33},{2,34},{3,35},{4,36},{5,37},{6,38},{7,39},{8,40},{9,... | collective-permute-start | bytes 589832 | tf_op jit(solution)/shard_map/ppermute | solution.py:39
  9.8 1.4 %collective-permute-start.8 = (f32[256,128]{1,0:T(8,128)S(1)}, f32[256,128]{1,0:T(8,128)S(1)}, u32[]{:S(2)}, u32[]{:S(2)}) collective-permute-start(f32[256,128]{1,0:T(8,128)S(1)} %split.1), channel_id=1, source_target_pairs={{0,1},{1,0},{2,3},{3,2},{4,5},{5,4},{6,7},{7,6},{8,9},{9,8},{10,11... | collective-permute-start | bytes 393224 | tf_op jit(solution)/shard_map/ppermute | solution.py:39
  11.3 16.9 %collective-permute-start.11 = (f32[512,128]{1,0:T(8,128)S(1)}, f32[512,128]{1,0:T(8,128)S(1)}, u32[]{:S(2)}, u32[]{:S(2)}) collective-permute-start(f32[512,128]{1,0:T(8,128)S(1)} %group.1.g0), channel_id=1, source_target_pairs={{0,8},{1,9},{2,10},{3,11},{4,12},{5,13},{6,14},{7,15},{8,0},{9,1},... | collective-permute-start | bytes 786440 | tf_op jit(solution)/shard_map/ppermute | solution.py:39
  14.4 15.6 %collective-permute-start.10 = (f32[512,128]{1,0:T(8,128)S(1)}, f32[512,128]{1,0:T(8,128)S(1)}, u32[]{:S(2)}, u32[]{:S(2)}) collective-permute-start(f32[512,128]{1,0:T(8,128)S(1)} %group.1.g0), channel_id=1, source_target_pairs={{0,12},{1,13},{2,14},{3,15},{4,8},{5,9},{6,10},{7,11},{8,4},{9,5},... | collective-permute-start | bytes 786440 | tf_op jit(solution)/shard_map/ppermute | solution.py:39
  15.5 14.5 %collective-permute-start.9 = (f32[512,128]{1,0:T(8,128)S(1)}, f32[512,128]{1,0:T(8,128)S(1)}, u32[]{:S(2)}, u32[]{:S(2)}) collective-permute-start(f32[512,128]{1,0:T(8,128)S(1)} %group.1.g0), channel_id=1, source_target_pairs={{0,4},{1,5},{2,6},{3,7},{4,0},{5,1},{6,2},{7,3},{8,12},{9,13},{10,... | collective-permute-start | bytes 786440 | tf_op jit(solution)/shard_map/ppermute | solution.py:39
  18.4 7.3 %collective-permute-start.3 = (f32[384,128]{1,0:T(8,128)S(1)}, f32[384,128]{1,0:T(8,128)S(1)}, u32[]{:S(2)}, u32[]{:S(2)}) collective-permute-start(f32[384,128]{1,0:T(8,128)S(1)} %total.1.refs_0_), channel_id=1, source_target_pairs={{0,64},{1,65},{2,66},{3,67},{4,68},{5,69},{6,70},{7,71},{8,72},{9,... | collective-permute-start | bytes 589832 | tf_op jit(solution)/shard_map/ppermute | solution.py:39
  25.8 18.6 %collective-permute-start.6 = (f32[384,128]{1,0:T(8,128)S(1)}, f32[384,128]{1,0:T(8,128)S(1)}, u32[]{:S(2)}, u32[]{:S(2)}) collective-permute-start(f32[384,128]{1,0:T(8,128)S(1)} %shift.1.own), channel_id=1, source_target_pairs={{0,16},{1,17},{2,18},{3,19},{4,20},{5,21},{6,22},{7,23},{8,24},{9,... | collective-permute-start | bytes 589832 | tf_op jit(solution)/shard_map/ppermute | solution.py:39
  26.1 18.3 %collective-permute-start.5 = (f32[384,128]{1,0:T(8,128)S(1)}, f32[384,128]{1,0:T(8,128)S(1)}, u32[]{:S(2)}, u32[]{:S(2)}) collective-permute-start(f32[384,128]{1,0:T(8,128)S(1)} %shift.1.own), channel_id=1, source_target_pairs={{0,48},{1,49},{2,50},{3,51},{4,52},{5,53},{6,54},{7,55},{8,56},{9,... | collective-permute-start | bytes 589832 | tf_op jit(solution)/shard_map/ppermute | solution.py:39
  28.2 16.2 %collective-permute-start.4 = (f32[384,128]{1,0:T(8,128)S(1)}, f32[384,128]{1,0:T(8,128)S(1)}, u32[]{:S(2)}, u32[]{:S(2)}) collective-permute-start(f32[384,128]{1,0:T(8,128)S(1)} %shift.1.own), channel_id=1, source_target_pairs={{0,32},{1,33},{2,34},{3,35},{4,36},{5,37},{6,38},{7,39},{8,40},{9,... | collective-permute-start | bytes 589832 | tf_op jit(solution)/shard_map/ppermute | solution.py:39
  31.1 1.3 %collective-permute-start.14 = (f32[64,128]{1,0:T(8,128)S(1)}, f32[64,128]{1,0:T(8,128)S(1)}, u32[]{:S(2)}, u32[]{:S(2)}) collective-permute-start(f32[64,128]{1,0:T(8,128)S(1)} %get-tuple-element.30), channel_id=1, source_target_pairs={{0,1},{1,0},{2,3},{3,2},{4,5},{5,4},{6,7},{7,6},{8,9},{9,8},{10,11... | collective-permute-start | bytes 98312 | tf_op jit(solution)/shard_map/ppermute | solution.py:39
  31.1 4.8 %collective-permute-start.12 = (f32[128,128]{1,0:T(8,128)S(1)}, f32[128,128]{1,0:T(8,128)S(1)}, u32[]{:S(2)}, u32[]{:S(2)}) collective-permute-start(f32[128,128]{1,0:T(8,128)S(1)} %get-tuple-element.27), channel_id=1, source_target_pairs={{0,2},{1,3},{2,0},{3,1},{4,6},{5,7},{6,4},{7,5},{8,10},{9,11},{10,... | collective-permute-start | bytes 196616 | tf_op jit(solution)/shard_map/ppermute | solution.py:39
  32.4 5.9 %collective-permute-start.15 = (f32[64,128]{1,0:T(8,128)S(1)}, f32[64,128]{1,0:T(8,128)S(1)}, u32[]{:S(2)}, u32[]{:S(2)}) collective-permute-start(f32[64,128]{1,0:T(8,128)S(1)} %merge.1.refs_0_), channel_id=1, source_target_pairs={{0,64},{1,65},{2,66},{3,67},{4,68},{5,69},{6,70},{7,71},{8,72},{9,... | collective-permute-start | bytes 98312 | tf_op jit(solution)/shard_map/ppermute | solution.py:39
  38.3 3.9 %collective-permute-start.16 = (f32[64,128]{1,0:T(8,128)S(1)}, f32[64,128]{1,0:T(8,128)S(1)}, u32[]{:S(2)}, u32[]{:S(2)}) collective-permute-start(f32[64,128]{1,0:T(8,128)S(1)} %edge.2.refs_0_), channel_id=1, source_target_pairs={{0,16},{1,17},{2,18},{3,19},{4,20},{5,21},{6,22},{7,23},{8,24},{9,... | collective-permute-start | bytes 98312 | tf_op jit(solution)/shard_map/ppermute | solution.py:39
  38.4 9.1 %collective-permute-start.13 = (f32[128,128]{1,0:T(8,128)S(1)}, f32[128,128]{1,0:T(8,128)S(1)}, u32[]{:S(2)}, u32[]{:S(2)}) collective-permute-start(f32[128,128]{1,0:T(8,128)S(1)} %couple.1), channel_id=1, source_target_pairs={{0,1},{1,0},{2,3},{3,2},{4,5},{5,4},{6,7},{7,6},{8,9},{9,8},{10,11... | collective-permute-start | bytes 196616 | tf_op jit(solution)/shard_map/ppermute | solution.py:39
  42.2 5.3 %collective-permute-start.17 = (f32[64,128]{1,0:T(8,128)S(1)}, f32[64,128]{1,0:T(8,128)S(1)}, u32[]{:S(2)}, u32[]{:S(2)}) collective-permute-start(f32[64,128]{1,0:T(8,128)S(1)} %edge.3.edge0), channel_id=1, source_target_pairs={{0,48},{1,49},{2,50},{3,51},{4,52},{5,53},{6,54},{7,55},{8,56},{9,... | collective-permute-start | bytes 98312 | tf_op jit(solution)/shard_map/ppermute | solution.py:39

commit v7 on v6

--- a/solution.py
+++ b/solution.py
@@ -419,9 +419,9 @@
     back = send(leave, lambda m, d: (m, d ^ 2))
     got = swap_cores(small(couple_kernel, "couple", 2 * STRIP, [stay_sib, back]))
     edge = small(merge_kernel, "merge", STRIP, [half, came])
-    edge = small(sum_kernel, "edge", STRIP, [edge, over_z_hi(edge)])
     edge = small(sum_kernel, "edge", STRIP, [edge, send(edge, lambda m, d: (m ^ 1, d))])
-    other = send(edge, lambda m, d: (m ^ 3, d))
+    edge = small(sum_kernel, "edge", STRIP, [edge, send(edge, lambda m, d: (m ^ 3, d))])
+    other = over_z_hi(edge)
     fields, slopes = recentre(ensemble, [total, *chunks[::-1]])
     out = advance(fields, slopes, stay, back, got, edge, other)
     return out.reshape(shape)

time: 51.9 us -> 52.6 us (1.013)
  transfers between devices with their start and end apart: 18 -> 18, of which waited for: 7 -> 8; matrix products, arithmetic and copies ran while one was open for 0% -> 0% of each run, Pallas kernels for 8% -> 8%
where the time goes in v7:
time: 52.6 us; the launch traced here: 52.5 us
  starting transfers between devices  25.3 us (48%)
  waiting for transfers between devices  15.3 us (29%)
  Pallas kernels  11.8 us (22%)
    ppermute x18, starting transfers between devices, send(): return lax.ppermute(array, MESH, pairs(target))  25.3 us
    ppermute x18, waiting for transfers between devices, send(): return lax.ppermute(array, MESH, pairs(target))  15.3 us
    pallas_call x1, Pallas kernels, advance(): pl.pallas_call(advance_kernel, out_shape=jax.ShapeDtypeStruct((LOCAL, PLA...  4.34 us
    pallas_call x1, Pallas kernels, prepare(): pl.pallas_call(prepare_kernel, out_shape=shaped(*[2 * CHUNK] * 4, 2 * REC...  3.22 us
    pallas_call x1, Pallas kernels, recentre(): pl.pallas_call(recentre_kernel, out_shape=[pltpu.VMEM((LOCAL, PLANES, SIZ...  3.08 us
    pallas_call x1, Pallas kernels, pick(): pl.pallas_call(pick_kernel, out_shape=shaped(STRIP, STRIP, 2 * STRIP, STR...  1.08 us
  transfers between devices with their start and end apart: 18, of which 8 were waited for; matrix products, arithmetic and copies ran while one was open for 0% of the time, Pallas kernels for 8%

profile of v7, /device:TPU:0, one launch (start us, length us, event | category | flops | bytes accessed | tf_op | source)
XLA Modules:
  0.0 52.5 jit_solution(1578981095460421949)
XLA Ops:
  0.0 3.2 %prepare.1 = (f32[384,128]{1,0:T(8,128)S(1)}, f32[384,128]{1,0:T(8,128)S(1)}, f32[384,128]{1,0:T(8,128)S(1)}, f32[384,128]{1,0:T(8,128)S(1)}, f32[256,128]{1,0:T(8,128)S(1)}, /*index=5*/f32[256,128]{1,0:T(8,128)S(1)}) custom-call(s32[16]{0:T(128)} %owner_hbm.1, f32[4,12,128,128]{3,2,1,0:T(8,128)} %bitcast.5, f32[12,128,128]{2,1,0:T(8,128)} %bitcast.7), custom_call_target="tpu_custom_call" | custom-call | flops 2000000 | bytes 5000000 | tf_op jit(solution)/shard_map/prepare/pallas_call | solution.py:143
  3.2 2.1 %collective-permute-start.7 = (f32[256,128]{1,0:T(8,128)S(1)}, f32[256,128]{1,0:T(8,128)S(1)}, u32[]{:S(2)}, u32[]{:S(2)}) collective-permute-start(f32[256,128]{1,0:T(8,128)S(1)} %get-tuple-element.25), channel_id=1, source_target_pairs={{0,2},{1,3},{2,0},{3,1},{4,6},{5,7},{6,4},{7,5},{8,10},{9,11},{10,... | collective-permute-start | bytes 393224 | tf_op jit(solution)/shard_map/ppermute | solution.py:39
  5.3 1.6 %collective-permute-start = (f32[384,128]{1,0:T(8,128)S(1)}, f32[384,128]{1,0:T(8,128)S(1)}, u32[]{:S(2)}, u32[]{:S(2)}) collective-permute-start(f32[384,128]{1,0:T(8,128)S(1)} %get-tuple-element.18), channel_id=1, source_target_pairs={{0,16},{1,17},{2,18},{3,19},{4,20},{5,21},{6,22},{7,23},{8,24},{9,... | collective-permute-start | bytes 589832 | tf_op jit(solution)/shard_map/ppermute | solution.py:39
  6.9 2.2 %collective-permute-start.1 = (f32[384,128]{1,0:T(8,128)S(1)}, f32[384,128]{1,0:T(8,128)S(1)}, u32[]{:S(2)}, u32[]{:S(2)}) collective-permute-start(f32[384,128]{1,0:T(8,128)S(1)} %get-tuple-element.19), channel_id=1, source_target_pairs={{0,48},{1,49},{2,50},{3,51},{4,52},{5,53},{6,54},{7,55},{8,56},{9,... | collective-permute-start | bytes 589832 | tf_op jit(solution)/shard_map/ppermute | solution.py:39
  9.1 0.7 %collective-permute-start.2 = (f32[384,128]{1,0:T(8,128)S(1)}, f32[384,128]{1,0:T(8,128)S(1)}, u32[]{:S(2)}, u32[]{:S(2)}) collective-permute-start(f32[384,128]{1,0:T(8,128)S(1)} %get-tuple-element.20), channel_id=1, source_target_pairs={{0,32},{1,33},{2,34},{3,35},{4,36},{5,37},{6,38},{7,39},{8,40},{9,... | collective-permute-start | bytes 589832 | tf_op jit(solution)/shard_map/ppermute | solution.py:39
  9.8 0.0 collective-permute-done.7.came
  9.8 0.1 collective-permute-start.8
  9.9 1.3 %collective-permute-done.8.got = f32[256,128]{1,0:T(8,128)S(1)} collective-permute-done((f32[256,128]{1,0:T(8,128)S(1)}, f32[256,128]{1,0:T(8,128)S(1)}, u32[]{:S(2)}, u32[]{:S(2)}) %collective-permute-start.8) | collective-permute-done | bytes 131104 | tf_op jit(solution)/shard_map/ppermute | solution.py:39
  11.3 3.1 %collective-permute-start.11 = (f32[512,128]{1,0:T(8,128)S(1)}, f32[512,128]{1,0:T(8,128)S(1)}, u32[]{:S(2)}, u32[]{:S(2)}) collective-permute-start(f32[512,128]{1,0:T(8,128)S(1)} %group.1.g0), channel_id=1, source_target_pairs={{0,8},{1,9},{2,10},{3,11},{4,12},{5,13},{6,14},{7,15},{8,0},{9,1},... | collective-permute-start | bytes 786440 | tf_op jit(solution)/shard_map/ppermute | solution.py:39
  14.4 1.1 %collective-permute-start.10 = (f32[512,128]{1,0:T(8,128)S(1)}, f32[512,128]{1,0:T(8,128)S(1)}, u32[]{:S(2)}, u32[]{:S(2)}) collective-permute-start(f32[512,128]{1,0:T(8,128)S(1)} %group.1.g0), channel_id=1, source_target_pairs={{0,12},{1,13},{2,14},{3,15},{4,8},{5,9},{6,10},{7,11},{8,4},{9,5},... | collective-permute-start | bytes 786440 | tf_op jit(solution)/shard_map/ppermute | solution.py:39
  15.5 0.0 collective-permute-done.refs_0_
  15.5 0.0 collective-permute-start.9
  15.5 1.4 %collective-permute-done.1.refs_1_ = f32[384,128]{1,0:T(8,128)S(1)} collective-permute-done((f32[384,128]{1,0:T(8,128)S(1)}, f32[384,128]{1,0:T(8,128)S(1)}, u32[]{:S(2)}, u32[]{:S(2)}) %collective-permute-start.1) | collective-permute-done | bytes 196640 | tf_op jit(solution)/shard_map/ppermute | solution.py:39
  16.9 1.5 %collective-permute-done.2.refs_2_ = f32[384,128]{1,0:T(8,128)S(1)} collective-permute-done((f32[384,128]{1,0:T(8,128)S(1)}, f32[384,128]{1,0:T(8,128)S(1)}, u32[]{:S(2)}, u32[]{:S(2)}) %collective-permute-start.2) | collective-permute-done | bytes 196640 | tf_op jit(solution)/shard_map/ppermute | solution.py:39
  18.4 3.7 %collective-permute-start.3 = (f32[384,128]{1,0:T(8,128)S(1)}, f32[384,128]{1,0:T(8,128)S(1)}, u32[]{:S(2)}, u32[]{:S(2)}) collective-permute-start(f32[384,128]{1,0:T(8,128)S(1)} %total.1.refs_0_), channel_id=1, source_target_pairs={{0,64},{1,65},{2,66},{3,67},{4,68},{5,69},{6,70},{7,71},{8,72},{9,... | collective-permute-start | bytes 589832 | tf_op jit(solution)/shard_map/ppermute | solution.py:39
  22.1 3.7 %collective-permute-done.3.refs_1_ = f32[384,128]{1,0:T(8,128)S(1)} collective-permute-done((f32[384,128]{1,0:T(8,128)S(1)}, f32[384,128]{1,0:T(8,128)S(1)}, u32[]{:S(2)}, u32[]{:S(2)}) %collective-permute-start.3) | collective-permute-done | bytes 196640 | tf_op jit(solution)/shard_map/ppermute | solution.py:39
  25.8 0.3 collective-permute-start.6
  26.1 2.1 %collective-permute-start.5 = (f32[384,128]{1,0:T(8,128)S(1)}, f32[384,128]{1,0:T(8,128)S(1)}, u32[]{:S(2)}, u32[]{:S(2)}) collective-permute-start(f32[384,128]{1,0:T(8,128)S(1)} %shift.1.own), channel_id=1, source_target_pairs={{0,48},{1,49},{2,50},{3,51},{4,52},{5,53},{6,54},{7,55},{8,56},{9,... | collective-permute-start | bytes 589832 | tf_op jit(solution)/shard_map/ppermute | solution.py:39
  28.2 0.0 collective-permute-done.11.g2
  28.2 1.8 %collective-permute-start.4 = (f32[384,128]{1,0:T(8,128)S(1)}, f32[384,128]{1,0:T(8,128)S(1)}, u32[]{:S(2)}, u32[]{:S(2)}) collective-permute-start(f32[384,128]{1,0:T(8,128)S(1)} %shift.1.own), channel_id=1, source_target_pairs={{0,32},{1,33},{2,34},{3,35},{4,36},{5,37},{6,38},{7,39},{8,40},{9,... | collective-permute-start | bytes 589832 | tf_op jit(solution)/shard_map/ppermute | solution.py:39
  30.0 0.0 collective-permute-done.10.g3
  30.0 0.0 collective-permute-done.9.g1
  30.0 1.1 %pick.1 = (f32[64,128]{1,0:T(8,128)S(1)}, f32[64,128]{1,0:T(8,128)S(1)}, f32[128,128]{1,0:T(8,128)S(1)}, f32[64,128]{1,0:T(8,128)S(1)}, f32[64,128]{1,0:T(8,128)S(1)}) custom-call(s32[4,16]{1,0:T(4,128)} %bitcast.8, s32[4,16]{1,0:T(4,128)} %bitcast.9, f32[512,128]{1,0:T(8,128)S(1)} %group.1.g0, f32[512,128]{1,0:T(8,128)S(1)} %collective-permute-done.9.g1, ...), custom_call_target="tpu_custom_call" | custom-call | tf_op jit(solution)/shard_map/pick/pallas_call | solution.py:232
  31.1 0.1 collective-permute-start.14
  31.1 0.4 collective-permute-start.12
  31.6 0.8 %collective-permute-done.14.came = f32[64,128]{1,0:T(8,128)S(1)} collective-permute-done((f32[64,128]{1,0:T(8,128)S(1)}, f32[64,128]{1,0:T(8,128)S(1)}, u32[]{:S(2)}, u32[]{:S(2)}) %collective-permute-start.14) | collective-permute-done | bytes 32800 | tf_op jit(solution)/shard_map/ppermute | solution.py:39
  32.4 0.3 collective-permute-start.15
  32.7 3.0 %collective-permute-done.12.back = f32[128,128]{1,0:T(8,128)S(1)} collective-permute-done((f32[128,128]{1,0:T(8,128)S(1)}, f32[128,128]{1,0:T(8,128)S(1)}, u32[]{:S(2)}, u32[]{:S(2)}) %collective-permute-start.12) | collective-permute-done | bytes 65568 | tf_op jit(solution)/shard_map/ppermute | solution.py:39
  35.7 0.7 %collective-permute-done.15.refs_1_ = f32[64,128]{1,0:T(8,128)S(1)} collective-permute-done((f32[64,128]{1,0:T(8,128)S(1)}, f32[64,128]{1,0:T(8,128)S(1)}, u32[]{:S(2)}, u32[]{:S(2)}) %collective-permute-start.15) | collective-permute-done | bytes 32800 | tf_op jit(solution)/shard_map/ppermute | solution.py:39
  36.4 2.2 %collective-permute-start.16 = (f32[64,128]{1,0:T(8,128)S(1)}, f32[64,128]{1,0:T(8,128)S(1)}, u32[]{:S(2)}, u32[]{:S(2)}) collective-permute-start(f32[64,128]{1,0:T(8,128)S(1)} %edge.2.refs_0_), channel_id=1, source_target_pairs={{0,48},{1,49},{2,50},{3,51},{4,52},{5,53},{6,54},{7,55},{8,56},{9,... | collective-permute-start | bytes 98312 | tf_op jit(solution)/shard_map/ppermute | solution.py:39
  38.6 0.0 collective-permute-start.13
  38.6 2.9 %collective-permute-done.16.refs_1_ = f32[64,128]{1,0:T(8,128)S(1)} collective-permute-done((f32[64,128]{1,0:T(8,128)S(1)}, f32[64,128]{1,0:T(8,128)S(1)}, u32[]{:S(2)}, u32[]{:S(2)}) %collective-permute-start.16) | collective-permute-done | bytes 32800 | tf_op jit(solution)/shard_map/ppermute | solution.py:39
  41.5 3.5 %collective-permute-start.17 = (f32[64,128]{1,0:T(8,128)S(1)}, f32[64,128]{1,0:T(8,128)S(1)}, u32[]{:S(2)}, u32[]{:S(2)}) collective-permute-start(f32[64,128]{1,0:T(8,128)S(1)} %edge.3.edge0), channel_id=1, source_target_pairs={{0,64},{1,65},{2,66},{3,67},{4,68},{5,69},{6,70},{7,71},{8,72},{9,... | collective-permute-start | bytes 98312 | tf_op jit(solution)/shard_map/ppermute | solution.py:39
  45.0 0.0 collective-permute-done.6.a
  45.0 0.0 collective-permute-done.5.b
  45.0 0.0 collective-permute-done.4.c
  45.0 3.1 %recentre.1 = (f32[4,12,144,128]{3,2,1,0:T(8,128)S(1)}, f32[4,12,128,128]{3,2,1,0:T(8,128)S(1)}) custom-call(f32[4,12,128,128]{3,2,1,0:T(8,128)} %bitcast.6, f32[384,128]{1,0:T(8,128)S(1)} %shift.1.own, f32[384,128]{1,0:T(8,128)S(1)} %collective-permute-done.4.c, f32[384,128]{1,0:T(8,128)S(1)} %collective-permute-done.5.b, ...), custom_call_target="tpu_custom_call" | custom-call | tf_op jit(solution)/shard_map/recentre/pallas_call | solution.py:289
  48.1 0.0 collective-permute-done.13.got
  48.1 0.0 collective-permute-done.17.edge1
  48.1 4.3 %advance.1 = f32[4,12,128,128]{3,2,1,0:T(8,128)} custom-call(f32[4,12,144,128]{3,2,1,0:T(8,128)S(1)} %get-tuple-element.22.fields, f32[4,12,128,128]{3,2,1,0:T(8,128)S(1)} %get-tuple-element.23.slopes, f32[64,128]{1,0:T(8,128)S(1)} %get-tuple-element.26.stay, f32[128,128]{1,0:T(8,128)S(1)} %collective-permute-done.12.back, ...), custom_call_target="tpu_custom_call" | custom-call | flops 40000000 | bytes 8000000 | tf_op jit(solution)/shard_map/advance/pallas_call | solution.py:387
  (8 shorter events, 0.1 us)
Async XLA Ops:
  3.2 6.6 %collective-permute-start.7 = (f32[256,128]{1,0:T(8,128)S(1)}, f32[256,128]{1,0:T(8,128)S(1)}, u32[]{:S(2)}, u32[]{:S(2)}) collective-permute-start(f32[256,128]{1,0:T(8,128)S(1)} %get-tuple-element.25), channel_id=1, source_target_pairs={{0,2},{1,3},{2,0},{3,1},{4,6},{5,7},{6,4},{7,5},{8,10},{9,11},{10,... | collective-permute-start | bytes 393224 | tf_op jit(solution)/shard_map/ppermute | solution.py:39
  5.3 10.2 %collective-permute-start = (f32[384,128]{1,0:T(8,128)S(1)}, f32[384,128]{1,0:T(8,128)S(1)}, u32[]{:S(2)}, u32[]{:S(2)}) collective-permute-start(f32[384,128]{1,0:T(8,128)S(1)} %get-tuple-element.18), channel_id=1, source_target_pairs={{0,16},{1,17},{2,18},{3,19},{4,20},{5,21},{6,22},{7,23},{8,24},{9,... | collective-permute-start | bytes 589832 | tf_op jit(solution)/shard_map/ppermute | solution.py:39
  6.9 10.0 %collective-permute-start.1 = (f32[384,128]{1,0:T(8,128)S(1)}, f32[384,128]{1,0:T(8,128)S(1)}, u32[]{:S(2)}, u32[]{:S(2)}) collective-permute-start(f32[384,128]{1,0:T(8,128)S(1)} %get-tuple-element.19), channel_id=1, source_target_pairs={{0,48},{1,49},{2,50},{3,51},{4,52},{5,53},{6,54},{7,55},{8,56},{9,... | collective-permute-start | bytes 589832 | tf_op jit(solution)/shard_map/ppermute | solution.py:39
  9.1 9.3 %collective-permute-start.2 = (f32[384,128]{1,0:T(8,128)S(1)}, f32[384,128]{1,0:T(8,128)S(1)}, u32[]{:S(2)}, u32[]{:S(2)}) collective-permute-start(f32[384,128]{1,0:T(8,128)S(1)} %get-tuple-element.20), channel_id=1, source_target_pairs={{0,32},{1,33},{2,34},{3,35},{4,36},{5,37},{6,38},{7,39},{8,40},{9,... | collective-permute-start | bytes 589832 | tf_op jit(solution)/shard_map/ppermute | solution.py:39
  9.8 1.4 %collective-permute-start.8 = (f32[256,128]{1,0:T(8,128)S(1)}, f32[256,128]{1,0:T(8,128)S(1)}, u32[]{:S(2)}, u32[]{:S(2)}) collective-permute-start(f32[256,128]{1,0:T(8,128)S(1)} %split.1), channel_id=1, source_target_pairs={{0,1},{1,0},{2,3},{3,2},{4,5},{5,4},{6,7},{7,6},{8,9},{9,8},{10,11... | collective-permute-start | bytes 393224 | tf_op jit(solution)/shard_map/ppermute | solution.py:39
  11.3 16.9 %collective-permute-start.11 = (f32[512,128]{1,0:T(8,128)S(1)}, f32[512,128]{1,0:T(8,128)S(1)}, u32[]{:S(2)}, u32[]{:S(2)}) collective-permute-start(f32[512,128]{1,0:T(8,128)S(1)} %group.1.g0), channel_id=1, source_target_pairs={{0,8},{1,9},{2,10},{3,11},{4,12},{5,13},{6,14},{7,15},{8,0},{9,1},... | collective-permute-start | bytes 786440 | tf_op jit(solution)/shard_map/ppermute | solution.py:39
  14.4 15.6 %collective-permute-start.10 = (f32[512,128]{1,0:T(8,128)S(1)}, f32[512,128]{1,0:T(8,128)S(1)}, u32[]{:S(2)}, u32[]{:S(2)}) collective-permute-start(f32[512,128]{1,0:T(8,128)S(1)} %group.1.g0), channel_id=1, source_target_pairs={{0,12},{1,13},{2,14},{3,15},{4,8},{5,9},{6,10},{7,11},{8,4},{9,5},... | collective-permute-start | bytes 786440 | tf_op jit(solution)/shard_map/ppermute | solution.py:39
  15.5 14.5 %collective-permute-start.9 = (f32[512,128]{1,0:T(8,128)S(1)}, f32[512,128]{1,0:T(8,128)S(1)}, u32[]{:S(2)}, u32[]{:S(2)}) collective-permute-start(f32[512,128]{1,0:T(8,128)S(1)} %group.1.g0), channel_id=1, source_target_pairs={{0,4},{1,5},{2,6},{3,7},{4,0},{5,1},{6,2},{7,3},{8,12},{9,13},{10,... | collective-permute-start | bytes 786440 | tf_op jit(solution)/shard_map/ppermute | solution.py:39
  18.4 7.3 %collective-permute-start.3 = (f32[384,128]{1,0:T(8,128)S(1)}, f32[384,128]{1,0:T(8,128)S(1)}, u32[]{:S(2)}, u32[]{:S(2)}) collective-permute-start(f32[384,128]{1,0:T(8,128)S(1)} %total.1.refs_0_), channel_id=1, source_target_pairs={{0,64},{1,65},{2,66},{3,67},{4,68},{5,69},{6,70},{7,71},{8,72},{9,... | collective-permute-start | bytes 589832 | tf_op jit(solution)/shard_map/ppermute | solution.py:39
  25.8 19.2 %collective-permute-start.6 = (f32[384,128]{1,0:T(8,128)S(1)}, f32[384,128]{1,0:T(8,128)S(1)}, u32[]{:S(2)}, u32[]{:S(2)}) collective-permute-start(f32[384,128]{1,0:T(8,128)S(1)} %shift.1.own), channel_id=1, source_target_pairs={{0,16},{1,17},{2,18},{3,19},{4,20},{5,21},{6,22},{7,23},{8,24},{9,... | collective-permute-start | bytes 589832 | tf_op jit(solution)/shard_map/ppermute | solution.py:39
  26.1 18.9 %collective-permute-start.5 = (f32[384,128]{1,0:T(8,128)S(1)}, f32[384,128]{1,0:T(8,128)S(1)}, u32[]{:S(2)}, u32[]{:S(2)}) collective-permute-start(f32[384,128]{1,0:T(8,128)S(1)} %shift.1.own), channel_id=1, source_target_pairs={{0,48},{1,49},{2,50},{3,51},{4,52},{5,53},{6,54},{7,55},{8,56},{9,... | collective-permute-start | bytes 589832 | tf_op jit(solution)/shard_map/ppermute | solution.py:39
  28.2 16.8 %collective-permute-start.4 = (f32[384,128]{1,0:T(8,128)S(1)}, f32[384,128]{1,0:T(8,128)S(1)}, u32[]{:S(2)}, u32[]{:S(2)}) collective-permute-start(f32[384,128]{1,0:T(8,128)S(1)} %shift.1.own), channel_id=1, source_target_pairs={{0,32},{1,33},{2,34},{3,35},{4,36},{5,37},{6,38},{7,39},{8,40},{9,... | collective-permute-start | bytes 589832 | tf_op jit(solution)/shard_map/ppermute | solution.py:39
  31.1 1.3 %collective-permute-start.14 = (f32[64,128]{1,0:T(8,128)S(1)}, f32[64,128]{1,0:T(8,128)S(1)}, u32[]{:S(2)}, u32[]{:S(2)}) collective-permute-start(f32[64,128]{1,0:T(8,128)S(1)} %get-tuple-element.30), channel_id=1, source_target_pairs={{0,1},{1,0},{2,3},{3,2},{4,5},{5,4},{6,7},{7,6},{8,9},{9,8},{10,11... | collective-permute-start | bytes 98312 | tf_op jit(solution)/shard_map/ppermute | solution.py:39
  31.1 4.5 %collective-permute-start.12 = (f32[128,128]{1,0:T(8,128)S(1)}, f32[128,128]{1,0:T(8,128)S(1)}, u32[]{:S(2)}, u32[]{:S(2)}) collective-permute-start(f32[128,128]{1,0:T(8,128)S(1)} %get-tuple-element.27), channel_id=1, source_target_pairs={{0,2},{1,3},{2,0},{3,1},{4,6},{5,7},{6,4},{7,5},{8,10},{9,11},{10,... | collective-permute-start | bytes 196616 | tf_op jit(solution)/shard_map/ppermute | solution.py:39
  32.4 4.0 %collective-permute-start.15 = (f32[64,128]{1,0:T(8,128)S(1)}, f32[64,128]{1,0:T(8,128)S(1)}, u32[]{:S(2)}, u32[]{:S(2)}) collective-permute-start(f32[64,128]{1,0:T(8,128)S(1)} %merge.1.refs_0_), channel_id=1, source_target_pairs={{0,16},{1,17},{2,18},{3,19},{4,20},{5,21},{6,22},{7,23},{8,24},{9,... | collective-permute-start | bytes 98312 | tf_op jit(solution)/shard_map/ppermute | solution.py:39
  36.4 5.1 %collective-permute-start.16 = (f32[64,128]{1,0:T(8,128)S(1)}, f32[64,128]{1,0:T(8,128)S(1)}, u32[]{:S(2)}, u32[]{:S(2)}) collective-permute-start(f32[64,128]{1,0:T(8,128)S(1)} %edge.2.refs_0_), channel_id=1, source_target_pairs={{0,48},{1,49},{2,50},{3,51},{4,52},{5,53},{6,54},{7,55},{8,56},{9,... | collective-permute-start | bytes 98312 | tf_op jit(solution)/shard_map/ppermute | solution.py:39
  38.6 9.5 %collective-permute-start.13 = (f32[128,128]{1,0:T(8,128)S(1)}, f32[128,128]{1,0:T(8,128)S(1)}, u32[]{:S(2)}, u32[]{:S(2)}) collective-permute-start(f32[128,128]{1,0:T(8,128)S(1)} %couple.1), channel_id=1, source_target_pairs={{0,1},{1,0},{2,3},{3,2},{4,5},{5,4},{6,7},{7,6},{8,9},{9,8},{10,11... | collective-permute-start | bytes 196616 | tf_op jit(solution)/shard_map/ppermute | solution.py:39
  41.5 6.6 %collective-permute-start.17 = (f32[64,128]{1,0:T(8,128)S(1)}, f32[64,128]{1,0:T(8,128)S(1)}, u32[]{:S(2)}, u32[]{:S(2)}) collective-permute-start(f32[64,128]{1,0:T(8,128)S(1)} %edge.3.edge0), channel_id=1, source_target_pairs={{0,64},{1,65},{2,66},{3,67},{4,68},{5,69},{6,70},{7,71},{8,72},{9,... | collective-permute-start | bytes 98312 | tf_op jit(solution)/shard_map/ppermute | solution.py:39

commit v8 on v6

--- a/solution.py
+++ b/solution.py
@@ -304,7 +304,7 @@
     )(*on(pltpu.HBM, ensemble), *on(pltpu.VMEM, *arrays))
 
 
-def advance_kernel(fields, slopes, stay, back, got, edge0, edge1, out, rims, lines, columns, div):
+def advance_kernel(fields, slopes, stay, back, got, edge0, edge1, out, rims, lines, columns, div, slope_u):
     now_at = pl.program_id(0)
 
     @pl.when(now_at == 0)
@@ -367,7 +367,9 @@
             - fields[step, iv, 7 + SIZE : 8 + SIZE, :]
         )
         for r in range(0, SIZE, part):
-            div[8 + r : 8 + r + part, :] = 0.5 * (across(iu, r) + below(iv, r) - above(iv, r))
+            du = across(iu, r)
+            slope_u[r : r + part, :] = du
+            div[8 + r : 8 + r + part, :] = 0.5 * (du + below(iv, r) - above(iv, r))
         for r in range(0, SIZE, part):
             u, v, w = rows_at(iu, r), rows_at(iv, r), rows_at(iw, r)
             edge = pltpu.roll(columns[step, r : r + part, :], (SIZE - 1 - 2 * deep) % SIZE, 1)
@@ -375,7 +377,7 @@
             mid = div[8 + r : 8 + r + part, :]
             grad_x = jnp.where(at_right, edge, pltpu.roll(mid, SIZE - 1, 1)) - jnp.where(at_left, edge, pltpu.roll(mid, 1, 1))
             grad_y = div[9 + r : 9 + r + part, :] - div[7 + r : 7 + r + part, :]
-            new_u = u - 0.2 * (u * across(iu, r) + v * (below(iu, r) - above(iu, r)))
+            new_u = u - 0.2 * (u * slope_u[r : r + part, :] + v * (below(iu, r) - above(iu, r)))
             new_v = v - 0.2 * (u * across(iv, r) + v * (below(iv, r) - above(iv, r)))
             new_w = w - 0.2 * (u * across(iw, r) + v * (below(iw, r) - above(iw, r)))
             out[0, iu, r : r + part, :] = new_u + 0.1 * grad_x
@@ -395,6 +397,7 @@
             pltpu.VMEM((SIZE, SIZE), F32),
             pltpu.VMEM((LOCAL, SIZE, SIZE), F32),
             pltpu.VMEM((SIZE + 16, SIZE), F32),
+            pltpu.VMEM((SIZE, SIZE), F32),
         ],
         compiler_params=limit(8),
         cost_estimate=pl.CostEstimate(flops=40_000_000, bytes_accessed=8_000_000, transcendentals=0),

time: 51.9 us -> 51.8 us (level)
  no operation moved by 1% of the time
where the time goes in v8:
time: 51.8 us; the launch traced here: 51.6 us
  starting transfers between devices  25.1 us (48%)
  waiting for transfers between devices  14.8 us (29%)
  Pallas kernels  11.6 us (22%)
    ppermute x18, starting transfers between devices, send(): return lax.ppermute(array, MESH, pairs(target))  25.1 us
    ppermute x18, waiting for transfers between devices, send(): return lax.ppermute(array, MESH, pairs(target))  14.8 us
    pallas_call x1, Pallas kernels, advance(): pl.pallas_call(advance_kernel, out_shape=jax.ShapeDtypeStruct((LOCAL, PLA...  4.14 us
    pallas_call x1, Pallas kernels, prepare(): pl.pallas_call(prepare_kernel, out_shape=shaped(*[2 * CHUNK] * 4, 2 * REC...  3.22 us
    pallas_call x1, Pallas kernels, recentre(): pl.pallas_call(recentre_kernel, out_shape=[pltpu.VMEM((LOCAL, PLANES, SIZ...  3.08 us
    pallas_call x1, Pallas kernels, pick(): pl.pallas_call(pick_kernel, out_shape=shaped(STRIP, STRIP, 2 * STRIP, STR...  1.08 us
  transfers between devices with their start and end apart: 18, of which 7 were waited for; matrix products, arithmetic and copies ran while one was open for 0% of the time, Pallas kernels for 8%

profile of v8, /device:TPU:0, one launch (start us, length us, event | category | flops | bytes accessed | tf_op | source)
XLA Modules:
  0.0 51.6 jit_solution(10872284265386160401)
XLA Ops:
  0.0 3.2 %prepare.1 = (f32[384,128]{1,0:T(8,128)S(1)}, f32[384,128]{1,0:T(8,128)S(1)}, f32[384,128]{1,0:T(8,128)S(1)}, f32[384,128]{1,0:T(8,128)S(1)}, f32[256,128]{1,0:T(8,128)S(1)}, /*index=5*/f32[256,128]{1,0:T(8,128)S(1)}) custom-call(s32[16]{0:T(128)} %owner_hbm.1, f32[4,12,128,128]{3,2,1,0:T(8,128)} %bitcast.5, f32[12,128,128]{2,1,0:T(8,128)} %bitcast.7), custom_call_target="tpu_custom_call" | custom-call | flops 2000000 | bytes 5000000 | tf_op jit(solution)/shard_map/prepare/pallas_call | solution.py:143
  3.2 2.1 %collective-permute-start.7 = (f32[256,128]{1,0:T(8,128)S(1)}, f32[256,128]{1,0:T(8,128)S(1)}, u32[]{:S(2)}, u32[]{:S(2)}) collective-permute-start(f32[256,128]{1,0:T(8,128)S(1)} %get-tuple-element.25), channel_id=1, source_target_pairs={{0,2},{1,3},{2,0},{3,1},{4,6},{5,7},{6,4},{7,5},{8,10},{9,11},{10,... | collective-permute-start | bytes 393224 | tf_op jit(solution)/shard_map/ppermute | solution.py:39
  5.3 1.6 %collective-permute-start = (f32[384,128]{1,0:T(8,128)S(1)}, f32[384,128]{1,0:T(8,128)S(1)}, u32[]{:S(2)}, u32[]{:S(2)}) collective-permute-start(f32[384,128]{1,0:T(8,128)S(1)} %get-tuple-element.18), channel_id=1, source_target_pairs={{0,16},{1,17},{2,18},{3,19},{4,20},{5,21},{6,22},{7,23},{8,24},{9,... | collective-permute-start | bytes 589832 | tf_op jit(solution)/shard_map/ppermute | solution.py:39
  6.9 2.2 %collective-permute-start.1 = (f32[384,128]{1,0:T(8,128)S(1)}, f32[384,128]{1,0:T(8,128)S(1)}, u32[]{:S(2)}, u32[]{:S(2)}) collective-permute-start(f32[384,128]{1,0:T(8,128)S(1)} %get-tuple-element.19), channel_id=1, source_target_pairs={{0,48},{1,49},{2,50},{3,51},{4,52},{5,53},{6,54},{7,55},{8,56},{9,... | collective-permute-start | bytes 589832 | tf_op jit(solution)/shard_map/ppermute | solution.py:39
  9.1 0.7 %collective-permute-start.2 = (f32[384,128]{1,0:T(8,128)S(1)}, f32[384,128]{1,0:T(8,128)S(1)}, u32[]{:S(2)}, u32[]{:S(2)}) collective-permute-start(f32[384,128]{1,0:T(8,128)S(1)} %get-tuple-element.20), channel_id=1, source_target_pairs={{0,32},{1,33},{2,34},{3,35},{4,36},{5,37},{6,38},{7,39},{8,40},{9,... | collective-permute-start | bytes 589832 | tf_op jit(solution)/shard_map/ppermute | solution.py:39
  9.8 0.0 collective-permute-done.7.came
  9.8 0.1 collective-permute-start.8
  9.9 1.3 %collective-permute-done.8.got = f32[256,128]{1,0:T(8,128)S(1)} collective-permute-done((f32[256,128]{1,0:T(8,128)S(1)}, f32[256,128]{1,0:T(8,128)S(1)}, u32[]{:S(2)}, u32[]{:S(2)}) %collective-permute-start.8) | collective-permute-done | bytes 131104 | tf_op jit(solution)/shard_map/ppermute | solution.py:39
  11.3 3.1 %collective-permute-start.11 = (f32[512,128]{1,0:T(8,128)S(1)}, f32[512,128]{1,0:T(8,128)S(1)}, u32[]{:S(2)}, u32[]{:S(2)}) collective-permute-start(f32[512,128]{1,0:T(8,128)S(1)} %group.1.g0), channel_id=1, source_target_pairs={{0,8},{1,9},{2,10},{3,11},{4,12},{5,13},{6,14},{7,15},{8,0},{9,1},... | collective-permute-start | bytes 786440 | tf_op jit(solution)/shard_map/ppermute | solution.py:39
  14.4 1.1 %collective-permute-start.10 = (f32[512,128]{1,0:T(8,128)S(1)}, f32[512,128]{1,0:T(8,128)S(1)}, u32[]{:S(2)}, u32[]{:S(2)}) collective-permute-start(f32[512,128]{1,0:T(8,128)S(1)} %group.1.g0), channel_id=1, source_target_pairs={{0,12},{1,13},{2,14},{3,15},{4,8},{5,9},{6,10},{7,11},{8,4},{9,5},... | collective-permute-start | bytes 786440 | tf_op jit(solution)/shard_map/ppermute | solution.py:39
  15.5 0.0 collective-permute-done.refs_0_
  15.5 0.0 collective-permute-start.9
  15.5 1.4 %collective-permute-done.1.refs_1_ = f32[384,128]{1,0:T(8,128)S(1)} collective-permute-done((f32[384,128]{1,0:T(8,128)S(1)}, f32[384,128]{1,0:T(8,128)S(1)}, u32[]{:S(2)}, u32[]{:S(2)}) %collective-permute-start.1) | collective-permute-done | bytes 196640 | tf_op jit(solution)/shard_map/ppermute | solution.py:39
  16.9 1.5 %collective-permute-done.2.refs_2_ = f32[384,128]{1,0:T(8,128)S(1)} collective-permute-done((f32[384,128]{1,0:T(8,128)S(1)}, f32[384,128]{1,0:T(8,128)S(1)}, u32[]{:S(2)}, u32[]{:S(2)}) %collective-permute-start.2) | collective-permute-done | bytes 196640 | tf_op jit(solution)/shard_map/ppermute | solution.py:39
  18.4 3.7 %collective-permute-start.3 = (f32[384,128]{1,0:T(8,128)S(1)}, f32[384,128]{1,0:T(8,128)S(1)}, u32[]{:S(2)}, u32[]{:S(2)}) collective-permute-start(f32[384,128]{1,0:T(8,128)S(1)} %total.1.refs_0_), channel_id=1, source_target_pairs={{0,64},{1,65},{2,66},{3,67},{4,68},{5,69},{6,70},{7,71},{8,72},{9,... | collective-permute-start | bytes 589832 | tf_op jit(solution)/shard_map/ppermute | solution.py:39
  22.1 3.7 %collective-permute-done.3.refs_1_ = f32[384,128]{1,0:T(8,128)S(1)} collective-permute-done((f32[384,128]{1,0:T(8,128)S(1)}, f32[384,128]{1,0:T(8,128)S(1)}, u32[]{:S(2)}, u32[]{:S(2)}) %collective-permute-start.3) | collective-permute-done | bytes 196640 | tf_op jit(solution)/shard_map/ppermute | solution.py:39
  25.8 0.3 collective-permute-start.6
  26.1 2.1 %collective-permute-start.5 = (f32[384,128]{1,0:T(8,128)S(1)}, f32[384,128]{1,0:T(8,128)S(1)}, u32[]{:S(2)}, u32[]{:S(2)}) collective-permute-start(f32[384,128]{1,0:T(8,128)S(1)} %shift.1.own), channel_id=1, source_target_pairs={{0,48},{1,49},{2,50},{3,51},{4,52},{5,53},{6,54},{7,55},{8,56},{9,... | collective-permute-start | bytes 589832 | tf_op jit(solution)/shard_map/ppermute | solution.py:39
  28.2 0.0 collective-permute-done.11.g2
  28.2 1.8 %collective-permute-start.4 = (f32[384,128]{1,0:T(8,128)S(1)}, f32[384,128]{1,0:T(8,128)S(1)}, u32[]{:S(2)}, u32[]{:S(2)}) collective-permute-start(f32[384,128]{1,0:T(8,128)S(1)} %shift.1.own), channel_id=1, source_target_pairs={{0,32},{1,33},{2,34},{3,35},{4,36},{5,37},{6,38},{7,39},{8,40},{9,... | collective-permute-start | bytes 589832 | tf_op jit(solution)/shard_map/ppermute | solution.py:39
  30.0 0.0 collective-permute-done.10.g3
  30.0 0.0 collective-permute-done.9.g1
  30.0 1.1 %pick.1 = (f32[64,128]{1,0:T(8,128)S(1)}, f32[64,128]{1,0:T(8,128)S(1)}, f32[128,128]{1,0:T(8,128)S(1)}, f32[64,128]{1,0:T(8,128)S(1)}, f32[64,128]{1,0:T(8,128)S(1)}) custom-call(s32[4,16]{1,0:T(4,128)} %bitcast.8, s32[4,16]{1,0:T(4,128)} %bitcast.9, f32[512,128]{1,0:T(8,128)S(1)} %group.1.g0, f32[512,128]{1,0:T(8,128)S(1)} %collective-permute-done.9.g1, ...), custom_call_target="tpu_custom_call" | custom-call | tf_op jit(solution)/shard_map/pick/pallas_call | solution.py:232
  31.1 0.1 collective-permute-start.14
  31.1 0.4 collective-permute-start.12
  31.6 0.8 %collective-permute-done.14.came = f32[64,128]{1,0:T(8,128)S(1)} collective-permute-done((f32[64,128]{1,0:T(8,128)S(1)}, f32[64,128]{1,0:T(8,128)S(1)}, u32[]{:S(2)}, u32[]{:S(2)}) %collective-permute-start.14) | collective-permute-done | bytes 32800 | tf_op jit(solution)/shard_map/ppermute | solution.py:39
  32.4 3.6 %collective-permute-start.15 = (f32[64,128]{1,0:T(8,128)S(1)}, f32[64,128]{1,0:T(8,128)S(1)}, u32[]{:S(2)}, u32[]{:S(2)}) collective-permute-start(f32[64,128]{1,0:T(8,128)S(1)} %merge.1.refs_0_), channel_id=1, source_target_pairs={{0,64},{1,65},{2,66},{3,67},{4,68},{5,69},{6,70},{7,71},{8,72},{9,... | collective-permute-start | bytes 98312 | tf_op jit(solution)/shard_map/ppermute | solution.py:39
  36.0 0.0 collective-permute-done.12.back
  36.0 2.3 %collective-permute-done.15.refs_1_ = f32[64,128]{1,0:T(8,128)S(1)} collective-permute-done((f32[64,128]{1,0:T(8,128)S(1)}, f32[64,128]{1,0:T(8,128)S(1)}, u32[]{:S(2)}, u32[]{:S(2)}) %collective-permute-start.15) | collective-permute-done | bytes 32800 | tf_op jit(solution)/shard_map/ppermute | solution.py:39
  38.3 0.1 collective-permute-start.16
  38.4 0.0 collective-permute-start.13
  38.4 3.8 %collective-permute-done.16.refs_1_ = f32[64,128]{1,0:T(8,128)S(1)} collective-permute-done((f32[64,128]{1,0:T(8,128)S(1)}, f32[64,128]{1,0:T(8,128)S(1)}, u32[]{:S(2)}, u32[]{:S(2)}) %collective-permute-start.16) | collective-permute-done | bytes 32800 | tf_op jit(solution)/shard_map/ppermute | solution.py:39
  42.2 2.2 %collective-permute-start.17 = (f32[64,128]{1,0:T(8,128)S(1)}, f32[64,128]{1,0:T(8,128)S(1)}, u32[]{:S(2)}, u32[]{:S(2)}) collective-permute-start(f32[64,128]{1,0:T(8,128)S(1)} %edge.3.edge0), channel_id=1, source_target_pairs={{0,48},{1,49},{2,50},{3,51},{4,52},{5,53},{6,54},{7,55},{8,56},{9,... | collective-permute-start | bytes 98312 | tf_op jit(solution)/shard_map/ppermute | solution.py:39
  44.4 0.0 collective-permute-done.6.a
  44.4 0.0 collective-permute-done.5.b
  44.4 0.0 collective-permute-done.4.c
  44.4 3.1 %recentre.1 = (f32[4,12,144,128]{3,2,1,0:T(8,128)S(1)}, f32[4,12,128,128]{3,2,1,0:T(8,128)S(1)}) custom-call(f32[4,12,128,128]{3,2,1,0:T(8,128)} %bitcast.6, f32[384,128]{1,0:T(8,128)S(1)} %shift.1.own, f32[384,128]{1,0:T(8,128)S(1)} %collective-permute-done.4.c, f32[384,128]{1,0:T(8,128)S(1)} %collective-permute-done.5.b, ...), custom_call_target="tpu_custom_call" | custom-call | tf_op jit(solution)/shard_map/recentre/pallas_call | solution.py:289
  47.5 0.0 collective-permute-done.13.got
  47.5 0.0 collective-permute-done.17.edge1
  47.5 4.1 %advance.1 = f32[4,12,128,128]{3,2,1,0:T(8,128)} custom-call(f32[4,12,144,128]{3,2,1,0:T(8,128)S(1)} %get-tuple-element.22.fields, f32[4,12,128,128]{3,2,1,0:T(8,128)S(1)} %get-tuple-element.23.slopes, f32[64,128]{1,0:T(8,128)S(1)} %get-tuple-element.26.stay, f32[128,128]{1,0:T(8,128)S(1)} %collective-permute-done.12.back, ...), custom_call_target="tpu_custom_call" | custom-call | flops 40000000 | bytes 8000000 | tf_op jit(solution)/shard_map/advance/pallas_call | solution.py:389
  (8 shorter events, 0.1 us)
Async XLA Ops:
  3.2 6.6 %collective-permute-start.7 = (f32[256,128]{1,0:T(8,128)S(1)}, f32[256,128]{1,0:T(8,128)S(1)}, u32[]{:S(2)}, u32[]{:S(2)}) collective-permute-start(f32[256,128]{1,0:T(8,128)S(1)} %get-tuple-element.25), channel_id=1, source_target_pairs={{0,2},{1,3},{2,0},{3,1},{4,6},{5,7},{6,4},{7,5},{8,10},{9,11},{10,... | collective-permute-start | bytes 393224 | tf_op jit(solution)/shard_map/ppermute | solution.py:39
  5.3 10.2 %collective-permute-start = (f32[384,128]{1,0:T(8,128)S(1)}, f32[384,128]{1,0:T(8,128)S(1)}, u32[]{:S(2)}, u32[]{:S(2)}) collective-permute-start(f32[384,128]{1,0:T(8,128)S(1)} %get-tuple-element.18), channel_id=1, source_target_pairs={{0,16},{1,17},{2,18},{3,19},{4,20},{5,21},{6,22},{7,23},{8,24},{9,... | collective-permute-start | bytes 589832 | tf_op jit(solution)/shard_map/ppermute | solution.py:39
  6.9 10.0 %collective-permute-start.1 = (f32[384,128]{1,0:T(8,128)S(1)}, f32[384,128]{1,0:T(8,128)S(1)}, u32[]{:S(2)}, u32[]{:S(2)}) collective-permute-start(f32[384,128]{1,0:T(8,128)S(1)} %get-tuple-element.19), channel_id=1, source_target_pairs={{0,48},{1,49},{2,50},{3,51},{4,52},{5,53},{6,54},{7,55},{8,56},{9,... | collective-permute-start | bytes 589832 | tf_op jit(solution)/shard_map/ppermute | solution.py:39
  9.1 9.3 %collective-permute-start.2 = (f32[384,128]{1,0:T(8,128)S(1)}, f32[384,128]{1,0:T(8,128)S(1)}, u32[]{:S(2)}, u32[]{:S(2)}) collective-permute-start(f32[384,128]{1,0:T(8,128)S(1)} %get-tuple-element.20), channel_id=1, source_target_pairs={{0,32},{1,33},{2,34},{3,35},{4,36},{5,37},{6,38},{7,39},{8,40},{9,... | collective-permute-start | bytes 589832 | tf_op jit(solution)/shard_map/ppermute | solution.py:39
  9.8 1.4 %collective-permute-start.8 = (f32[256,128]{1,0:T(8,128)S(1)}, f32[256,128]{1,0:T(8,128)S(1)}, u32[]{:S(2)}, u32[]{:S(2)}) collective-permute-start(f32[256,128]{1,0:T(8,128)S(1)} %split.1), channel_id=1, source_target_pairs={{0,1},{1,0},{2,3},{3,2},{4,5},{5,4},{6,7},{7,6},{8,9},{9,8},{10,11... | collective-permute-start | bytes 393224 | tf_op jit(solution)/shard_map/ppermute | solution.py:39
  11.3 16.9 %collective-permute-start.11 = (f32[512,128]{1,0:T(8,128)S(1)}, f32[512,128]{1,0:T(8,128)S(1)}, u32[]{:S(2)}, u32[]{:S(2)}) collective-permute-start(f32[512,128]{1,0:T(8,128)S(1)} %group.1.g0), channel_id=1, source_target_pairs={{0,8},{1,9},{2,10},{3,11},{4,12},{5,13},{6,14},{7,15},{8,0},{9,1},... | collective-permute-start | bytes 786440 | tf_op jit(solution)/shard_map/ppermute | solution.py:39
  14.4 15.6 %collective-permute-start.10 = (f32[512,128]{1,0:T(8,128)S(1)}, f32[512,128]{1,0:T(8,128)S(1)}, u32[]{:S(2)}, u32[]{:S(2)}) collective-permute-start(f32[512,128]{1,0:T(8,128)S(1)} %group.1.g0), channel_id=1, source_target_pairs={{0,12},{1,13},{2,14},{3,15},{4,8},{5,9},{6,10},{7,11},{8,4},{9,5},... | collective-permute-start | bytes 786440 | tf_op jit(solution)/shard_map/ppermute | solution.py:39
  15.5 14.5 %collective-permute-start.9 = (f32[512,128]{1,0:T(8,128)S(1)}, f32[512,128]{1,0:T(8,128)S(1)}, u32[]{:S(2)}, u32[]{:S(2)}) collective-permute-start(f32[512,128]{1,0:T(8,128)S(1)} %group.1.g0), channel_id=1, source_target_pairs={{0,4},{1,5},{2,6},{3,7},{4,0},{5,1},{6,2},{7,3},{8,12},{9,13},{10,... | collective-permute-start | bytes 786440 | tf_op jit(solution)/shard_map/ppermute | solution.py:39
  18.4 7.3 %collective-permute-start.3 = (f32[384,128]{1,0:T(8,128)S(1)}, f32[384,128]{1,0:T(8,128)S(1)}, u32[]{:S(2)}, u32[]{:S(2)}) collective-permute-start(f32[384,128]{1,0:T(8,128)S(1)} %total.1.refs_0_), channel_id=1, source_target_pairs={{0,64},{1,65},{2,66},{3,67},{4,68},{5,69},{6,70},{7,71},{8,72},{9,... | collective-permute-start | bytes 589832 | tf_op jit(solution)/shard_map/ppermute | solution.py:39
  25.8 18.6 %collective-permute-start.6 = (f32[384,128]{1,0:T(8,128)S(1)}, f32[384,128]{1,0:T(8,128)S(1)}, u32[]{:S(2)}, u32[]{:S(2)}) collective-permute-start(f32[384,128]{1,0:T(8,128)S(1)} %shift.1.own), channel_id=1, source_target_pairs={{0,16},{1,17},{2,18},{3,19},{4,20},{5,21},{6,22},{7,23},{8,24},{9,... | collective-permute-start | bytes 589832 | tf_op jit(solution)/shard_map/ppermute | solution.py:39
  26.1 18.3 %collective-permute-start.5 = (f32[384,128]{1,0:T(8,128)S(1)}, f32[384,128]{1,0:T(8,128)S(1)}, u32[]{:S(2)}, u32[]{:S(2)}) collective-permute-start(f32[384,128]{1,0:T(8,128)S(1)} %shift.1.own), channel_id=1, source_target_pairs={{0,48},{1,49},{2,50},{3,51},{4,52},{5,53},{6,54},{7,55},{8,56},{9,... | collective-permute-start | bytes 589832 | tf_op jit(solution)/shard_map/ppermute | solution.py:39
  28.2 16.2 %collective-permute-start.4 = (f32[384,128]{1,0:T(8,128)S(1)}, f32[384,128]{1,0:T(8,128)S(1)}, u32[]{:S(2)}, u32[]{:S(2)}) collective-permute-start(f32[384,128]{1,0:T(8,128)S(1)} %shift.1.own), channel_id=1, source_target_pairs={{0,32},{1,33},{2,34},{3,35},{4,36},{5,37},{6,38},{7,39},{8,40},{9,... | collective-permute-start | bytes 589832 | tf_op jit(solution)/shard_map/ppermute | solution.py:39
  31.1 1.3 %collective-permute-start.14 = (f32[64,128]{1,0:T(8,128)S(1)}, f32[64,128]{1,0:T(8,128)S(1)}, u32[]{:S(2)}, u32[]{:S(2)}) collective-permute-start(f32[64,128]{1,0:T(8,128)S(1)} %get-tuple-element.30), channel_id=1, source_target_pairs={{0,1},{1,0},{2,3},{3,2},{4,5},{5,4},{6,7},{7,6},{8,9},{9,8},{10,11... | collective-permute-start | bytes 98312 | tf_op jit(solution)/shard_map/ppermute | solution.py:39
  31.1 4.8 %collective-permute-start.12 = (f32[128,128]{1,0:T(8,128)S(1)}, f32[128,128]{1,0:T(8,128)S(1)}, u32[]{:S(2)}, u32[]{:S(2)}) collective-permute-start(f32[128,128]{1,0:T(8,128)S(1)} %get-tuple-element.27), channel_id=1, source_target_pairs={{0,2},{1,3},{2,0},{3,1},{4,6},{5,7},{6,4},{7,5},{8,10},{9,11},{10,... | collective-permute-start | bytes 196616 | tf_op jit(solution)/shard_map/ppermute | solution.py:39
  32.4 5.9 %collective-permute-start.15 = (f32[64,128]{1,0:T(8,128)S(1)}, f32[64,128]{1,0:T(8,128)S(1)}, u32[]{:S(2)}, u32[]{:S(2)}) collective-permute-start(f32[64,128]{1,0:T(8,128)S(1)} %merge.1.refs_0_), channel_id=1, source_target_pairs={{0,64},{1,65},{2,66},{3,67},{4,68},{5,69},{6,70},{7,71},{8,72},{9,... | collective-permute-start | bytes 98312 | tf_op jit(solution)/shard_map/ppermute | solution.py:39
  38.3 3.9 %collective-permute-start.16 = (f32[64,128]{1,0:T(8,128)S(1)}, f32[64,128]{1,0:T(8,128)S(1)}, u32[]{:S(2)}, u32[]{:S(2)}) collective-permute-start(f32[64,128]{1,0:T(8,128)S(1)} %edge.2.refs_0_), channel_id=1, source_target_pairs={{0,16},{1,17},{2,18},{3,19},{4,20},{5,21},{6,22},{7,23},{8,24},{9,... | collective-permute-start | bytes 98312 | tf_op jit(solution)/shard_map/ppermute | solution.py:39
  38.4 9.1 %collective-permute-start.13 = (f32[128,128]{1,0:T(8,128)S(1)}, f32[128,128]{1,0:T(8,128)S(1)}, u32[]{:S(2)}, u32[]{:S(2)}) collective-permute-start(f32[128,128]{1,0:T(8,128)S(1)} %couple.1), channel_id=1, source_target_pairs={{0,1},{1,0},{2,3},{3,2},{4,5},{5,4},{6,7},{7,6},{8,9},{9,8},{10,11... | collective-permute-start | bytes 196616 | tf_op jit(solution)/shard_map/ppermute | solution.py:39
  42.2 5.3 %collective-permute-start.17 = (f32[64,128]{1,0:T(8,128)S(1)}, f32[64,128]{1,0:T(8,128)S(1)}, u32[]{:S(2)}, u32[]{:S(2)}) collective-permute-start(f32[64,128]{1,0:T(8,128)S(1)} %edge.3.edge0), channel_id=1, source_target_pairs={{0,48},{1,49},{2,50},{3,51},{4,52},{5,53},{6,54},{7,55},{8,56},{9,... | collective-permute-start | bytes 98312 | tf_op jit(solution)/shard_map/ppermute | solution.py:39
